TPU v7x, 256 devices: a whole 4x4x8 slice. The times are simulated.
256 devices in a mesh: wide: 32 (over z, y_lo, core), narrow: 8 (over y_hi, x).
Axes of the slice: x: 4, y: 4 (y_hi: 2, y_lo: 2; y = y_hi * 2 + y_lo), z: 8, core: 2. Of those that a mesh axis runs over, the one named last changes fastest.
Arguments:
- samples: bfloat16 [1536, 2048], P('wide', 'narrow'), may hold values from -6 to 6
- inverse_factors: bfloat16 [128, 2048, 2048], P('wide', 'narrow'), as said below
- offsets: float32 [128, 2048], P('wide', 'narrow'), may hold values from -1.2 to 1.2
- log_weights: float32 [128], P('wide'), may hold values from -3 to 3
Outputs:
- log_norm: float32 [1536], P('wide')
- means: float32 [128, 2048], P('wide', 'narrow')
- covariance: bfloat16 [128, 2048, 2048], P('wide', 'narrow')
Inputs may be any that keep to these rules, and one draw needn't show every extreme that they name: `inverse_factors`: each component's factor is lower triangular, its diagonal entries from about 0.12 to 0.18.
All inputs are finite; a program needn't handle non-finite values.
Results may differ from a plain program's by a relative error of at most 0.0095.
Values may be sent and summed in bfloat16 or wider, within the bound.
No kernel may reach another device: no remote copies, remote signals or barrier semaphores. Data moves between devices by JAX's collectives and lax.ppermute only.
A program may use at most 128 MiB of HBM per device.

v0:
```python
import math

import jax
import jax.numpy as jnp
from jax import lax
from jax.sharding import PartitionSpec as P


def shards(samples, inverse_factors, offsets, log_weights):
    per_device, feat_span, features = inverse_factors.shape
    rows_here = samples.shape[0]
    feat_start = lax.axis_index("narrow") * feat_span
    full_rows = lax.all_gather(samples, "narrow", axis=1, tiled=True)
    gathered = lax.all_gather(full_rows, "wide", axis=0, tiled=True)
    total_rows = gathered.shape[0]
    flat_factors = inverse_factors.reshape(per_device * feat_span, features)
    row_block = math.gcd(total_rows, 512)

    def score_tile(row_tile):
        projected = lax.dot_general(
            row_tile, flat_factors, (((1,), (1,)), ((), ())), preferred_element_type=jnp.float32
        )
        centered = projected.reshape(row_tile.shape[0], per_device, feat_span) - offsets[None, :, :]
        return jnp.sum(centered * centered, axis=2)

    quadratic = lax.map(score_tile, gathered.reshape(total_rows // row_block, row_block, features))
    quadratic = quadratic.reshape(total_rows, per_device)
    square_part = lax.dynamic_slice_in_dim(inverse_factors, feat_start, feat_span, 2)
    diagonal_vals = jnp.diagonal(square_part, axis1=1, axis2=2).astype(jnp.float32)
    log_diag = jnp.sum(jnp.log(diagonal_vals), axis=1)
    partial_terms = log_diag[None, :] - 0.5 * quadratic
    summed = lax.psum(partial_terms, "narrow")
    loglik = summed + log_weights[None, :]
    row_peak = lax.pmax(jnp.max(loglik, axis=1), "wide")
    row_total = lax.psum(jnp.sum(jnp.exp(loglik - row_peak[:, None]), axis=1), "wide")
    log_norm = jnp.log(row_total)
    responsibility = jnp.exp(loglik - row_peak[:, None] - log_norm[:, None])
    counts = jnp.sum(responsibility, axis=0)
    sums = jnp.dot(
        responsibility.T,
        gathered,
        precision=lax.Precision.HIGHEST,
        preferred_element_type=jnp.float32,
    )
    inverse_count = 1.0 / (counts + 1.0)
    full_means = sums * inverse_count[:, None]
    own_cols = lax.dynamic_slice_in_dim(gathered, feat_start, feat_span, 1)
    weighted = (responsibility.T[:, :, None] * own_cols[None, :, :]).astype(jnp.bfloat16)
    gram = lax.dot_general(
        weighted, gathered, (((1,), (0,)), ((), ())), preferred_element_type=jnp.float32
    )
    own_means = lax.dynamic_slice_in_dim(full_means, feat_start, feat_span, 1)
    covariance = (
        gram * inverse_count[:, None, None] - own_means[:, :, None] * full_means[:, None, :]
    ).astype(jnp.bfloat16)
    own_norm = lax.dynamic_slice_in_dim(log_norm, lax.axis_index("wide") * rows_here, rows_here, 0)
    return (own_norm, own_means, covariance)


def solution(mesh):
    return jax.shard_map(
        shards,
        mesh=mesh,
        in_specs=(P("wide", "narrow"), P("wide", "narrow", None), P("wide", "narrow"), P("wide")),
        out_specs=(P("wide"), P("wide", "narrow"), P("wide", "narrow", None)),
        check_vma=False,
    )
```

profile of v0, /device:TPU:1, one launch (start us, length us, event | category | flops | bytes accessed | tf_op | source)
XLA Modules:
  0.0 309.1 jit_solution(12451935492650402820)
XLA Ops:
  7.2 0.0 all-gather.2.cloned.1.call-start
  7.2 31.5 %all_gather.6 = bf16[48,2048]{1,0:T(8,128)(2,1)} all-gather(bf16[48,256]{1,0:T(8,128)(2,1)} %param.6), channel_id=1, replica_groups=mesh['wide'=32,'narrow'=8] {'narrow'}, dimensions={1}, use_global_device_ids=true | all-gather | bytes 221184 | tf_op jit(solution)/shard_map/all_gather | solution.py:13
  38.8 0.0 all-gather.2.cloned.1.call-update
  38.8 1.1 constant_dynamic-slice_fusion.1
  39.9 0.0 copy-start.2
  39.9 11.4 %copy.11 = bf16[4,256,256]{0,2,1:T(8,128)(2,1)} copy(bf16[4,256,256]{2,1,0:T(8,128)(2,1)S(1)} %constant_dynamic-slice_fusion.1) | data formatting | bytes 1048576
  51.4 2.7 gather_fusion
  54.0 0.1 log_reduce_fusion
  54.1 64.0 %all-gather.2.cloned.1.call-done = bf16[1536,2048]{1,0:T(8,128)(2,1)} async-done(((bf16[48,2048]{1,0:T(8,128)(2,1)}), bf16[1536,2048]{1,0:T(8,128)(2,1)}) %all-gather.2.cloned.1.call-update) | async-done | bytes 6291472 | tf_op jit(solution)/shard_map/all_gather | solution.py:14
  118.1 0.0 copy-done.2
  118.1 0.0 copy-start
  118.1 15.7 %while.10 = (s32[]{:T(128)}, f32[3,512,4]{1,2,0:T(4,128)S(1)}, bf16[3,512,2048]{2,1,0:T(8,128)(2,1)}, bf16[1024,2048]{1,0:T(8,128)(2,1)}, f32[4,256]{1,0:T(4,128)S(1)}, /*index=5*/s32[]{:T(128)}) while((s32[]{:T(128)}, f32[3,512,4]{1,2,0:T(4,128)S(1)}, bf16[3,512,2048]{2,1,0:T(8,128)(2,1)}, bf16[1024,2048]{1,0:T(8,128)(2,1)}, ...), condition=%wide.region_3.4_spmd, body=%wide.region_1.3_spmd.sunk | while | flops 2149054464 | bytes 6320713 | solution.py:26
  118.1 5.2 %multiply_reduce_fusion.2 = f32[512,4]{0,1:T(4,128)S(1)} fusion(f32[4,256]{1,0:T(4,128)S(1)} %get-tuple-element.90, bf16[4,256,2048]{2,1,0:T(8,128)(2,1)} %bitcast.38, bf16[3,512,2048]{2,1,0:T(8,128)(2,1)} %get-tuple-element.88, s32[]{:T(128)} %get-tuple-element.80), kind=kOutput, calls=%fused_computation.3.clone.1 | convolution fusion | flops 2149054464 | bytes 6304256 | tf_op jit(solution)/shard_map/while/body/eval_jaxpr/dot_general | solution.py:20
  123.3 5.2 %multiply_reduce_fusion.2 = f32[512,4]{0,1:T(4,128)S(1)} fusion(f32[4,256]{1,0:T(4,128)S(1)} %get-tuple-element.90, bf16[4,256,2048]{2,1,0:T(8,128)(2,1)} %bitcast.38, bf16[3,512,2048]{2,1,0:T(8,128)(2,1)} %get-tuple-element.88, s32[]{:T(128)} %get-tuple-element.80), kind=kOutput, calls=%fused_computation.3.clone.1 | convolution fusion | flops 2149054464 | bytes 6304256 | tf_op jit(solution)/shard_map/while/body/eval_jaxpr/dot_general | solution.py:20
  128.6 5.2 %multiply_reduce_fusion.2 = f32[512,4]{0,1:T(4,128)S(1)} fusion(f32[4,256]{1,0:T(4,128)S(1)} %get-tuple-element.90, bf16[4,256,2048]{2,1,0:T(8,128)(2,1)} %bitcast.38, bf16[3,512,2048]{2,1,0:T(8,128)(2,1)} %get-tuple-element.88, s32[]{:T(128)} %get-tuple-element.80), kind=kOutput, calls=%fused_computation.3.clone.1 | convolution fusion | flops 2149054464 | bytes 6304256 | tf_op jit(solution)/shard_map/while/body/eval_jaxpr/dot_general | solution.py:20
  133.8 0.1 broadcast_subtract_fusion
  133.9 34.4 %psum.14 = f32[1536,4]{0,1:T(4,128)S(1)} all-reduce(f32[1536,4]{0,1:T(4,128)S(1)} %broadcast_subtract_fusion), channel_id=1, replica_groups=mesh['wide'=32,'narrow'=8] {'narrow'}, use_global_device_ids=true, to_apply=%region_4.5 | all-reduce | flops 6144 | bytes 49152 | tf_op jit(solution)/shard_map/psum | solution.py:32
  168.3 0.0 copy-done
  168.3 0.1 add_reduce_fusion
  168.4 60.9 %pmax.7 = f32[1536]{0:T(1024)S(1)} all-reduce(f32[1536]{0:T(1024)S(1)} %add_reduce_fusion), channel_id=1, replica_groups=mesh['wide'=32,'narrow'=8] {'wide'}, use_global_device_ids=true, to_apply=%region_6.7 | all-reduce | flops 1536 | bytes 12288 | tf_op jit(solution)/shard_map/pmax | solution.py:34
  229.2 0.1 exponential_reduce_fusion
  229.3 54.0 %psum.15 = f32[1536]{0:T(1024)S(1)} all-reduce(f32[1536]{0:T(1024)S(1)} %exponential_reduce_fusion), channel_id=1, replica_groups=mesh['wide'=32,'narrow'=8] {'wide'}, use_global_device_ids=true, to_apply=%region_8.9 | all-reduce | flops 1536 | bytes 12288 | tf_op jit(solution)/shard_map/psum | solution.py:35
  283.4 0.2 fusion.12
  283.6 5.3 %convolution_multiply_fusion = f32[4,2048]{1,0:T(4,128)S(1)} fusion(f32[1536,4]{0,1:T(4,128)S(1)} %get-tuple-element.42, bf16[1536,2048]{1,0:T(8,128)(2,1)} %bitcast.32, f32[4]{0:T(128)S(1)} %add_divide_fusion), kind=kOutput, calls=%fused_computation.13 | convolution fusion | flops 151003136 | bytes 6348816 | tf_op jit(solution)/shard_map/dot_general | solution.py:39
  288.9 0.0 copy-start.1
  288.9 1.3 dynamic-slice_convert_fusion
  290.2 0.5 copy.10
  290.7 0.6 dynamic_slice.17
  291.2 11.0 %subtract_convert_fusion = bf16[4,256,2048]{2,1,0:T(8,128)(2,1)} fusion(f32[4,2048]{1,0:T(4,128)S(1)} %convolution_multiply_fusion, f32[4,256]{1,0:T(4,128)S(1)} %constant_dynamic-slice_fusion, f32[4]{0:T(128)S(1)} %add_divide_fusion, bf16[1536,2048]{1,0:T(8,128)(2,1)} %bitcast.34, f32[1536,256]{0,1:T(8,128)S(1)} %copy.10, f32[4,1536]{1,0:T(4,128)S(1)} %bitcast.35), kind=kOutput, calls=%fused_computation.7 | convolution fusion | flops 6453985280 | bytes 12120080 | tf_op jit(solution)/shard_map/dot_general | solution.py:49
  302.3 0.0 copy-done.1
  (9 shorter events, 0.1 us)
Async XLA Ops:
  7.2 110.9 %all-gather.2.cloned.1.call-start = ((), (), s32[]{:S(2)}) async-start(), calls=%async_computation | async-start | bytes 6488064 | tf_op jit(solution)/shard_map/all_gather | solution.py:14
  39.9 78.2 %copy-start.2 = (f32[4,256]{1,0:T(4,128)S(1)}, f32[4,256]{1,0:T(4,128)}, u32[]{:S(2)}) copy-start(f32[4,256]{1,0:T(4,128)} %param.8) | copy-start | bytes 12292
  118.1 50.2 %copy-start = (f32[4]{0:T(128)S(1)}, f32[4]{0:T(128)}, u32[]{:S(2)}) copy-start(f32[4]{0:T(128)} %param.9) | copy-start | bytes 52
  288.9 13.4 %copy-start.1 = (f32[4,256]{1,0:T(4,128)}, f32[4,256]{1,0:T(4,128)S(1)}, u32[]{:S(2)}) copy-start(f32[4,256]{1,0:T(4,128)S(1)} %constant_dynamic-slice_fusion) | copy-start | bytes 12292
Sparse Core Ops, SparseCore 0:
  38.9 79.1 all-gather.1
where the time goes:
time: 309 us
  blocking collectives  181 us (59%)
  waiting for transfers between devices  64 us (21%)
  matrix products  32 us (10%)
  local copies, waits for them, and re-layouts  16.3 us (5%)
  between operations  14.1 us (5%)
    all_gather x1, waiting for transfers between devices, shards(): gathered = lax.all_gather(full_rows, 'wide', axis=0, tiled=True)  64 us
    pmax x1, blocking collectives, shards(): row_peak = lax.pmax(jnp.max(loglik, axis=1), 'wide')  60.9 us
    psum x1, blocking collectives, shards(): lax.psum(jnp.sum(jnp.exp(loglik - row_peak[:, None]), axis=1), 'wide')  54 us
    psum x1, blocking collectives, shards(): summed = lax.psum(partial_terms, 'narrow')  34.4 us
    all_gather x1, blocking collectives, shards(): full_rows = lax.all_gather(samples, 'narrow', axis=1, tiled=True)  31.5 us
    dot_general x3, matrix products, score_tile(): lax.dot_general(row_tile, flat_factors, (((1,), (1,)), ((), ())), preferr...  15.6 us
    unnamed x7, local copies, waits for them, and re-layouts  11.5 us
    dot_general x1, matrix products, shards(): lax.dot_general(weighted, gathered, (((1,), (0,)), ((), ())), preferred_e...  11 us
  transfers between devices with their start and end apart: 1, of which 1 were waited for; matrix products, arithmetic and copies ran while one was open for 5% of the time, Pallas kernels for 0%

commit v1 on v0

v1 whole, which is shorter than its diff:
```python
import functools

import jax
import jax.numpy as jnp
from jax import lax
from jax.experimental import pallas as pl
from jax.experimental.pallas import tpu as pltpu
from jax.sharding import PartitionSpec as P

AXES = ("wide", "narrow")
NZ, NY, NX = 8, 4, 4


def linear(z, y, x, c):
    return ((z * 2 + y % 2) * 2 + c) * 8 + (y // 2) * 4 + x


def pairs(move):
    out = []
    for z in range(NZ):
        for y in range(NY):
            for x in range(NX):
                for c in range(2):
                    tz, ty, tx, tc = move(z, y, x, c)
                    out.append((linear(z, y, x, c), linear(tz % NZ, ty % NY, tx % NX, tc)))
    return out


def send(value, move):
    return lax.ppermute(value, AXES, pairs(move))


def z_step(d):
    return lambda z, y, x, c: (z + d, y, x, c)


def first_step(d):
    return lambda z, y, x, c: (z, y + d, x, c) if c == 0 else (z, y, x + d, c)


def second_step(d):
    return lambda z, y, x, c: (z, y, x + d, c) if c == 0 else (z, y + d, x, c)


def core_swap(z, y, x, c):
    return (z, y, x, 1 - c)


def place():
    w, n = lax.axis_index("wide"), lax.axis_index("narrow")
    return w // 4, (n // 4) * 2 + (w // 2) % 2, n % 4, w % 2


def gather(samples):
    z, y, x, c = place()
    up = [samples]
    down = [samples]
    for _ in range(3):
        up.append(send(up[-1], z_step(1)))
        down.append(send(down[-1], z_step(-1)))
    far = send(down[-1], z_step(-1))
    ring = jnp.stack([samples, down[1], down[2], down[3], far, up[3], up[2], up[1]])
    ring = jnp.concatenate([ring, ring], axis=0)
    column = lax.dynamic_slice_in_dim(ring, NZ - z, NZ, 0)
    before = send(column, first_step(1))
    after = send(column, first_step(-1))
    far_lo = send(before[: NZ // 2], first_step(1))
    far_hi = send(after[NZ // 2 :], first_step(-1))
    plane = jnp.stack([column, after, jnp.concatenate([far_lo, far_hi], axis=0), before])
    plane_before = send(plane, second_step(1))
    plane_after = send(plane, second_step(-1))
    plane_lo = send(plane_before[:2], second_step(1))
    plane_hi = send(plane_after[2:], second_step(-1))
    mine = [plane, plane_after, plane_lo, plane_hi, plane_before]
    return mine, [send(part, core_swap) for part in mine]


PARTS = ((0, 0, 4), (1, 0, 4), (2, 0, 2), (2, 2, 2), (3, 0, 4))


def score_kernel(spot, offsets_ref, factors_ref, *refs):
    parts, (partial_ref, rows_out, rows, sems, out_sem) = refs[:10], refs[10:]
    here_y, here_x, here_c, block = spot[0], spot[1], spot[2], spot[3]
    copies = []
    count = 0
    blocks = rows.reshape(NZ, 4, 48, rows.shape[1])
    for half in range(2):
        core = here_c if half == 0 else 1 - here_c
        for part, (second, first, many) in zip(parts[half * 5 : half * 5 + 5], PARTS, strict=True):
            for i in range(many):
                ay, ax = (here_y + first + i) % 4, (here_x + second) % 4
                by, bx = (here_y + second) % 4, (here_x + first + i) % 4
                at_y = jnp.where(core == 0, ay, by)
                at_x = jnp.where(core == 0, ax, bx)
                col = pl.multiple_of(((at_y // 2) * 4 + at_x) * 256, 256)
                slot = (at_y % 2) * 2 + core
                copy = pltpu.make_async_copy(
                    part.at[i], blocks.at[:, slot, :, pl.ds(col, 256)], sems.at[count]
                )
                copy.start()
                copies.append(copy)
                count += 1
    comps, span, feats = factors_ref.shape
    own = pl.multiple_of(block * span, span)
    eye = lax.broadcasted_iota(jnp.int32, (span, span), 0) == lax.broadcasted_iota(
        jnp.int32, (span, span), 1
    )
    log_dets = []
    for k in range(comps):
        square = factors_ref[k, :, pl.ds(own, span)].astype(jnp.float32)
        diag = jnp.sum(jnp.where(eye, square, 0.0), axis=1, keepdims=True)
        log_dets.append(jnp.sum(jnp.log(diag), axis=0, keepdims=True))
    for copy in copies:
        copy.wait()
    out_copy = pltpu.make_async_copy(rows, rows_out, out_sem)
    out_copy.start()
    tile = 256

    def score(t, carry):
        at = pl.multiple_of(t * tile, tile)
        chunk = rows[pl.ds(at, tile), :]
        projected = lax.dot_general(
            factors_ref[...].reshape(comps * span, feats),
            chunk,
            (((1,), (1,)), ((), ())),
            preferred_element_type=jnp.float32,
        )
        lines = []
        for k in range(comps):
            centered = projected[k * span : (k + 1) * span] - offsets_ref[k]
            quadratic = jnp.sum(centered * centered, axis=0, keepdims=True)
            lines.append(log_dets[k] - 0.5 * quadratic)
        partial_ref[:, pl.ds(at, tile)] = jnp.concatenate(lines, axis=0)
        return carry

    lax.fori_loop(0, rows.shape[0] // tile, score, 0)
    out_copy.wait()


def scores(spot, offsets, factors, parts):
    comps, span, feats = factors.shape
    total = 1536
    anywhere = pl.BlockSpec(memory_space=pl.ANY)
    whole = pl.BlockSpec(memory_space=pltpu.VMEM)
    return pl.pallas_call(
        score_kernel,
        out_shape=(
            jax.ShapeDtypeStruct((comps, total), jnp.float32),
            jax.ShapeDtypeStruct((total, feats), jnp.bfloat16),
        ),
        in_specs=[pl.BlockSpec(memory_space=pltpu.SMEM), whole, whole] + [anywhere] * 10,
        out_specs=(whole, anywhere),
        scratch_shapes=[
            pltpu.VMEM((total, feats), jnp.bfloat16),
            pltpu.SemaphoreType.DMA((32,)),
            pltpu.SemaphoreType.DMA,
        ],
        compiler_params=pltpu.CompilerParams(vmem_limit_bytes=40 * 2**20),
        name="scores",
    )(spot, offsets[:, :, None], factors, *parts)


def moment_kernel(spot, resp_ref, own_ref, rows_ref, means_ref, cov_ref, left, own_means, inverse):
    step = pl.program_id(0)
    comps, total = resp_ref.shape
    span = own_ref.shape[1]

    @pl.when(step == 0)
    def _():
        own_t = own_ref[...].T.astype(jnp.float32)
        resp = resp_ref[...]
        inv = 1.0 / (jnp.sum(resp, axis=1, keepdims=True) + 1.0)
        inverse[...] = jnp.broadcast_to(inv, inverse.shape)
        high = resp.astype(jnp.bfloat16)
        low = (resp - high.astype(jnp.float32)).astype(jnp.bfloat16)
        zero = jnp.zeros((8, total), jnp.bfloat16)
        left[pl.ds(comps * span, 16), :] = jnp.concatenate([high, low, zero], axis=0)
        for k in range(comps):
            weighted = own_t * resp[k : k + 1]
            left[pl.ds(k * span, span), :] = weighted.astype(jnp.bfloat16)
            own_means[k] = jnp.sum(weighted, axis=1, keepdims=True) * inv[k : k + 1]

    gram = jnp.dot(left[...], rows_ref[...], preferred_element_type=jnp.float32)
    sums = gram[comps * span : comps * span + comps] + gram[comps * span + comps : comps * span + 2 * comps]
    means = sums * inverse[:, 0:1]

    @pl.when(step == spot[3])
    def _():
        means_ref[...] = means

    for k in range(comps):
        cov_ref[k] = (
            gram[k * span : (k + 1) * span] * inverse[k : k + 1, 0:1] - own_means[k] * means[k : k + 1]
        ).astype(jnp.bfloat16)


def moments(spot, resp, rows, span):
    comps, total = resp.shape
    feats = rows.shape[1]
    tile = 256
    grid_spec = pltpu.PrefetchScalarGridSpec(
        num_scalar_prefetch=1,
        grid=(feats // tile,),
        in_specs=[
            pl.BlockSpec((comps, total), lambda t, spot: (0, 0)),
            pl.BlockSpec((total, span), lambda t, spot: (0, spot[3])),
            pl.BlockSpec((total, tile), lambda t, spot: (0, t)),
        ],
        out_specs=(
            pl.BlockSpec((comps, tile), lambda t, spot: (0, 0)),
            pl.BlockSpec((comps, span, tile), lambda t, spot: (0, 0, t)),
        ),
        scratch_shapes=[
            pltpu.VMEM((comps * span + 16, total), jnp.bfloat16),
            pltpu.VMEM((comps, span, 1), jnp.float32),
            pltpu.VMEM((comps, 128), jnp.float32),
        ],
    )
    return pl.pallas_call(
        moment_kernel,
        grid_spec=grid_spec,
        out_shape=(
            jax.ShapeDtypeStruct((comps, span), jnp.float32),
            jax.ShapeDtypeStruct((comps, span, feats), jnp.bfloat16),
        ),
        compiler_params=pltpu.CompilerParams(vmem_limit_bytes=40 * 2**20),
        name="moments",
    )(spot, resp, rows, rows)


def mirror(x):
    return x ^ 1


def x_even(z, y, x, c):
    return (z, y, x ^ 1, c)


def x_odd(z, y, x, c):
    return (z, y, 3 - x, c)


def y_far(z, y, x, c):
    return (z, y + 2, x, c)


def y_near(z, y, x, c):
    return (z, y ^ 1, x, c)


def z_even(z, y, x, c):
    return (z ^ 1, y, x, c)


def z_odd(z, y, x, c):
    return (z + 1 if z % 2 else z - 1, y, x, c)


Z_LAST = {1: 6, 6: 1, 2: 5, 5: 2, 3: 0, 0: 3, 4: 7, 7: 4}


def z_far(z, y, x, c):
    return (Z_LAST[z], y, x, c)


def shards(samples, inverse_factors, offsets, log_weights):
    z, y, x, c = place()
    rows_here = samples.shape[0]
    spot = jnp.stack([y, x, c, lax.axis_index("narrow")]).astype(jnp.int32)
    mine, theirs = gather(samples)
    loglik, rows = scores(spot, offsets, inverse_factors, mine + theirs)
    for move in (x_even, x_odd, y_far):
        loglik = loglik + send(loglik, move)
    loglik = loglik + log_weights[:, None]
    peak = jnp.max(loglik, axis=0)
    total = jnp.sum(jnp.exp(loglik - peak[None, :]), axis=0)
    pair = jnp.stack([peak, total])
    for move in (core_swap, y_near, z_even, z_odd, z_far):
        other = send(pair, move)
        peak = jnp.maximum(pair[0], other[0])
        total = pair[1] * jnp.exp(pair[0] - peak) + other[1] * jnp.exp(other[0] - peak)
        pair = jnp.stack([peak, total])
    log_norm = jnp.log(pair[1])
    responsibility = jnp.exp((loglik - pair[0][None, :]) - log_norm[None, :])
    means, covariance = moments(spot, responsibility, rows, inverse_factors.shape[1])
    own_norm = lax.dynamic_slice_in_dim(log_norm, lax.axis_index("wide") * rows_here, rows_here, 0)
    return (own_norm, means, covariance)


def solution(mesh):
    return jax.shard_map(
        shards,
        mesh=mesh,
        in_specs=(P("wide", "narrow"), P("wide", "narrow", None), P("wide", "narrow"), P("wide")),
        out_specs=(P("wide"), P("wide", "narrow"), P("wide", "narrow", None)),
        check_vma=False,
    )
```

time: 309 us -> 133 us (0.43)
  the two profiles are of different devices: /device:TPU:1 before, /device:TPU:6 now
where the time goes in v1:
time: 133 us
  waiting for transfers between devices  61.7 us (46%)
  starting transfers between devices  37.7 us (28%)
  Pallas kernels  24.4 us (18%)
  local copies, waits for them, and re-layouts  6.88 us (5%)
  other arithmetic  1.36 us (1%)
    ppermute x28, waiting for transfers between devices, send(): return lax.ppermute(value, AXES, pairs(move))  61.7 us
    ppermute x28, starting transfers between devices, send(): return lax.ppermute(value, AXES, pairs(move))  37.7 us
    pallas_call x1, Pallas kernels, moments(): pl.pallas_call(moment_kernel, grid_spec=grid_spec, out_shape=(jax.ShapeDt...  13.2 us
    pallas_call x1, Pallas kernels, scores(): pl.pallas_call(score_kernel, out_shape=(jax.ShapeDtypeStruct((comps, tota...  11.2 us
    unnamed x23, local copies, waits for them, and re-layouts  6.53 us
  transfers between devices with their start and end apart: 28, of which 19 were waited for; matrix products, arithmetic and copies ran while one was open for 1% of the time, Pallas kernels for 0%

profile of v1, /device:TPU:6, one launch (start us, length us, event | category | flops | bytes accessed | tf_op | source)
XLA Modules:
  0.0 133.0 jit_solution(5168995117750303169)
XLA Ops:
  0.6 2.0 %collective-permute-start.4 = (bf16[48,256]{1,0:T(8,128)(2,1)}, bf16[48,256]{1,0:T(8,128)(2,1)S(1)}, u32[]{:S(2)}, u32[]{:S(2)}) collective-permute-start(bf16[48,256]{1,0:T(8,128)(2,1)} %param.4), channel_id=1, source_target_pairs={{0,32},{8,40},{1,33},{9,41},{2,34},{10,42},{3,35},{11,43},{16,48},... | collective-permute-start | bytes 73736 | tf_op jit(solution)/shard_map/ppermute | solution.py:30
  2.6 4.0 %collective-permute-start = (bf16[48,256]{1,0:T(8,128)(2,1)}, bf16[48,256]{1,0:T(8,128)(2,1)S(1)}, u32[]{:S(2)}, u32[]{:S(2)}) collective-permute-start(bf16[48,256]{1,0:T(8,128)(2,1)} %param.4), channel_id=1, source_target_pairs={{0,224},{8,232},{1,225},{9,233},{2,226},{10,234},{3,227},{11,235},... | collective-permute-start | bytes 73736 | tf_op jit(solution)/shard_map/ppermute | solution.py:30
  8.6 3.3 %collective-permute-start.1 = (bf16[48,256]{1,0:T(8,128)(2,1)S(1)}, bf16[48,256]{1,0:T(8,128)(2,1)S(1)}, u32[]{:S(2)}, u32[]{:S(2)}) collective-permute-start(bf16[48,256]{1,0:T(8,128)(2,1)S(1)} %collective-permute-done), channel_id=1, source_target_pairs={{0,224},{8,232},{1,225},{9,233},{2,226},{10,234},{3,227},{11,235},... | collective-permute-start | bytes 73736 | tf_op jit(solution)/shard_map/ppermute | solution.py:30
  11.9 1.7 %collective-permute-done.5 = bf16[48,256]{1,0:T(8,128)(2,1)S(1)} collective-permute-done((bf16[48,256]{1,0:T(8,128)(2,1)S(1)}, bf16[48,256]{1,0:T(8,128)(2,1)S(1)}, u32[]{:S(2)}, u32[]{:S(2)}) %collective-permute-start.5) | collective-permute-done | bytes 24608 | tf_op jit(solution)/shard_map/ppermute | solution.py:30
  13.6 3.3 %collective-permute-start.2 = (bf16[48,256]{1,0:T(8,128)(2,1)S(1)}, bf16[48,256]{1,0:T(8,128)(2,1)S(1)}, u32[]{:S(2)}, u32[]{:S(2)}) collective-permute-start(bf16[48,256]{1,0:T(8,128)(2,1)S(1)} %collective-permute-done.1), channel_id=1, source_target_pairs={{0,224},{8,232},{1,225},{9,233},{2,226},{10,234},{3,227},{11,235},... | collective-permute-start | bytes 73736 | tf_op jit(solution)/shard_map/ppermute | solution.py:30
  17.0 1.5 %collective-permute-done.2 = bf16[48,256]{1,0:T(8,128)(2,1)S(1)} collective-permute-done((bf16[48,256]{1,0:T(8,128)(2,1)S(1)}, bf16[48,256]{1,0:T(8,128)(2,1)S(1)}, u32[]{:S(2)}, u32[]{:S(2)}) %collective-permute-start.2) | collective-permute-done | bytes 24608 | tf_op jit(solution)/shard_map/ppermute | solution.py:30
  18.5 3.5 %collective-permute-start.3 = (bf16[48,256]{1,0:T(8,128)(2,1)S(1)}, bf16[48,256]{1,0:T(8,128)(2,1)S(1)}, u32[]{:S(2)}, u32[]{:S(2)}) collective-permute-start(bf16[48,256]{1,0:T(8,128)(2,1)S(1)} %collective-permute-done.2), channel_id=1, source_target_pairs={{0,224},{8,232},{1,225},{9,233},{2,226},{10,234},{3,227},{11,235},... | collective-permute-start | bytes 73736 | tf_op jit(solution)/shard_map/ppermute | solution.py:30
  22.0 1.5 %collective-permute-done.3 = bf16[48,256]{1,0:T(8,128)(2,1)S(1)} collective-permute-done((bf16[48,256]{1,0:T(8,128)(2,1)S(1)}, bf16[48,256]{1,0:T(8,128)(2,1)S(1)}, u32[]{:S(2)}, u32[]{:S(2)}) %collective-permute-start.3) | collective-permute-done | bytes 24608 | tf_op jit(solution)/shard_map/ppermute | solution.py:30
  24.4 3.1 %collective-permute-start.7 = (bf16[8,48,256]{2,1,0:T(8,128)(2,1)S(1)}, bf16[8,48,256]{2,1,0:T(8,128)(2,1)S(1)}, u32[]{:S(2)}, u32[]{:S(2)}) collective-permute-start(bf16[8,48,256]{2,1,0:T(8,128)(2,1)S(1)} %constant_dynamic-slice_fusion), channel_id=1, source_target_pairs={{0,20},{8,11},{1,21},{9,8},{2,22},{10,9},{3,23},{11,10},{16,0},{24... | collective-permute-start | bytes 589832 | tf_op jit(solution)/shard_map/ppermute | solution.py:30
  27.5 3.2 %collective-permute-done.7 = bf16[8,48,256]{2,1,0:T(8,128)(2,1)S(1)} collective-permute-done((bf16[8,48,256]{2,1,0:T(8,128)(2,1)S(1)}, bf16[8,48,256]{2,1,0:T(8,128)(2,1)S(1)}, u32[]{:S(2)}, u32[]{:S(2)}) %collective-permute-start.7) | collective-permute-done | bytes 196640 | tf_op jit(solution)/shard_map/ppermute | solution.py:30
  30.7 3.8 %collective-permute-start.10 = (bf16[4,48,256]{2,1,0:T(8,128)(2,1)S(1)}, bf16[4,48,256]{2,1,0:T(8,128)(2,1)S(1)}, u32[]{:S(2)}, u32[]{:S(2)}) collective-permute-start(bf16[4,48,256]{2,1,0:T(8,128)(2,1)S(1)} %slice.62), channel_id=1, source_target_pairs={{0,20},{8,11},{1,21},{9,8},{2,22},{10,9},{3,23},{11,10},{16,0},{24... | collective-permute-start | bytes 294920 | tf_op jit(solution)/shard_map/ppermute | solution.py:30
  34.6 3.1 %collective-permute-done.10 = bf16[4,48,256]{2,1,0:T(8,128)(2,1)S(1)} collective-permute-done((bf16[4,48,256]{2,1,0:T(8,128)(2,1)S(1)}, bf16[4,48,256]{2,1,0:T(8,128)(2,1)S(1)}, u32[]{:S(2)}, u32[]{:S(2)}) %collective-permute-start.10) | collective-permute-done | bytes 98336 | tf_op jit(solution)/shard_map/ppermute | solution.py:30
  37.7 3.8 %collective-permute-done.9 = bf16[4,48,256]{2,1,0:T(8,128)(2,1)S(1)} collective-permute-done((bf16[4,48,256]{2,1,0:T(8,128)(2,1)S(1)}, bf16[4,48,256]{2,1,0:T(8,128)(2,1)S(1)}, u32[]{:S(2)}, u32[]{:S(2)}) %collective-permute-start.9) | collective-permute-done | bytes 98336 | tf_op jit(solution)/shard_map/ppermute | solution.py:30
  42.2 1.6 %collective-permute-start.11 = (bf16[4,8,48,256]{3,2,1,0:T(8,128)(2,1)S(1)}, bf16[4,8,48,256]{3,2,1,0:T(8,128)(2,1)S(1)}, u32[]{:S(2)}, u32[]{:S(2)}) collective-permute-start(bf16[4,8,48,256]{3,2,1,0:T(8,128)(2,1)S(1)} %pad_maximum_fusion.refs_0_), channel_id=1, source_target_pairs={{0,3},{8,28},{1,0},{9,29},{2,1},{10,30},{3,2},{11,31},{16,19},{24,... | collective-permute-start | bytes 2359304 | tf_op jit(solution)/shard_map/ppermute | solution.py:30
  43.8 9.9 %collective-permute-done.12.refs_4_ = bf16[4,8,48,256]{3,2,1,0:T(8,128)(2,1)S(1)} collective-permute-done((bf16[4,8,48,256]{3,2,1,0:T(8,128)(2,1)S(1)}, bf16[4,8,48,256]{3,2,1,0:T(8,128)(2,1)S(1)}, u32[]{:S(2)}, u32[]{:S(2)}) %collective-permute-start.12) | collective-permute-done | bytes 786464 | tf_op jit(solution)/shard_map/ppermute | solution.py:30
  53.7 1.8 %collective-permute-start.13 = (bf16[2,8,48,256]{3,2,1,0:T(8,128)(2,1)S(1)}, bf16[2,8,48,256]{3,2,1,0:T(8,128)(2,1)S(1)}, u32[]{:S(2)}, u32[]{:S(2)}) collective-permute-start(bf16[2,8,48,256]{3,2,1,0:T(8,128)(2,1)S(1)} %slice.63), channel_id=1, source_target_pairs={{0,1},{8,24},{1,2},{9,25},{2,3},{10,26},{3,0},{11,27},{16,17},{24,... | collective-permute-start | bytes 1179656 | tf_op jit(solution)/shard_map/ppermute | solution.py:30
  56.6 4.9 %collective-permute-done.13.refs_2_ = bf16[2,8,48,256]{3,2,1,0:T(8,128)(2,1)S(1)} collective-permute-done((bf16[2,8,48,256]{3,2,1,0:T(8,128)(2,1)S(1)}, bf16[2,8,48,256]{3,2,1,0:T(8,128)(2,1)S(1)}, u32[]{:S(2)}, u32[]{:S(2)}) %collective-permute-start.13) | collective-permute-done | bytes 393248 | tf_op jit(solution)/shard_map/ppermute | solution.py:30
  61.6 3.3 %collective-permute-done.14.refs_3_ = bf16[2,8,48,256]{3,2,1,0:T(8,128)(2,1)} collective-permute-done((bf16[2,8,48,256]{3,2,1,0:T(8,128)(2,1)S(1)}, bf16[2,8,48,256]{3,2,1,0:T(8,128)(2,1)}, u32[]{:S(2)}, u32[]{:S(2)}) %collective-permute-start.14) | collective-permute-done | bytes 393248 | tf_op jit(solution)/shard_map/ppermute | solution.py:30
  65.2 1.7 %collective-permute-done.18.refs_8_ = bf16[2,8,48,256]{3,2,1,0:T(8,128)(2,1)} collective-permute-done((bf16[2,8,48,256]{3,2,1,0:T(8,128)(2,1)}, bf16[2,8,48,256]{3,2,1,0:T(8,128)(2,1)}, u32[]{:S(2)}, u32[]{:S(2)}) %collective-permute-start.18) | collective-permute-done | bytes 393248 | tf_op jit(solution)/shard_map/ppermute | solution.py:30
  66.9 2.2 %copy-done.1 = bf16[4,256,2048]{2,1,0:T(8,128)(2,1)S(1)} copy-done((bf16[4,256,2048]{2,1,0:T(8,128)(2,1)S(1)}, bf16[4,256,2048]{2,1,0:T(8,128)(2,1)}, u32[]{:S(2)}) %copy-start.1) | copy-done | bytes 4194328
  69.1 11.2 %scores.1 = (f32[4,1536]{1,0:T(4,128)S(1)}, bf16[1536,2048]{1,0:T(8,128)(2,1)}) custom-call(s32[4]{0:T(128)S(1)} %pad_add_fusion.spot, f32[4,256,1]{2,1,0:T(8,128)S(1)} %copy.7.offsets_ref, bf16[4,256,2048]{2,1,0:T(8,128)(2,1)S(1)} %copy-done.1, bf16[4,8,48,256]{3,2,1,0:T(8,128)(2,1)S(1)} %pad_maximum_fusion.refs_0_, ...), custom_call_target="tpu_custom_call" | custom-call | tf_op jit(solution)/shard_map/scores/pallas_call | solution.py:145
  80.4 3.8 %collective-permute-done.20 = f32[4,1536]{1,0:T(4,128)S(1)} collective-permute-done((f32[4,1536]{1,0:T(4,128)S(1)}, f32[4,1536]{1,0:T(4,128)S(1)}, u32[]{:S(2)}, u32[]{:S(2)}) %collective-permute-start.20) | collective-permute-done | bytes 24608 | tf_op jit(solution)/shard_map/ppermute | solution.py:30
  84.5 4.9 %collective-permute-done.21 = f32[4,1536]{1,0:T(4,128)S(1)} collective-permute-done((f32[4,1536]{1,0:T(4,128)S(1)}, f32[4,1536]{1,0:T(4,128)S(1)}, u32[]{:S(2)}, u32[]{:S(2)}) %collective-permute-start.21) | collective-permute-done | bytes 24608 | tf_op jit(solution)/shard_map/ppermute | solution.py:30
  89.5 5.3 %collective-permute-done.22 = f32[4,1536]{1,0:T(4,128)S(1)} collective-permute-done((f32[4,1536]{1,0:T(4,128)S(1)}, f32[4,1536]{1,0:T(4,128)S(1)}, u32[]{:S(2)}, u32[]{:S(2)}) %collective-permute-start.22) | collective-permute-done | bytes 24608 | tf_op jit(solution)/shard_map/ppermute | solution.py:30
  96.4 3.7 %collective-permute-done.24 = f32[2,1536]{1,0:T(2,128)S(1)} collective-permute-done((f32[2,1536]{1,0:T(2,128)S(1)}, f32[2,1536]{1,0:T(2,128)S(1)}, u32[]{:S(2)}, u32[]{:S(2)}) %collective-permute-start.24) | collective-permute-done | bytes 12320 | tf_op jit(solution)/shard_map/ppermute | solution.py:30
  100.3 3.7 %collective-permute-done.25 = f32[2,1536]{1,0:T(2,128)S(1)} collective-permute-done((f32[2,1536]{1,0:T(2,128)S(1)}, f32[2,1536]{1,0:T(2,128)S(1)}, u32[]{:S(2)}, u32[]{:S(2)}) %collective-permute-start.25) | collective-permute-done | bytes 12320 | tf_op jit(solution)/shard_map/ppermute | solution.py:30
  104.0 3.6 %collective-permute-start.26 = (f32[2,1536]{1,0:T(2,128)S(1)}, f32[2,1536]{1,0:T(2,128)S(1)}, u32[]{:S(2)}, u32[]{:S(2)}) collective-permute-start(f32[2,1536]{1,0:T(2,128)S(1)} %pad_maximum_fusion.4), channel_id=1, source_target_pairs={{0,224},{8,232},{1,225},{9,233},{2,226},{10,234},{3,227},{11,235},... | collective-permute-start | bytes 36872 | tf_op jit(solution)/shard_map/ppermute | solution.py:30
  107.6 1.7 %collective-permute-done.26 = f32[2,1536]{1,0:T(2,128)S(1)} collective-permute-done((f32[2,1536]{1,0:T(2,128)S(1)}, f32[2,1536]{1,0:T(2,128)S(1)}, u32[]{:S(2)}, u32[]{:S(2)}) %collective-permute-start.26) | collective-permute-done | bytes 12320 | tf_op jit(solution)/shard_map/ppermute | solution.py:30
  109.4 5.2 %collective-permute-start.27 = (f32[2,1536]{1,0:T(2,128)S(1)}, f32[2,1536]{1,0:T(2,128)S(1)}, u32[]{:S(2)}, u32[]{:S(2)}) collective-permute-start(f32[2,1536]{1,0:T(2,128)S(1)} %pad_maximum_fusion.5), channel_id=1, source_target_pairs={{0,96},{8,104},{1,97},{9,105},{2,98},{10,106},{3,99},{11,107},{16,... | collective-permute-start | bytes 36872 | tf_op jit(solution)/shard_map/ppermute | solution.py:30
  114.6 1.7 %collective-permute-done.27 = f32[2,1536]{1,0:T(2,128)S(1)} collective-permute-done((f32[2,1536]{1,0:T(2,128)S(1)}, f32[2,1536]{1,0:T(2,128)S(1)}, u32[]{:S(2)}, u32[]{:S(2)}) %collective-permute-start.27) | collective-permute-done | bytes 12320 | tf_op jit(solution)/shard_map/ppermute | solution.py:30
  116.4 2.8 %copy-done = bf16[1536,2048]{1,0:T(8,128)(2,1)S(1)} copy-done((bf16[1536,2048]{1,0:T(8,128)(2,1)S(1)}, bf16[1536,2048]{1,0:T(8,128)(2,1)}, u32[]{:S(2)}) %copy-start) | copy-done | bytes 6291480
  119.2 13.2 %moments.1 = (f32[4,256]{1,0:T(4,128)}, bf16[4,256,2048]{2,1,0:T(8,128)(2,1)}) custom-call(s32[4]{0:T(128)S(1)} %pad_add_fusion.spot, f32[4,1536]{1,0:T(4,128)S(1)} %subtract_exponential_fusion.resp_ref, bf16[1536,2048]{1,0:T(8,128)(2,1)S(1)} %copy-done, bf16[1536,2048]{1,0:T(8,128)(2,1)S(1)} %copy-done), custom_call_target="tpu_custom_call" | custom-call | tf_op jit(solution)/shard_map/moments/pallas_call | solution.py:219
  (82 shorter events, 8.1 us)
Async XLA Ops:
  0.6 64.2 %copy-start.2 = (f32[4,256]{1,0:T(4,128)S(1)}, f32[4,256]{1,0:T(4,128)}, u32[]{:S(2)}) copy-start(f32[4,256]{1,0:T(4,128)} %param.6) | copy-start | bytes 12292
  0.6 8.0 %collective-permute-start.4 = (bf16[48,256]{1,0:T(8,128)(2,1)}, bf16[48,256]{1,0:T(8,128)(2,1)S(1)}, u32[]{:S(2)}, u32[]{:S(2)}) collective-permute-start(bf16[48,256]{1,0:T(8,128)(2,1)} %param.4), channel_id=1, source_target_pairs={{0,32},{8,40},{1,33},{9,41},{2,34},{10,42},{3,35},{11,43},{16,48},... | collective-permute-start | bytes 73736 | tf_op jit(solution)/shard_map/ppermute | solution.py:30
  2.6 6.0 %collective-permute-start = (bf16[48,256]{1,0:T(8,128)(2,1)}, bf16[48,256]{1,0:T(8,128)(2,1)S(1)}, u32[]{:S(2)}, u32[]{:S(2)}) collective-permute-start(bf16[48,256]{1,0:T(8,128)(2,1)} %param.4), channel_id=1, source_target_pairs={{0,224},{8,232},{1,225},{9,233},{2,226},{10,234},{3,227},{11,235},... | collective-permute-start | bytes 73736 | tf_op jit(solution)/shard_map/ppermute | solution.py:30
  8.6 5.0 %collective-permute-start.5 = (bf16[48,256]{1,0:T(8,128)(2,1)S(1)}, bf16[48,256]{1,0:T(8,128)(2,1)S(1)}, u32[]{:S(2)}, u32[]{:S(2)}) collective-permute-start(bf16[48,256]{1,0:T(8,128)(2,1)S(1)} %collective-permute-done.4), channel_id=1, source_target_pairs={{0,32},{8,40},{1,33},{9,41},{2,34},{10,42},{3,35},{11,43},{16,48},... | collective-permute-start | bytes 73736 | tf_op jit(solution)/shard_map/ppermute | solution.py:30
  8.6 5.0 %collective-permute-start.1 = (bf16[48,256]{1,0:T(8,128)(2,1)S(1)}, bf16[48,256]{1,0:T(8,128)(2,1)S(1)}, u32[]{:S(2)}, u32[]{:S(2)}) collective-permute-start(bf16[48,256]{1,0:T(8,128)(2,1)S(1)} %collective-permute-done), channel_id=1, source_target_pairs={{0,224},{8,232},{1,225},{9,233},{2,226},{10,234},{3,227},{11,235},... | collective-permute-start | bytes 73736 | tf_op jit(solution)/shard_map/ppermute | solution.py:30
  13.6 9.9 %collective-permute-start.6 = (bf16[48,256]{1,0:T(8,128)(2,1)S(1)}, bf16[48,256]{1,0:T(8,128)(2,1)S(1)}, u32[]{:S(2)}, u32[]{:S(2)}) collective-permute-start(bf16[48,256]{1,0:T(8,128)(2,1)S(1)} %collective-permute-done.5), channel_id=1, source_target_pairs={{0,32},{8,40},{1,33},{9,41},{2,34},{10,42},{3,35},{11,43},{16,48},... | collective-permute-start | bytes 73736 | tf_op jit(solution)/shard_map/ppermute | solution.py:30
  13.6 4.8 %collective-permute-start.2 = (bf16[48,256]{1,0:T(8,128)(2,1)S(1)}, bf16[48,256]{1,0:T(8,128)(2,1)S(1)}, u32[]{:S(2)}, u32[]{:S(2)}) collective-permute-start(bf16[48,256]{1,0:T(8,128)(2,1)S(1)} %collective-permute-done.1), channel_id=1, source_target_pairs={{0,224},{8,232},{1,225},{9,233},{2,226},{10,234},{3,227},{11,235},... | collective-permute-start | bytes 73736 | tf_op jit(solution)/shard_map/ppermute | solution.py:30
  18.5 5.0 %collective-permute-start.3 = (bf16[48,256]{1,0:T(8,128)(2,1)S(1)}, bf16[48,256]{1,0:T(8,128)(2,1)S(1)}, u32[]{:S(2)}, u32[]{:S(2)}) collective-permute-start(bf16[48,256]{1,0:T(8,128)(2,1)S(1)} %collective-permute-done.2), channel_id=1, source_target_pairs={{0,224},{8,232},{1,225},{9,233},{2,226},{10,234},{3,227},{11,235},... | collective-permute-start | bytes 73736 | tf_op jit(solution)/shard_map/ppermute | solution.py:30
  24.4 6.3 %collective-permute-start.7 = (bf16[8,48,256]{2,1,0:T(8,128)(2,1)S(1)}, bf16[8,48,256]{2,1,0:T(8,128)(2,1)S(1)}, u32[]{:S(2)}, u32[]{:S(2)}) collective-permute-start(bf16[8,48,256]{2,1,0:T(8,128)(2,1)S(1)} %constant_dynamic-slice_fusion), channel_id=1, source_target_pairs={{0,20},{8,11},{1,21},{9,8},{2,22},{10,9},{3,23},{11,10},{16,0},{24... | collective-permute-start | bytes 589832 | tf_op jit(solution)/shard_map/ppermute | solution.py:30
  27.5 7.0 %collective-permute-start.8 = (bf16[8,48,256]{2,1,0:T(8,128)(2,1)S(1)}, bf16[8,48,256]{2,1,0:T(8,128)(2,1)S(1)}, u32[]{:S(2)}, u32[]{:S(2)}) collective-permute-start(bf16[8,48,256]{2,1,0:T(8,128)(2,1)S(1)} %constant_dynamic-slice_fusion), channel_id=1, source_target_pairs={{0,16},{8,9},{1,17},{9,10},{2,18},{10,11},{3,19},{11,8},{16,4},{24... | collective-permute-start | bytes 589832 | tf_op jit(solution)/shard_map/ppermute | solution.py:30
  30.7 7.0 %collective-permute-start.10 = (bf16[4,48,256]{2,1,0:T(8,128)(2,1)S(1)}, bf16[4,48,256]{2,1,0:T(8,128)(2,1)S(1)}, u32[]{:S(2)}, u32[]{:S(2)}) collective-permute-start(bf16[4,48,256]{2,1,0:T(8,128)(2,1)S(1)} %slice.62), channel_id=1, source_target_pairs={{0,20},{8,11},{1,21},{9,8},{2,22},{10,9},{3,23},{11,10},{16,0},{24... | collective-permute-start | bytes 294920 | tf_op jit(solution)/shard_map/ppermute | solution.py:30
  34.5 7.0 %collective-permute-start.9 = (bf16[4,48,256]{2,1,0:T(8,128)(2,1)S(1)}, bf16[4,48,256]{2,1,0:T(8,128)(2,1)S(1)}, u32[]{:S(2)}, u32[]{:S(2)}) collective-permute-start(bf16[4,48,256]{2,1,0:T(8,128)(2,1)S(1)} %slice.61), channel_id=1, source_target_pairs={{0,16},{8,9},{1,17},{9,10},{2,18},{10,11},{3,19},{11,8},{16,4},{24... | collective-permute-start | bytes 294920 | tf_op jit(solution)/shard_map/ppermute | solution.py:30
  41.6 12.1 %collective-permute-start.12 = (bf16[4,8,48,256]{3,2,1,0:T(8,128)(2,1)S(1)}, bf16[4,8,48,256]{3,2,1,0:T(8,128)(2,1)S(1)}, u32[]{:S(2)}, u32[]{:S(2)}) collective-permute-start(bf16[4,8,48,256]{3,2,1,0:T(8,128)(2,1)S(1)} %pad_maximum_fusion.refs_0_), channel_id=1, source_target_pairs={{0,1},{8,24},{1,2},{9,25},{2,3},{10,26},{3,0},{11,27},{16,17},{24,... | collective-permute-start | bytes 2359304 | tf_op jit(solution)/shard_map/ppermute | solution.py:30
  42.2 13.3 %collective-permute-start.11 = (bf16[4,8,48,256]{3,2,1,0:T(8,128)(2,1)S(1)}, bf16[4,8,48,256]{3,2,1,0:T(8,128)(2,1)S(1)}, u32[]{:S(2)}, u32[]{:S(2)}) collective-permute-start(bf16[4,8,48,256]{3,2,1,0:T(8,128)(2,1)S(1)} %pad_maximum_fusion.refs_0_), channel_id=1, source_target_pairs={{0,3},{8,28},{1,0},{9,29},{2,1},{10,30},{3,2},{11,31},{16,19},{24,... | collective-permute-start | bytes 2359304 | tf_op jit(solution)/shard_map/ppermute | solution.py:30
  43.8 21.4 %collective-permute-start.15 = (bf16[4,8,48,256]{3,2,1,0:T(8,128)(2,1)S(1)}, bf16[4,8,48,256]{3,2,1,0:T(8,128)(2,1)}, u32[]{:S(2)}, u32[]{:S(2)}) collective-permute-start(bf16[4,8,48,256]{3,2,1,0:T(8,128)(2,1)S(1)} %pad_maximum_fusion.refs_0_), channel_id=1, source_target_pairs={{0,8},{8,0},{1,9},{9,1},{2,10},{10,2},{3,11},{11,3},{16,24},{24,16... | collective-permute-start | bytes 2359304 | tf_op jit(solution)/shard_map/ppermute | solution.py:30
  53.7 7.9 %collective-permute-start.13 = (bf16[2,8,48,256]{3,2,1,0:T(8,128)(2,1)S(1)}, bf16[2,8,48,256]{3,2,1,0:T(8,128)(2,1)S(1)}, u32[]{:S(2)}, u32[]{:S(2)}) collective-permute-start(bf16[2,8,48,256]{3,2,1,0:T(8,128)(2,1)S(1)} %slice.63), channel_id=1, source_target_pairs={{0,1},{8,24},{1,2},{9,25},{2,3},{10,26},{3,0},{11,27},{16,17},{24,... | collective-permute-start | bytes 1179656 | tf_op jit(solution)/shard_map/ppermute | solution.py:30
  55.5 9.4 %collective-permute-start.14 = (bf16[2,8,48,256]{3,2,1,0:T(8,128)(2,1)S(1)}, bf16[2,8,48,256]{3,2,1,0:T(8,128)(2,1)}, u32[]{:S(2)}, u32[]{:S(2)}) collective-permute-start(bf16[2,8,48,256]{3,2,1,0:T(8,128)(2,1)S(1)} %slice.64), channel_id=1, source_target_pairs={{0,3},{8,28},{1,0},{9,29},{2,1},{10,30},{3,2},{11,31},{16,19},{24,... | collective-permute-start | bytes 1179656 | tf_op jit(solution)/shard_map/ppermute | solution.py:30
  56.1 9.1 %collective-permute-start.19 = (bf16[4,8,48,256]{3,2,1,0:T(8,128)(2,1)S(1)}, bf16[4,8,48,256]{3,2,1,0:T(8,128)(2,1)}, u32[]{:S(2)}, u32[]{:S(2)}) collective-permute-start(bf16[4,8,48,256]{3,2,1,0:T(8,128)(2,1)S(1)} %collective-permute-done.12.refs_4_), channel_id=1, source_target_pairs={{0,8},{8,0},{1,9},{9,1},{2,10},{10,2},{3,11},{11,3},{16,24},{24,16... | collective-permute-start | bytes 2359304 | tf_op jit(solution)/shard_map/ppermute | solution.py:30
  56.1 10.8 %collective-permute-start.16 = (bf16[4,8,48,256]{3,2,1,0:T(8,128)(2,1)S(1)}, bf16[4,8,48,256]{3,2,1,0:T(8,128)(2,1)}, u32[]{:S(2)}, u32[]{:S(2)}) collective-permute-start(bf16[4,8,48,256]{3,2,1,0:T(8,128)(2,1)S(1)} %collective-permute-done.11.refs_1_), channel_id=1, source_target_pairs={{0,8},{8,0},{1,9},{9,1},{2,10},{10,2},{3,11},{11,3},{16,24},{24,16... | collective-permute-start | bytes 2359304 | tf_op jit(solution)/shard_map/ppermute | solution.py:30
  61.6 3.7 %collective-permute-start.17 = (bf16[2,8,48,256]{3,2,1,0:T(8,128)(2,1)S(1)}, bf16[2,8,48,256]{3,2,1,0:T(8,128)(2,1)}, u32[]{:S(2)}, u32[]{:S(2)}) collective-permute-start(bf16[2,8,48,256]{3,2,1,0:T(8,128)(2,1)S(1)} %collective-permute-done.13.refs_2_), channel_id=1, source_target_pairs={{0,8},{8,0},{1,9},{9,1},{2,10},{10,2},{3,11},{11,3},{16,24},{24,16... | collective-permute-start | bytes 1179656 | tf_op jit(solution)/shard_map/ppermute | solution.py:30
  64.9 2.1 %collective-permute-start.18 = (bf16[2,8,48,256]{3,2,1,0:T(8,128)(2,1)}, bf16[2,8,48,256]{3,2,1,0:T(8,128)(2,1)}, u32[]{:S(2)}, u32[]{:S(2)}) collective-permute-start(bf16[2,8,48,256]{3,2,1,0:T(8,128)(2,1)} %collective-permute-done.14.refs_3_), channel_id=1, source_target_pairs={{0,8},{8,0},{1,9},{9,1},{2,10},{10,2},{3,11},{11,3},{16,24},{24,16... | collective-permute-start | bytes 1179656 | tf_op jit(solution)/shard_map/ppermute | solution.py:30
  65.1 29.7 %copy-start.3 = (f32[4]{0:T(128)S(1)}, f32[4]{0:T(128)}, u32[]{:S(2)}) copy-start(f32[4]{0:T(128)} %param.7) | copy-start | bytes 52
  66.9 2.2 %copy-start.1 = (bf16[4,256,2048]{2,1,0:T(8,128)(2,1)S(1)}, bf16[4,256,2048]{2,1,0:T(8,128)(2,1)}, u32[]{:S(2)}) copy-start(bf16[4,256,2048]{2,1,0:T(8,128)(2,1)} %factors_ref.1) | copy-start | bytes 12582916
  80.3 3.9 %collective-permute-start.20 = (f32[4,1536]{1,0:T(4,128)S(1)}, f32[4,1536]{1,0:T(4,128)S(1)}, u32[]{:S(2)}, u32[]{:S(2)}) collective-permute-start(f32[4,1536]{1,0:T(4,128)S(1)} %get-tuple-element.7), channel_id=1, source_target_pairs={{0,1},{8,9},{1,0},{9,8},{2,3},{10,11},{3,2},{11,10},{16,17},{24,25... | collective-permute-start | bytes 73736 | tf_op jit(solution)/shard_map/ppermute | solution.py:30
  84.2 5.1 %collective-permute-start.21 = (f32[4,1536]{1,0:T(4,128)S(1)}, f32[4,1536]{1,0:T(4,128)S(1)}, u32[]{:S(2)}, u32[]{:S(2)}) collective-permute-start(f32[4,1536]{1,0:T(4,128)S(1)} %add.85), channel_id=1, source_target_pairs={{0,3},{8,11},{1,2},{9,10},{2,1},{10,9},{3,0},{11,8},{16,19},{24,27... | collective-permute-start | bytes 73736 | tf_op jit(solution)/shard_map/ppermute | solution.py:30
  89.4 5.4 %collective-permute-start.22 = (f32[4,1536]{1,0:T(4,128)S(1)}, f32[4,1536]{1,0:T(4,128)S(1)}, u32[]{:S(2)}, u32[]{:S(2)}) collective-permute-start(f32[4,1536]{1,0:T(4,128)S(1)} %add.86), channel_id=1, source_target_pairs={{0,4},{8,12},{1,5},{9,13},{2,6},{10,14},{3,7},{11,15},{16,20},{24,... | collective-permute-start | bytes 73736 | tf_op jit(solution)/shard_map/ppermute | solution.py:30
  95.0 1.3 collective-permute-start.23
  96.3 3.8 %collective-permute-start.24 = (f32[2,1536]{1,0:T(2,128)S(1)}, f32[2,1536]{1,0:T(2,128)S(1)}, u32[]{:S(2)}, u32[]{:S(2)}) collective-permute-start(f32[2,1536]{1,0:T(2,128)S(1)} %pad_maximum_fusion.2), channel_id=1, source_target_pairs={{0,16},{8,24},{1,17},{9,25},{2,18},{10,26},{3,19},{11,27},{16,0},{... | collective-permute-start | bytes 36872 | tf_op jit(solution)/shard_map/ppermute | solution.py:30
  100.2 3.8 %collective-permute-start.25 = (f32[2,1536]{1,0:T(2,128)S(1)}, f32[2,1536]{1,0:T(2,128)S(1)}, u32[]{:S(2)}, u32[]{:S(2)}) collective-permute-start(f32[2,1536]{1,0:T(2,128)S(1)} %pad_maximum_fusion.3), channel_id=1, source_target_pairs={{0,32},{8,40},{1,33},{9,41},{2,34},{10,42},{3,35},{11,43},{16,48},... | collective-permute-start | bytes 36872 | tf_op jit(solution)/shard_map/ppermute | solution.py:30
  104.0 5.3 %collective-permute-start.26 = (f32[2,1536]{1,0:T(2,128)S(1)}, f32[2,1536]{1,0:T(2,128)S(1)}, u32[]{:S(2)}, u32[]{:S(2)}) collective-permute-start(f32[2,1536]{1,0:T(2,128)S(1)} %pad_maximum_fusion.4), channel_id=1, source_target_pairs={{0,224},{8,232},{1,225},{9,233},{2,226},{10,234},{3,227},{11,235},... | collective-permute-start | bytes 36872 | tf_op jit(solution)/shard_map/ppermute | solution.py:30
  109.4 6.9 %collective-permute-start.27 = (f32[2,1536]{1,0:T(2,128)S(1)}, f32[2,1536]{1,0:T(2,128)S(1)}, u32[]{:S(2)}, u32[]{:S(2)}) collective-permute-start(f32[2,1536]{1,0:T(2,128)S(1)} %pad_maximum_fusion.5), channel_id=1, source_target_pairs={{0,96},{8,104},{1,97},{9,105},{2,98},{10,106},{3,99},{11,107},{16,... | collective-permute-start | bytes 36872 | tf_op jit(solution)/shard_map/ppermute | solution.py:30
  116.4 2.8 %copy-start = (bf16[1536,2048]{1,0:T(8,128)(2,1)S(1)}, bf16[1536,2048]{1,0:T(8,128)(2,1)}, u32[]{:S(2)}) copy-start(bf16[1536,2048]{1,0:T(8,128)(2,1)} %get-tuple-element.8.own_ref.rows_ref) | copy-start | bytes 18874372

commit v2 on v0

v2 whole, which is shorter than its diff:
```python
import functools

import jax
import jax.numpy as jnp
from jax import lax
from jax.experimental import pallas as pl
from jax.experimental.pallas import tpu as pltpu
from jax.sharding import PartitionSpec as P

AXES = ("wide", "narrow")
NZ, NY, NX = 8, 4, 4


def linear(z, y, x, c):
    return ((z * 2 + y % 2) * 2 + c) * 8 + (y // 2) * 4 + x


def pairs(move):
    out = []
    for z in range(NZ):
        for y in range(NY):
            for x in range(NX):
                for c in range(2):
                    tz, ty, tx, tc = move(z, y, x, c)
                    out.append((linear(z, y, x, c), linear(tz % NZ, ty % NY, tx % NX, tc)))
    return out


def send(value, move):
    return lax.ppermute(value, AXES, pairs(move))


def z_step(d):
    return lambda z, y, x, c: (z + d, y, x, c)


def first_step(d):
    return lambda z, y, x, c: (z, y + d, x, c) if c == 0 else (z, y, x + d, c)


def second_step(d):
    return lambda z, y, x, c: (z, y, x + d, c) if c == 0 else (z, y + d, x, c)


def core_swap(z, y, x, c):
    return (z, y, x, 1 - c)


def place():
    w, n = lax.axis_index("wide"), lax.axis_index("narrow")
    return w // 4, (n // 4) * 2 + (w // 2) % 2, n % 4, w % 2


def column_kernel(spot, *refs):
    out_ref = refs[-1]
    for i, ref in enumerate(refs[:-1]):
        out_ref[(spot[4] + i) % NZ] = ref[...]


def make_column(spot, ring):
    return pl.pallas_call(
        column_kernel,
        out_shape=pltpu.VMEM((NZ,) + ring[0].shape, ring[0].dtype),
        in_specs=[SMEM] + [VMEM] * NZ,
        out_specs=VMEM,
        compiler_params=pltpu.CompilerParams(vmem_limit_bytes=2 * 2**20),
        name="column",
    )(spot, *ring)


def gather(spot, samples, log_det):
    back, ahead, back2, ahead2 = (send(samples, z_step(d)) for d in (1, -1, 2, -2))
    ahead3, back3, far = send(ahead2, z_step(-1)), send(back2, z_step(1)), send(ahead2, z_step(-2))
    column = make_column(spot, [samples, ahead, ahead2, ahead3, far, back3, back2, back])
    before, after, across = (send(column, first_step(d)) for d in (1, -1, 2))
    plane = jnp.stack([column, after, across, before])
    low, high = plane[:2], plane[2:]
    before_low = send(low, second_step(1))
    after_high = send(high, second_step(-1))
    before_high = send(high, second_step(1))
    after_low = send(low, second_step(-1))
    far_low = send(before_low, second_step(1))
    far_high = send(after_high, second_step(-1))
    plane, log_det = lax.optimization_barrier((plane, log_det))
    near = [plane, before_low, after_high, before_high, after_low]
    return lay(spot, FAR, lay(spot, NEAR, None, near), [far_low, far_high]), log_det


NEAR = ((0, 0, 4), (3, 0, 2), (1, 2, 2), (3, 2, 2), (1, 0, 2))
FAR = ((2, 0, 2), (2, 2, 2))
VMEM = pl.BlockSpec(memory_space=pltpu.VMEM)
ANY = pl.BlockSpec(memory_space=pl.ANY)
SMEM = pl.BlockSpec(memory_space=pltpu.SMEM)


def lay_kernel(places, has_rows, spot, *refs):
    parts = refs[has_rows : has_rows + len(places)]
    rows, sems = refs[-2:]
    here_y, here_x = spot[0], spot[1]
    core = spot[2]
    blocks = rows.reshape(NZ, 2, 48, rows.shape[1])
    copies = []
    for part, (second, first, many) in zip(parts, places, strict=True):
        for i in range(many):
            ay, ax = (here_y + first + i) % 4, (here_x + second) % 4
            by, bx = (here_y + second) % 4, (here_x + first + i) % 4
            at_y = jnp.where(core == 0, ay, by)
            at_x = jnp.where(core == 0, ax, bx)
            col = pl.multiple_of(((at_y // 2) * 4 + at_x) * 256, 256)
            copy = pltpu.make_async_copy(
                part.at[i], blocks.at[:, at_y % 2, :, pl.ds(col, 256)], sems.at[len(copies)]
            )
            copy.start()
            copies.append(copy)
    for copy in copies:
        copy.wait()


def lay(spot, places, rows, parts):
    has_rows = 0 if rows is None else 1
    return pl.pallas_call(
        functools.partial(lay_kernel, places, has_rows),
        out_shape=pltpu.VMEM((768, 2048), jnp.bfloat16),
        in_specs=[SMEM] + [VMEM] * has_rows + [ANY] * len(parts),
        out_specs=VMEM,
        scratch_shapes=[pltpu.SemaphoreType.DMA((12,))],
        input_output_aliases={1: 0} if has_rows else {},
        compiler_params=pltpu.CompilerParams(vmem_limit_bytes=2 * 2**20),
        name="lay",
    )(spot, *([rows] if has_rows else []), *parts)


def log_det_kernel(spot, factors_ref, log_det_ref, square, sem):
    comps, span, _ = factors_ref.shape
    own = pl.multiple_of(spot[3] * span, span)
    copy = pltpu.make_async_copy(factors_ref.at[:, :, pl.ds(own, span)], square, sem)
    copy.start()
    eye = lax.broadcasted_iota(jnp.int32, (span, span), 0) == lax.broadcasted_iota(
        jnp.int32, (span, span), 1
    )
    copy.wait()
    for k in range(comps):
        diag = jnp.sum(jnp.where(eye, square[k].astype(jnp.float32), 0.0), axis=1, keepdims=True)
        total = jnp.sum(jnp.log(diag), axis=0, keepdims=True)
        log_det_ref[k : k + 1, :] = jnp.broadcast_to(total, (1, log_det_ref.shape[1]))


def log_dets(spot, factors):
    comps, span, _ = factors.shape
    return pl.pallas_call(
        log_det_kernel,
        out_shape=jax.ShapeDtypeStruct((comps, 128), jnp.float32),
        in_specs=[SMEM, ANY],
        out_specs=VMEM,
        scratch_shapes=[pltpu.VMEM((comps, span, span), factors.dtype), pltpu.SemaphoreType.DMA],
        compiler_params=pltpu.CompilerParams(vmem_limit_bytes=4 * 2**20),
        name="log_dets",
    )(spot, factors)


def score_kernel(offsets_ref, log_det_ref, factors_ref, rows_ref, partial_ref):
    comps, span, feats = factors_ref.shape
    offsets = offsets_ref[...].T
    projected = lax.dot_general(
        factors_ref[...].reshape(comps * span, feats),
        rows_ref[...],
        (((1,), (1,)), ((), ())),
        preferred_element_type=jnp.float32,
    )
    for k in range(comps):
        centered = projected[k * span : (k + 1) * span] - offsets[:, k : k + 1]
        quadratic = jnp.sum(centered * centered, axis=0, keepdims=True)
        partial_ref[k : k + 1, :] = log_det_ref[k : k + 1, 0:1] - 0.5 * quadratic


def score(offsets, log_det, factors, rows):
    comps, span, feats = factors.shape
    total = rows.shape[0]
    return pl.pallas_call(
        score_kernel,
        out_shape=jax.ShapeDtypeStruct((comps, total), jnp.float32),
        in_specs=[VMEM, VMEM, VMEM, VMEM],
        out_specs=VMEM,
        compiler_params=pltpu.CompilerParams(vmem_limit_bytes=10 * 2**20),
        cost_estimate=pl.CostEstimate(
            flops=2 * total * comps * span * feats, bytes_accessed=8 * 2**20, transcendentals=0
        ),
        name="score",
    )(offsets, log_det, factors, rows)


def score_moved_kernel(offsets_ref, log_det_ref, factors_ref, rows_ref, partial_ref, held, sem):
    copy = pltpu.make_async_copy(rows_ref, held, sem)
    copy.start()
    copy.wait()
    score_kernel(offsets_ref, log_det_ref, factors_ref, held, partial_ref)


def score_moved(offsets, log_det, factors, rows):
    comps, span, feats = factors.shape
    total = rows.shape[0]
    return pl.pallas_call(
        score_moved_kernel,
        out_shape=(
            jax.ShapeDtypeStruct((comps, total), jnp.float32),
            pltpu.VMEM(rows.shape, rows.dtype),
        ),
        in_specs=[VMEM, VMEM, VMEM, ANY],
        out_specs=(VMEM, VMEM),
        scratch_shapes=[pltpu.SemaphoreType.DMA],
        compiler_params=pltpu.CompilerParams(vmem_limit_bytes=10 * 2**20),
        cost_estimate=pl.CostEstimate(
            flops=2 * total * comps * span * feats, bytes_accessed=8 * 2**20, transcendentals=0
        ),
        name="score_moved",
    )(offsets, log_det, factors, rows)


def turn_kernel(spot, mine_ref, theirs_ref, out_ref):
    span, half = out_ref.shape[0], mine_ref.shape[0]
    own = pl.multiple_of(spot[3] * span, span)
    out_ref[:, :half] = mine_ref[:, pl.ds(own, span)].T
    out_ref[:, half:] = theirs_ref[:, pl.ds(own, span)].T


def turn(spot, mine, theirs, span):
    return pl.pallas_call(
        turn_kernel,
        out_shape=pltpu.VMEM((span, 2 * mine.shape[0]), mine.dtype),
        in_specs=[SMEM, VMEM, VMEM],
        out_specs=VMEM,
        compiler_params=pltpu.CompilerParams(vmem_limit_bytes=4 * 2**20),
        name="turn",
    )(spot, mine, theirs)


def moment_kernel(spot, resp_ref, own_ref, mine_ref, theirs_ref, means_ref, cov_ref, all_means, stage, sems):
    comps, total = resp_ref.shape
    span, half = own_ref.shape[0], mine_ref.shape[0]
    feats = mine_ref.shape[1]
    core = spot[2]
    resp = jnp.concatenate(
        [
            resp_ref[:, pl.ds(pl.multiple_of(core * half, half), half)],
            resp_ref[:, pl.ds(pl.multiple_of((1 - core) * half, half), half)],
        ],
        axis=1,
    )
    inverse = 1.0 / (jnp.sum(resp, axis=1, keepdims=True) + 1.0)
    high = resp.astype(jnp.bfloat16)
    low = (resp - high.astype(jnp.float32)).astype(jnp.bfloat16)
    zero = jnp.zeros((8, total), jnp.bfloat16)

    def product(left, cols):
        right = jnp.concatenate([mine_ref[:, cols], theirs_ref[:, cols]], axis=0)
        return jnp.dot(left, right, preferred_element_type=jnp.float32)

    sums = product(jnp.concatenate([high, low, zero], axis=0), pl.ds(0, feats))
    all_means[...] = (sums[:comps] + sums[comps : 2 * comps]) * inverse
    means_ref[...] = all_means[:, pl.ds(pl.multiple_of(spot[3] * span, span), span)]
    copies = []
    for k in range(comps):
        weighted = own_ref[...].astype(jnp.float32) * resp[k : k + 1]
        own_means = jnp.sum(weighted, axis=1, keepdims=True) * inverse[k : k + 1]
        left = weighted.astype(jnp.bfloat16)
        tile = feats if k + 1 < comps else feats // 4
        for at in range(0, feats, tile):
            cols = pl.ds(at, tile)
            gram = product(left, cols)
            stage[k, :, cols] = (
                gram * inverse[k : k + 1] - own_means * all_means[k : k + 1, cols]
            ).astype(jnp.bfloat16)
            copy = pltpu.make_async_copy(stage.at[k, :, cols], cov_ref.at[k, :, cols], sems.at[len(copies)])
            copy.start()
            copies.append(copy)
    for copy in copies:
        copy.wait()


def moments(spot, resp, own, mine, theirs):
    comps, total = resp.shape
    span, feats = own.shape[0], mine.shape[1]
    return pl.pallas_call(
        moment_kernel,
        out_shape=(
            jax.ShapeDtypeStruct((comps, span), jnp.float32),
            jax.ShapeDtypeStruct((comps, span, feats), jnp.bfloat16),
        ),
        in_specs=[SMEM, VMEM, VMEM, VMEM, VMEM],
        out_specs=(VMEM, ANY),
        scratch_shapes=[
            pltpu.VMEM((comps, feats), jnp.float32),
            pltpu.VMEM((comps, span, feats), jnp.bfloat16),
            pltpu.SemaphoreType.DMA((comps + 3,)),
        ],
        compiler_params=pltpu.CompilerParams(vmem_limit_bytes=14 * 2**20),
        name="moments",
    )(spot, resp, own, mine, theirs)


def x_even(z, y, x, c):
    return (z, y, x ^ 1, c)


def x_odd(z, y, x, c):
    return (z, y, 3 - x, c)


def y_far(z, y, x, c):
    return (z, y + 2, x, c)


def y_near(z, y, x, c):
    return (z, y ^ 1, x, c)


def z_even(z, y, x, c):
    return (z ^ 1, y, x, c)


def z_odd(z, y, x, c):
    return (z + 1 if z % 2 else z - 1, y, x, c)


Z_LAST = {1: 6, 6: 1, 2: 5, 5: 2, 3: 0, 0: 3, 4: 7, 7: 4}


def z_far(z, y, x, c):
    return (Z_LAST[z], y, x, c)


def shards(samples, inverse_factors, offsets, log_weights):
    z, y, x, c = place()
    rows_here = samples.shape[0]
    spot = jnp.stack([y, x, c, lax.axis_index("narrow"), z]).astype(jnp.int32)
    span = inverse_factors.shape[1]
    log_det = log_dets(spot, inverse_factors)
    mine, log_det = gather(spot, samples, log_det)
    theirs = send(mine, core_swap)
    first = score(offsets, log_det, inverse_factors, mine)
    second, theirs = score_moved(offsets, log_det, inverse_factors, theirs)
    own = turn(spot, mine, theirs, span)
    loglik = jnp.where(
        c == 0, jnp.concatenate([first, second], axis=1), jnp.concatenate([second, first], axis=1)
    )
    for move in (x_even, x_odd, y_far):
        loglik = loglik + send(loglik, move)
    loglik = loglik + log_weights[:, None]
    peak = jnp.max(loglik, axis=0)
    total = jnp.sum(jnp.exp(loglik - peak[None, :]), axis=0)
    pair = jnp.stack([peak, total])
    for move in (core_swap, y_near, z_even, z_odd, z_far):
        other = send(pair, move)
        peak = jnp.maximum(pair[0], other[0])
        total = pair[1] * jnp.exp(pair[0] - peak) + other[1] * jnp.exp(other[0] - peak)
        pair = jnp.stack([peak, total])
    log_norm = jnp.log(pair[1])
    responsibility = jnp.exp((loglik - pair[0][None, :]) - log_norm[None, :])
    means, covariance = moments(spot, responsibility, own, mine, theirs)
    first_row = ((c * NZ + z) * 2 + y % 2) * rows_here
    own_norm = lax.dynamic_slice_in_dim(log_norm, first_row, rows_here, 0)
    return (own_norm, means, covariance)


def solution(mesh):
    return jax.shard_map(
        shards,
        mesh=mesh,
        in_specs=(P("wide", "narrow"), P("wide", "narrow", None), P("wide", "narrow"), P("wide")),
        out_specs=(P("wide"), P("wide", "narrow"), P("wide", "narrow", None)),
        check_vma=False,
    )
```

time: 309 us -> 111 us (0.36)
  the two profiles are of different devices: /device:TPU:1 before, /device:TPU:8 now
where the time goes in v2:
time: 111 us; the launch traced here: 110 us
  waiting for transfers between devices  39.5 us (36%)
  starting transfers between devices  36.6 us (33%)
  Pallas kernels  23.1 us (21%)
  local copies, waits for them, and re-layouts  8.77 us (8%)
  other arithmetic  1.36 us (1%)
    ppermute x25, waiting for transfers between devices, send(): return lax.ppermute(value, AXES, pairs(move))  39.5 us
    ppermute x25, starting transfers between devices, send(): return lax.ppermute(value, AXES, pairs(move))  36.6 us
    pallas_call x1, Pallas kernels, moments(): pl.pallas_call(moment_kernel, out_shape=(jax.ShapeDtypeStruct((comps, spa...  10.2 us
    unnamed x16, local copies, waits for them, and re-layouts  8.67 us
    pallas_call x1, Pallas kernels, score_moved(): pl.pallas_call(score_moved_kernel, out_shape=(jax.ShapeDtypeStruct((comps...  5.42 us
    pallas_call x1, Pallas kernels, score(): pl.pallas_call(score_kernel, out_shape=jax.ShapeDtypeStruct((comps, total...  3.45 us
  transfers between devices with their start and end apart: 25, of which 20 were waited for; matrix products, arithmetic and copies ran while one was open for 0% of the time, Pallas kernels for 6%

profile of v2, /device:TPU:8, one launch (start us, length us, event | category | flops | bytes accessed | tf_op | source)
XLA Modules:
  0.0 110.2 jit_solution(11740453807044862403)
XLA Ops:
  0.6 3.3 %collective-permute-start.4 = (bf16[48,256]{1,0:T(8,128)(2,1)}, bf16[48,256]{1,0:T(8,128)(2,1)S(1)}, u32[]{:S(2)}, u32[]{:S(2)}) collective-permute-start(bf16[48,256]{1,0:T(8,128)(2,1)} %refs_0_.1), channel_id=1, source_target_pairs={{0,64},{8,72},{1,65},{9,73},{2,66},{10,74},{3,67},{11,75},{16,80},... | collective-permute-start | bytes 73736 | tf_op jit(solution)/shard_map/ppermute | solution.py:30
  4.0 3.1 %collective-permute-start.1 = (bf16[48,256]{1,0:T(8,128)(2,1)}, bf16[48,256]{1,0:T(8,128)(2,1)S(1)}, u32[]{:S(2)}, u32[]{:S(2)}) collective-permute-start(bf16[48,256]{1,0:T(8,128)(2,1)} %refs_0_.1), channel_id=1, source_target_pairs={{0,192},{8,200},{1,193},{9,201},{2,194},{10,202},{3,195},{11,203},... | collective-permute-start | bytes 73736 | tf_op jit(solution)/shard_map/ppermute | solution.py:30
  7.1 2.4 %collective-permute-start = (bf16[48,256]{1,0:T(8,128)(2,1)}, bf16[48,256]{1,0:T(8,128)(2,1)S(1)}, u32[]{:S(2)}, u32[]{:S(2)}) collective-permute-start(bf16[48,256]{1,0:T(8,128)(2,1)} %refs_0_.1), channel_id=1, source_target_pairs={{0,224},{8,232},{1,225},{9,233},{2,226},{10,234},{3,227},{11,235},... | collective-permute-start | bytes 73736 | tf_op jit(solution)/shard_map/ppermute | solution.py:30
  10.5 3.7 %collective-permute-start.3 = (bf16[48,256]{1,0:T(8,128)(2,1)S(1)}, bf16[48,256]{1,0:T(8,128)(2,1)S(1)}, u32[]{:S(2)}, u32[]{:S(2)}) collective-permute-start(bf16[48,256]{1,0:T(8,128)(2,1)S(1)} %collective-permute-done.1.refs_2_), channel_id=1, source_target_pairs={{0,192},{8,200},{1,193},{9,201},{2,194},{10,202},{3,195},{11,203},... | collective-permute-start | bytes 73736 | tf_op jit(solution)/shard_map/ppermute | solution.py:30
  15.0 1.4 %collective-permute-done.3.refs_4_ = bf16[48,256]{1,0:T(8,128)(2,1)S(1)} collective-permute-done((bf16[48,256]{1,0:T(8,128)(2,1)S(1)}, bf16[48,256]{1,0:T(8,128)(2,1)S(1)}, u32[]{:S(2)}, u32[]{:S(2)}) %collective-permute-start.3) | collective-permute-done | bytes 24608 | tf_op jit(solution)/shard_map/ppermute | solution.py:30
  16.4 1.6 %collective-permute-done.2.refs_3_ = bf16[48,256]{1,0:T(8,128)(2,1)S(1)} collective-permute-done((bf16[48,256]{1,0:T(8,128)(2,1)S(1)}, bf16[48,256]{1,0:T(8,128)(2,1)S(1)}, u32[]{:S(2)}, u32[]{:S(2)}) %collective-permute-start.2) | collective-permute-done | bytes 24608 | tf_op jit(solution)/shard_map/ppermute | solution.py:30
  19.3 1.7 %collective-permute-start.9 = (bf16[8,48,256]{2,1,0:T(8,128)(2,1)S(1)}, bf16[8,48,256]{2,1,0:T(8,128)(2,1)S(1)}, u32[]{:S(2)}, u32[]{:S(2)}) collective-permute-start(bf16[8,48,256]{2,1,0:T(8,128)(2,1)S(1)} %column.1), channel_id=1, source_target_pairs={{0,16},{8,9},{1,17},{9,10},{2,18},{10,11},{3,19},{11,8},{16,4},{24... | collective-permute-start | bytes 589832 | tf_op jit(solution)/shard_map/ppermute | solution.py:30
  21.9 2.4 %collective-permute-start.7 = (bf16[8,48,256]{2,1,0:T(8,128)(2,1)S(1)}, bf16[8,48,256]{2,1,0:T(8,128)(2,1)S(1)}, u32[]{:S(2)}, u32[]{:S(2)}) collective-permute-start(bf16[8,48,256]{2,1,0:T(8,128)(2,1)S(1)} %column.1), channel_id=1, source_target_pairs={{0,20},{8,11},{1,21},{9,8},{2,22},{10,9},{3,23},{11,10},{16,0},{24... | collective-permute-start | bytes 589832 | tf_op jit(solution)/shard_map/ppermute | solution.py:30
  25.1 3.2 %collective-permute-done.8 = bf16[8,48,256]{2,1,0:T(8,128)(2,1)S(1)} collective-permute-done((bf16[8,48,256]{2,1,0:T(8,128)(2,1)S(1)}, bf16[8,48,256]{2,1,0:T(8,128)(2,1)S(1)}, u32[]{:S(2)}, u32[]{:S(2)}) %collective-permute-start.8) | collective-permute-done | bytes 196640 | tf_op jit(solution)/shard_map/ppermute | solution.py:30
  28.3 4.5 %collective-permute-start.11 = (bf16[2,8,48,256]{3,2,1,0:T(8,128)(2,1)S(1)}, bf16[2,8,48,256]{3,2,1,0:T(8,128)(2,1)S(1)}, u32[]{:S(2)}, u32[]{:S(2)}) collective-permute-start(bf16[2,8,48,256]{3,2,1,0:T(8,128)(2,1)S(1)} %pad_maximum_fusion.2), channel_id=1, source_target_pairs={{0,3},{8,28},{1,0},{9,29},{2,1},{10,30},{3,2},{11,31},{16,19},{24,... | collective-permute-start | bytes 1179656 | tf_op jit(solution)/shard_map/ppermute | solution.py:30
  32.9 1.4 %collective-permute-start.12 = (bf16[2,8,48,256]{3,2,1,0:T(8,128)(2,1)S(1)}, bf16[2,8,48,256]{3,2,1,0:T(8,128)(2,1)S(1)}, u32[]{:S(2)}, u32[]{:S(2)}) collective-permute-start(bf16[2,8,48,256]{3,2,1,0:T(8,128)(2,1)S(1)} %pad_maximum_fusion.2), channel_id=1, source_target_pairs={{0,1},{8,24},{1,2},{9,25},{2,3},{10,26},{3,0},{11,27},{16,17},{24,... | collective-permute-start | bytes 1179656 | tf_op jit(solution)/shard_map/ppermute | solution.py:30
  34.3 1.9 %collective-permute-start.13 = (bf16[2,8,48,256]{3,2,1,0:T(8,128)(2,1)S(1)}, bf16[2,8,48,256]{3,2,1,0:T(8,128)(2,1)S(1)}, u32[]{:S(2)}, u32[]{:S(2)}) collective-permute-start(bf16[2,8,48,256]{3,2,1,0:T(8,128)(2,1)S(1)} %pad_maximum_fusion.1), channel_id=1, source_target_pairs={{0,3},{8,28},{1,0},{9,29},{2,1},{10,30},{3,2},{11,31},{16,19},{24,... | collective-permute-start | bytes 1179656 | tf_op jit(solution)/shard_map/ppermute | solution.py:30
  36.3 1.8 %collective-permute-done.11.refs_2_ = bf16[2,8,48,256]{3,2,1,0:T(8,128)(2,1)S(1)} collective-permute-done((bf16[2,8,48,256]{3,2,1,0:T(8,128)(2,1)S(1)}, bf16[2,8,48,256]{3,2,1,0:T(8,128)(2,1)S(1)}, u32[]{:S(2)}, u32[]{:S(2)}) %collective-permute-start.11) | collective-permute-done | bytes 393248 | tf_op jit(solution)/shard_map/ppermute | solution.py:30
  38.1 3.7 %collective-permute-start.15 = (bf16[2,8,48,256]{3,2,1,0:T(8,128)(2,1)S(1)}, bf16[2,8,48,256]{3,2,1,0:T(8,128)(2,1)S(1)}, u32[]{:S(2)}, u32[]{:S(2)}) collective-permute-start(bf16[2,8,48,256]{3,2,1,0:T(8,128)(2,1)S(1)} %collective-permute-done.11.refs_2_), channel_id=1, source_target_pairs={{0,3},{8,28},{1,0},{9,29},{2,1},{10,30},{3,2},{11,31},{16,19},{24,... | collective-permute-start | bytes 1179656 | tf_op jit(solution)/shard_map/ppermute | solution.py:30
  41.9 2.2 %copy-done.3 = bf16[4,256,2048]{2,1,0:T(8,128)(2,1)S(1)} copy-done((bf16[4,256,2048]{2,1,0:T(8,128)(2,1)S(1)}, bf16[4,256,2048]{2,1,0:T(8,128)(2,1)}, u32[]{:S(2)}) %copy-start.3) | copy-done | bytes 4194328
  47.2 3.7 %collective-permute-done.14.refs_1_ = bf16[2,8,48,256]{3,2,1,0:T(8,128)(2,1)S(1)} collective-permute-done((bf16[2,8,48,256]{3,2,1,0:T(8,128)(2,1)S(1)}, bf16[2,8,48,256]{3,2,1,0:T(8,128)(2,1)S(1)}, u32[]{:S(2)}, u32[]{:S(2)}) %collective-permute-start.14) | collective-permute-done | bytes 393248 | tf_op jit(solution)/shard_map/ppermute | solution.py:30
  51.8 2.2 %copy-done.4 = bf16[4,256,2048]{2,1,0:T(8,128)(2,1)S(1)} copy-done((bf16[4,256,2048]{2,1,0:T(8,128)(2,1)S(1)}, bf16[4,256,2048]{2,1,0:T(8,128)(2,1)}, u32[]{:S(2)}) %copy-start.4) | copy-done | bytes 4194328
  54.0 3.5 %score.1 = f32[4,768]{1,0:T(4,128)S(1)} custom-call(f32[4,256]{1,0:T(4,128)S(1)} %copy-done.6, f32[4,128]{1,0:T(4,128)S(1)} %log_dets.1.log_det_ref, bf16[4,256,2048]{2,1,0:T(8,128)(2,1)S(1)} %copy-done.4, bf16[768,2048]{1,0:T(8,128)(2,1)S(1)} %lay.3.rows_ref.mine_ref), custom_call_target="tpu_custom_call" | custom-call | flops 3221225472 | bytes 8388608 | tf_op jit(solution)/shard_map/score/pallas_call | solution.py:179
  57.6 5.4 %score_moved.1 = (f32[4,768]{1,0:T(4,128)S(1)}, bf16[768,2048]{1,0:T(8,128)(2,1)S(1)}) custom-call(f32[4,256]{1,0:T(4,128)S(1)} %copy-done.6, f32[4,128]{1,0:T(4,128)S(1)} %log_dets.1.log_det_ref, bf16[4,256,2048]{2,1,0:T(8,128)(2,1)S(1)} %copy-done.4, bf16[768,2048]{1,0:T(8,128)(2,1)} %collective-permute-done.16.rows_ref), custom_call_target="tpu_custom_call" | custom-call | flops 3221225472 | bytes 8388608 | tf_op jit(solution)/shard_map/score_moved/pallas_call | solution.py:202
  63.0 1.7 %copy-done = bf16[768,2048]{1,0:T(8,128)(2,1)} copy-done((bf16[768,2048]{1,0:T(8,128)(2,1)}, bf16[768,2048]{1,0:T(8,128)(2,1)S(1)}, u32[]{:S(2)}) %copy-start) | copy-done | bytes 3145752
  64.8 3.8 %collective-permute-done.17 = f32[4,1536]{1,0:T(4,128)S(1)} collective-permute-done((f32[4,1536]{1,0:T(4,128)S(1)}, f32[4,1536]{1,0:T(4,128)S(1)}, u32[]{:S(2)}, u32[]{:S(2)}) %collective-permute-start.17) | collective-permute-done | bytes 24608 | tf_op jit(solution)/shard_map/ppermute | solution.py:30
  68.7 5.0 %collective-permute-done.18 = f32[4,1536]{1,0:T(4,128)S(1)} collective-permute-done((f32[4,1536]{1,0:T(4,128)S(1)}, f32[4,1536]{1,0:T(4,128)S(1)}, u32[]{:S(2)}, u32[]{:S(2)}) %collective-permute-start.18) | collective-permute-done | bytes 24608 | tf_op jit(solution)/shard_map/ppermute | solution.py:30
  73.8 1.1 %collective-permute-start.19 = (f32[4,1536]{1,0:T(4,128)S(1)}, f32[4,1536]{1,0:T(4,128)S(1)}, u32[]{:S(2)}, u32[]{:S(2)}) collective-permute-start(f32[4,1536]{1,0:T(4,128)S(1)} %add.90), channel_id=1, source_target_pairs={{0,4},{8,12},{1,5},{9,13},{2,6},{10,14},{3,7},{11,15},{16,20},{24,... | collective-permute-start | bytes 73736 | tf_op jit(solution)/shard_map/ppermute | solution.py:30
  74.9 4.3 %collective-permute-done.19 = f32[4,1536]{1,0:T(4,128)S(1)} collective-permute-done((f32[4,1536]{1,0:T(4,128)S(1)}, f32[4,1536]{1,0:T(4,128)S(1)}, u32[]{:S(2)}, u32[]{:S(2)}) %collective-permute-start.19) | collective-permute-done | bytes 24608 | tf_op jit(solution)/shard_map/ppermute | solution.py:30
  79.5 1.2 %collective-permute-done.20 = f32[2,1536]{1,0:T(2,128)S(1)} collective-permute-done((f32[2,1536]{1,0:T(2,128)S(1)}, f32[2,1536]{1,0:T(2,128)S(1)}, u32[]{:S(2)}, u32[]{:S(2)}) %collective-permute-start.20) | collective-permute-done | bytes 12320 | tf_op jit(solution)/shard_map/ppermute | solution.py:30
  81.1 1.9 %copy-done.1 = bf16[768,2048]{1,0:T(8,128)(2,1)S(1)} copy-done((bf16[768,2048]{1,0:T(8,128)(2,1)S(1)}, bf16[768,2048]{1,0:T(8,128)(2,1)}, u32[]{:S(2)}) %copy-start.1) | copy-done | bytes 3145752
  84.7 3.7 %collective-permute-done.22 = f32[2,1536]{1,0:T(2,128)S(1)} collective-permute-done((f32[2,1536]{1,0:T(2,128)S(1)}, f32[2,1536]{1,0:T(2,128)S(1)}, u32[]{:S(2)}, u32[]{:S(2)}) %collective-permute-start.22) | collective-permute-done | bytes 12320 | tf_op jit(solution)/shard_map/ppermute | solution.py:30
  88.4 1.3 %collective-permute-start.23 = (f32[2,1536]{1,0:T(2,128)S(1)}, f32[2,1536]{1,0:T(2,128)S(1)}, u32[]{:S(2)}, u32[]{:S(2)}) collective-permute-start(f32[2,1536]{1,0:T(2,128)S(1)} %pad_maximum_fusion.6), channel_id=1, source_target_pairs={{0,224},{8,232},{1,225},{9,233},{2,226},{10,234},{3,227},{11,235},... | collective-permute-start | bytes 36872 | tf_op jit(solution)/shard_map/ppermute | solution.py:30
  89.7 3.7 %collective-permute-done.23 = f32[2,1536]{1,0:T(2,128)S(1)} collective-permute-done((f32[2,1536]{1,0:T(2,128)S(1)}, f32[2,1536]{1,0:T(2,128)S(1)}, u32[]{:S(2)}, u32[]{:S(2)}) %collective-permute-start.23) | collective-permute-done | bytes 12320 | tf_op jit(solution)/shard_map/ppermute | solution.py:30
  93.5 3.2 %collective-permute-start.24 = (f32[2,1536]{1,0:T(2,128)S(1)}, f32[2,1536]{1,0:T(2,128)S(1)}, u32[]{:S(2)}, u32[]{:S(2)}) collective-permute-start(f32[2,1536]{1,0:T(2,128)S(1)} %pad_maximum_fusion.7), channel_id=1, source_target_pairs={{0,96},{8,104},{1,97},{9,105},{2,98},{10,106},{3,99},{11,107},{16,... | collective-permute-start | bytes 36872 | tf_op jit(solution)/shard_map/ppermute | solution.py:30
  96.7 2.6 %collective-permute-done.24 = f32[2,1536]{1,0:T(2,128)S(1)} collective-permute-done((f32[2,1536]{1,0:T(2,128)S(1)}, f32[2,1536]{1,0:T(2,128)S(1)}, u32[]{:S(2)}, u32[]{:S(2)}) %collective-permute-start.24) | collective-permute-done | bytes 12320 | tf_op jit(solution)/shard_map/ppermute | solution.py:30
  99.4 10.2 %moments.1 = (f32[4,256]{1,0:T(4,128)}, bf16[4,256,2048]{2,1,0:T(8,128)(2,1)}) custom-call(s32[5]{0:T(128)S(1)} %stack.70.spot, f32[4,1536]{1,0:T(4,128)S(1)} %subtract_exponential_fusion.resp_ref, bf16[256,1536]{1,0:T(8,128)(2,1)S(1)} %turn.1.own_ref, bf16[768,2048]{1,0:T(8,128)(2,1)S(1)} %lay.3.rows_ref.mine_ref, bf16[768,2048]{1,0:T(8,128)(2,1)S(1)} %copy-done.2), custom_call_target="tpu_custom_call" | custom-call | tf_op jit(solution)/shard_map/moments/pallas_call | solution.py:283
  (69 shorter events, 12.6 us)
Async XLA Ops:
  0.6 8.9 %collective-permute-start.4 = (bf16[48,256]{1,0:T(8,128)(2,1)}, bf16[48,256]{1,0:T(8,128)(2,1)S(1)}, u32[]{:S(2)}, u32[]{:S(2)}) collective-permute-start(bf16[48,256]{1,0:T(8,128)(2,1)} %refs_0_.1), channel_id=1, source_target_pairs={{0,64},{8,72},{1,65},{9,73},{2,66},{10,74},{3,67},{11,75},{16,80},... | collective-permute-start | bytes 73736 | tf_op jit(solution)/shard_map/ppermute | solution.py:30
  4.0 6.5 %collective-permute-start.1 = (bf16[48,256]{1,0:T(8,128)(2,1)}, bf16[48,256]{1,0:T(8,128)(2,1)S(1)}, u32[]{:S(2)}, u32[]{:S(2)}) collective-permute-start(bf16[48,256]{1,0:T(8,128)(2,1)} %refs_0_.1), channel_id=1, source_target_pairs={{0,192},{8,200},{1,193},{9,201},{2,194},{10,202},{3,195},{11,203},... | collective-permute-start | bytes 73736 | tf_op jit(solution)/shard_map/ppermute | solution.py:30
  7.1 7.4 %collective-permute-start = (bf16[48,256]{1,0:T(8,128)(2,1)}, bf16[48,256]{1,0:T(8,128)(2,1)S(1)}, u32[]{:S(2)}, u32[]{:S(2)}) collective-permute-start(bf16[48,256]{1,0:T(8,128)(2,1)} %refs_0_.1), channel_id=1, source_target_pairs={{0,224},{8,232},{1,225},{9,233},{2,226},{10,234},{3,227},{11,235},... | collective-permute-start | bytes 73736 | tf_op jit(solution)/shard_map/ppermute | solution.py:30
  9.5 5.2 %collective-permute-start.6 = (bf16[48,256]{1,0:T(8,128)(2,1)}, bf16[48,256]{1,0:T(8,128)(2,1)S(1)}, u32[]{:S(2)}, u32[]{:S(2)}) collective-permute-start(bf16[48,256]{1,0:T(8,128)(2,1)} %refs_0_.1), channel_id=1, source_target_pairs={{0,32},{8,40},{1,33},{9,41},{2,34},{10,42},{3,35},{11,43},{16,48},... | collective-permute-start | bytes 73736 | tf_op jit(solution)/shard_map/ppermute | solution.py:30
  9.5 5.5 %collective-permute-start.5 = (bf16[48,256]{1,0:T(8,128)(2,1)S(1)}, bf16[48,256]{1,0:T(8,128)(2,1)S(1)}, u32[]{:S(2)}, u32[]{:S(2)}) collective-permute-start(bf16[48,256]{1,0:T(8,128)(2,1)S(1)} %collective-permute-done.4.refs_6_), channel_id=1, source_target_pairs={{0,32},{8,40},{1,33},{9,41},{2,34},{10,42},{3,35},{11,43},{16,48},... | collective-permute-start | bytes 73736 | tf_op jit(solution)/shard_map/ppermute | solution.py:30
  10.5 5.9 %collective-permute-start.3 = (bf16[48,256]{1,0:T(8,128)(2,1)S(1)}, bf16[48,256]{1,0:T(8,128)(2,1)S(1)}, u32[]{:S(2)}, u32[]{:S(2)}) collective-permute-start(bf16[48,256]{1,0:T(8,128)(2,1)S(1)} %collective-permute-done.1.refs_2_), channel_id=1, source_target_pairs={{0,192},{8,200},{1,193},{9,201},{2,194},{10,202},{3,195},{11,203},... | collective-permute-start | bytes 73736 | tf_op jit(solution)/shard_map/ppermute | solution.py:30
  14.2 3.8 %collective-permute-start.2 = (bf16[48,256]{1,0:T(8,128)(2,1)S(1)}, bf16[48,256]{1,0:T(8,128)(2,1)S(1)}, u32[]{:S(2)}, u32[]{:S(2)}) collective-permute-start(bf16[48,256]{1,0:T(8,128)(2,1)S(1)} %collective-permute-done.1.refs_2_), channel_id=1, source_target_pairs={{0,224},{8,232},{1,225},{9,233},{2,226},{10,234},{3,227},{11,235},... | collective-permute-start | bytes 73736 | tf_op jit(solution)/shard_map/ppermute | solution.py:30
  19.3 5.7 %collective-permute-start.9 = (bf16[8,48,256]{2,1,0:T(8,128)(2,1)S(1)}, bf16[8,48,256]{2,1,0:T(8,128)(2,1)S(1)}, u32[]{:S(2)}, u32[]{:S(2)}) collective-permute-start(bf16[8,48,256]{2,1,0:T(8,128)(2,1)S(1)} %column.1), channel_id=1, source_target_pairs={{0,16},{8,9},{1,17},{9,10},{2,18},{10,11},{3,19},{11,8},{16,4},{24... | collective-permute-start | bytes 589832 | tf_op jit(solution)/shard_map/ppermute | solution.py:30
  21.0 7.3 %collective-permute-start.8 = (bf16[8,48,256]{2,1,0:T(8,128)(2,1)S(1)}, bf16[8,48,256]{2,1,0:T(8,128)(2,1)S(1)}, u32[]{:S(2)}, u32[]{:S(2)}) collective-permute-start(bf16[8,48,256]{2,1,0:T(8,128)(2,1)S(1)} %column.1), channel_id=1, source_target_pairs={{0,4},{8,10},{1,5},{9,11},{2,6},{10,8},{3,7},{11,9},{16,20},{24,26... | collective-permute-start | bytes 589832 | tf_op jit(solution)/shard_map/ppermute | solution.py:30
  21.9 10.9 %collective-permute-start.7 = (bf16[8,48,256]{2,1,0:T(8,128)(2,1)S(1)}, bf16[8,48,256]{2,1,0:T(8,128)(2,1)S(1)}, u32[]{:S(2)}, u32[]{:S(2)}) collective-permute-start(bf16[8,48,256]{2,1,0:T(8,128)(2,1)S(1)} %column.1), channel_id=1, source_target_pairs={{0,20},{8,11},{1,21},{9,8},{2,22},{10,9},{3,23},{11,10},{16,0},{24... | collective-permute-start | bytes 589832 | tf_op jit(solution)/shard_map/ppermute | solution.py:30
  28.3 9.8 %collective-permute-start.11 = (bf16[2,8,48,256]{3,2,1,0:T(8,128)(2,1)S(1)}, bf16[2,8,48,256]{3,2,1,0:T(8,128)(2,1)S(1)}, u32[]{:S(2)}, u32[]{:S(2)}) collective-permute-start(bf16[2,8,48,256]{3,2,1,0:T(8,128)(2,1)S(1)} %pad_maximum_fusion.2), channel_id=1, source_target_pairs={{0,3},{8,28},{1,0},{9,29},{2,1},{10,30},{3,2},{11,31},{16,19},{24,... | collective-permute-start | bytes 1179656 | tf_op jit(solution)/shard_map/ppermute | solution.py:30
  32.9 9.1 %collective-permute-start.10 = (bf16[2,8,48,256]{3,2,1,0:T(8,128)(2,1)S(1)}, bf16[2,8,48,256]{3,2,1,0:T(8,128)(2,1)S(1)}, u32[]{:S(2)}, u32[]{:S(2)}) collective-permute-start(bf16[2,8,48,256]{3,2,1,0:T(8,128)(2,1)S(1)} %pad_maximum_fusion.1), channel_id=1, source_target_pairs={{0,1},{8,24},{1,2},{9,25},{2,3},{10,26},{3,0},{11,27},{16,17},{24,... | collective-permute-start | bytes 1179656 | tf_op jit(solution)/shard_map/ppermute | solution.py:30
  32.9 13.2 %collective-permute-start.12 = (bf16[2,8,48,256]{3,2,1,0:T(8,128)(2,1)S(1)}, bf16[2,8,48,256]{3,2,1,0:T(8,128)(2,1)S(1)}, u32[]{:S(2)}, u32[]{:S(2)}) collective-permute-start(bf16[2,8,48,256]{3,2,1,0:T(8,128)(2,1)S(1)} %pad_maximum_fusion.2), channel_id=1, source_target_pairs={{0,1},{8,24},{1,2},{9,25},{2,3},{10,26},{3,0},{11,27},{16,17},{24,... | collective-permute-start | bytes 1179656 | tf_op jit(solution)/shard_map/ppermute | solution.py:30
  34.3 11.8 %collective-permute-start.13 = (bf16[2,8,48,256]{3,2,1,0:T(8,128)(2,1)S(1)}, bf16[2,8,48,256]{3,2,1,0:T(8,128)(2,1)S(1)}, u32[]{:S(2)}, u32[]{:S(2)}) collective-permute-start(bf16[2,8,48,256]{3,2,1,0:T(8,128)(2,1)S(1)} %pad_maximum_fusion.1), channel_id=1, source_target_pairs={{0,3},{8,28},{1,0},{9,29},{2,1},{10,30},{3,2},{11,31},{16,19},{24,... | collective-permute-start | bytes 1179656 | tf_op jit(solution)/shard_map/ppermute | solution.py:30
  38.1 9.1 %collective-permute-start.15 = (bf16[2,8,48,256]{3,2,1,0:T(8,128)(2,1)S(1)}, bf16[2,8,48,256]{3,2,1,0:T(8,128)(2,1)S(1)}, u32[]{:S(2)}, u32[]{:S(2)}) collective-permute-start(bf16[2,8,48,256]{3,2,1,0:T(8,128)(2,1)S(1)} %collective-permute-done.11.refs_2_), channel_id=1, source_target_pairs={{0,3},{8,28},{1,0},{9,29},{2,1},{10,30},{3,2},{11,31},{16,19},{24,... | collective-permute-start | bytes 1179656 | tf_op jit(solution)/shard_map/ppermute | solution.py:30
  41.9 9.0 %collective-permute-start.14 = (bf16[2,8,48,256]{3,2,1,0:T(8,128)(2,1)S(1)}, bf16[2,8,48,256]{3,2,1,0:T(8,128)(2,1)S(1)}, u32[]{:S(2)}, u32[]{:S(2)}) collective-permute-start(bf16[2,8,48,256]{3,2,1,0:T(8,128)(2,1)S(1)} %collective-permute-done.10.refs_1_), channel_id=1, source_target_pairs={{0,1},{8,24},{1,2},{9,25},{2,3},{10,26},{3,0},{11,27},{16,17},{24,... | collective-permute-start | bytes 1179656 | tf_op jit(solution)/shard_map/ppermute | solution.py:30
  41.9 2.2 %copy-start.3 = (bf16[4,256,2048]{2,1,0:T(8,128)(2,1)S(1)}, bf16[4,256,2048]{2,1,0:T(8,128)(2,1)}, u32[]{:S(2)}) copy-start(bf16[4,256,2048]{2,1,0:T(8,128)(2,1)} %factors_ref.5) | copy-start | bytes 12582916
  47.2 4.7 %copy-start.6 = (f32[4,256]{1,0:T(4,128)S(1)}, f32[4,256]{1,0:T(4,128)}, u32[]{:S(2)}) copy-start(f32[4,256]{1,0:T(4,128)} %offsets_ref.3) | copy-start | bytes 12292
  51.7 5.9 %collective-permute-start.16 = (bf16[768,2048]{1,0:T(8,128)(2,1)S(1)}, bf16[768,2048]{1,0:T(8,128)(2,1)}, u32[]{:S(2)}, u32[]{:S(2)}) collective-permute-start(bf16[768,2048]{1,0:T(8,128)(2,1)S(1)} %lay.3.rows_ref.mine_ref), channel_id=1, source_target_pairs={{0,8},{8,0},{1,9},{9,1},{2,10},{10,2},{3,11},{11,3},{16,24},{24,16... | collective-permute-start | bytes 9437192 | tf_op jit(solution)/shard_map/ppermute | solution.py:30
  51.8 2.2 %copy-start.4 = (bf16[4,256,2048]{2,1,0:T(8,128)(2,1)S(1)}, bf16[4,256,2048]{2,1,0:T(8,128)(2,1)}, u32[]{:S(2)}) copy-start(bf16[4,256,2048]{2,1,0:T(8,128)(2,1)} %factors_ref.5) | copy-start | bytes 12582916
  57.5 21.7 %copy-start.7 = (f32[4]{0:T(128)S(1)}, f32[4]{0:T(128)}, u32[]{:S(2)}) copy-start(f32[4]{0:T(128)} %param.7) | copy-start | bytes 52
  63.0 1.7 %copy-start = (bf16[768,2048]{1,0:T(8,128)(2,1)}, bf16[768,2048]{1,0:T(8,128)(2,1)S(1)}, u32[]{:S(2)}) copy-start(bf16[768,2048]{1,0:T(8,128)(2,1)S(1)} %get-tuple-element.12.theirs_ref) | copy-start | bytes 9437188
  64.7 3.9 %collective-permute-start.17 = (f32[4,1536]{1,0:T(4,128)S(1)}, f32[4,1536]{1,0:T(4,128)S(1)}, u32[]{:S(2)}, u32[]{:S(2)}) collective-permute-start(f32[4,1536]{1,0:T(4,128)S(1)} %maximum_select_fusion), channel_id=1, source_target_pairs={{0,1},{8,9},{1,0},{9,8},{2,3},{10,11},{3,2},{11,10},{16,17},{24,25... | collective-permute-start | bytes 73736 | tf_op jit(solution)/shard_map/ppermute | solution.py:30
  68.6 5.1 %collective-permute-start.18 = (f32[4,1536]{1,0:T(4,128)S(1)}, f32[4,1536]{1,0:T(4,128)S(1)}, u32[]{:S(2)}, u32[]{:S(2)}) collective-permute-start(f32[4,1536]{1,0:T(4,128)S(1)} %add.89), channel_id=1, source_target_pairs={{0,3},{8,11},{1,2},{9,10},{2,1},{10,9},{3,0},{11,8},{16,19},{24,27... | collective-permute-start | bytes 73736 | tf_op jit(solution)/shard_map/ppermute | solution.py:30
  73.8 5.4 %collective-permute-start.19 = (f32[4,1536]{1,0:T(4,128)S(1)}, f32[4,1536]{1,0:T(4,128)S(1)}, u32[]{:S(2)}, u32[]{:S(2)}) collective-permute-start(f32[4,1536]{1,0:T(4,128)S(1)} %add.90), channel_id=1, source_target_pairs={{0,4},{8,12},{1,5},{9,13},{2,6},{10,14},{3,7},{11,15},{16,20},{24,... | collective-permute-start | bytes 73736 | tf_op jit(solution)/shard_map/ppermute | solution.py:30
  79.4 1.3 %collective-permute-start.20 = (f32[2,1536]{1,0:T(2,128)S(1)}, f32[2,1536]{1,0:T(2,128)S(1)}, u32[]{:S(2)}, u32[]{:S(2)}) collective-permute-start(f32[2,1536]{1,0:T(2,128)S(1)} %pad_maximum_fusion.3), channel_id=1, source_target_pairs={{0,8},{8,0},{1,9},{9,1},{2,10},{10,2},{3,11},{11,3},{16,24},{24,16... | collective-permute-start | bytes 36872 | tf_op jit(solution)/shard_map/ppermute | solution.py:30
  80.7 3.8 %collective-permute-start.21 = (f32[2,1536]{1,0:T(2,128)S(1)}, f32[2,1536]{1,0:T(2,128)S(1)}, u32[]{:S(2)}, u32[]{:S(2)}) collective-permute-start(f32[2,1536]{1,0:T(2,128)S(1)} %pad_maximum_fusion.4), channel_id=1, source_target_pairs={{0,16},{8,24},{1,17},{9,25},{2,18},{10,26},{3,19},{11,27},{16,0},{... | collective-permute-start | bytes 36872 | tf_op jit(solution)/shard_map/ppermute | solution.py:30
  81.1 1.9 %copy-start.1 = (bf16[768,2048]{1,0:T(8,128)(2,1)S(1)}, bf16[768,2048]{1,0:T(8,128)(2,1)}, u32[]{:S(2)}) copy-start(bf16[768,2048]{1,0:T(8,128)(2,1)} %copy-done) | copy-start | bytes 9437188
  83.0 16.4 %copy-start.2 = (bf16[768,2048]{1,0:T(8,128)(2,1)S(1)}, bf16[768,2048]{1,0:T(8,128)(2,1)}, u32[]{:S(2)}) copy-start(bf16[768,2048]{1,0:T(8,128)(2,1)} %copy-done) | copy-start | bytes 9437188
  84.6 3.8 %collective-permute-start.22 = (f32[2,1536]{1,0:T(2,128)S(1)}, f32[2,1536]{1,0:T(2,128)S(1)}, u32[]{:S(2)}, u32[]{:S(2)}) collective-permute-start(f32[2,1536]{1,0:T(2,128)S(1)} %pad_maximum_fusion.5), channel_id=1, source_target_pairs={{0,32},{8,40},{1,33},{9,41},{2,34},{10,42},{3,35},{11,43},{16,48},... | collective-permute-start | bytes 36872 | tf_op jit(solution)/shard_map/ppermute | solution.py:30
  88.4 5.0 %collective-permute-start.23 = (f32[2,1536]{1,0:T(2,128)S(1)}, f32[2,1536]{1,0:T(2,128)S(1)}, u32[]{:S(2)}, u32[]{:S(2)}) collective-permute-start(f32[2,1536]{1,0:T(2,128)S(1)} %pad_maximum_fusion.6), channel_id=1, source_target_pairs={{0,224},{8,232},{1,225},{9,233},{2,226},{10,234},{3,227},{11,235},... | collective-permute-start | bytes 36872 | tf_op jit(solution)/shard_map/ppermute | solution.py:30
  93.5 5.8 %collective-permute-start.24 = (f32[2,1536]{1,0:T(2,128)S(1)}, f32[2,1536]{1,0:T(2,128)S(1)}, u32[]{:S(2)}, u32[]{:S(2)}) collective-permute-start(f32[2,1536]{1,0:T(2,128)S(1)} %pad_maximum_fusion.7), channel_id=1, source_target_pairs={{0,96},{8,104},{1,97},{9,105},{2,98},{10,106},{3,99},{11,107},{16,... | collective-permute-start | bytes 36872 | tf_op jit(solution)/shard_map/ppermute | solution.py:30
  (1 other events, 0.7 us)

commit v3 on v2

v3 whole, which is shorter than its diff:
```python
import functools

import jax
import jax.numpy as jnp
from jax import lax
from jax.experimental import pallas as pl
from jax.experimental.pallas import tpu as pltpu
from jax.sharding import PartitionSpec as P

AXES = ("wide", "narrow")
NZ, NY, NX = 8, 4, 4


def linear(z, y, x, c):
    return ((z * 2 + y % 2) * 2 + c) * 8 + (y // 2) * 4 + x


def pairs(move):
    out = []
    for z in range(NZ):
        for y in range(NY):
            for x in range(NX):
                for c in range(2):
                    tz, ty, tx, tc = move(z, y, x, c)
                    out.append((linear(z, y, x, c), linear(tz % NZ, ty % NY, tx % NX, tc)))
    return out


def send(value, move):
    return lax.ppermute(value, AXES, pairs(move))


def z_step(d):
    return lambda z, y, x, c: (z + d, y, x, c)


def first_step(d):
    return lambda z, y, x, c: (z, y + d, x, c) if c == 0 else (z, y, x + d, c)


def second_step(d):
    return lambda z, y, x, c: (z, y, x + d, c) if c == 0 else (z, y + d, x, c)


def core_swap(z, y, x, c):
    return (z, y, x, 1 - c)


def place():
    w, n = lax.axis_index("wide"), lax.axis_index("narrow")
    return w // 4, (n // 4) * 2 + (w // 2) % 2, n % 4, w % 2


def column_kernel(spot, *refs):
    out_ref = refs[-1]
    for i, ref in enumerate(refs[:-1]):
        out_ref[(spot[4] + i) % NZ] = ref[...]


def make_column(spot, ring):
    return pl.pallas_call(
        column_kernel,
        out_shape=pltpu.VMEM((NZ,) + ring[0].shape, ring[0].dtype),
        in_specs=[SMEM] + [VMEM] * NZ,
        out_specs=VMEM,
        compiler_params=pltpu.CompilerParams(vmem_limit_bytes=2 * 2**20),
        name="column",
    )(spot, *ring)


def gather(spot, samples, factors, terms):
    back, ahead, back2, ahead2 = (send(samples, z_step(d)) for d in (1, -1, 2, -2))
    ahead3, back3, far = send(ahead2, z_step(-1)), send(back2, z_step(1)), send(ahead2, z_step(-2))
    column = make_column(spot, [samples, ahead, ahead2, ahead3, far, back3, back2, back])
    column, terms = lax.optimization_barrier((column, terms))
    before, after, across = (send(column, first_step(d)) for d in (1, -1, 2))
    low, high = jnp.stack([column, after]), jnp.stack([across, before])
    before_low = send(low, second_step(1))
    after_high = send(high, second_step(-1))
    before_high = send(high, second_step(1))
    after_low = send(low, second_step(-1))
    far_low = send(before_low, second_step(1))
    far_high = send(after_high, second_step(-1))
    near = [low, high, before_low, after_high, before_high, after_low]
    near_rows = lay(spot, NEAR, None, near)
    *held, mark = hold(*factors, near_rows)
    return lay(spot, FAR, near_rows, [far_low, far_high], [mark]), held, terms


NEAR = ((0, 0, 2), (0, 2, 2), (3, 0, 2), (1, 2, 2), (3, 2, 2), (1, 0, 2))
FAR = ((2, 0, 2), (2, 2, 2))
VMEM = pl.BlockSpec(memory_space=pltpu.VMEM)
ANY = pl.BlockSpec(memory_space=pl.ANY)
SMEM = pl.BlockSpec(memory_space=pltpu.SMEM)


def lay_kernel(places, has_rows, spot, *refs):
    parts = refs[has_rows : has_rows + len(places)]
    rows, sems = refs[-2:]
    here_y, here_x = spot[0], spot[1]
    core = spot[2]
    blocks = rows.reshape(NZ, 2, 48, rows.shape[1])
    copies = []
    for part, (second, first, many) in zip(parts, places, strict=True):
        for i in range(many):
            ay, ax = (here_y + first + i) % 4, (here_x + second) % 4
            by, bx = (here_y + second) % 4, (here_x + first + i) % 4
            at_y = jnp.where(core == 0, ay, by)
            at_x = jnp.where(core == 0, ax, bx)
            col = pl.multiple_of(((at_y // 2) * 4 + at_x) * 256, 256)
            copy = pltpu.make_async_copy(
                part.at[i], blocks.at[:, at_y % 2, :, pl.ds(col, 256)], sems.at[len(copies)]
            )
            copy.start()
            copies.append(copy)
    for copy in copies:
        copy.wait()


def lay(spot, places, rows, parts, after=()):
    has_rows = 0 if rows is None else 1
    return pl.pallas_call(
        functools.partial(lay_kernel, places, has_rows),
        out_shape=pltpu.VMEM((768, 2048), jnp.bfloat16),
        in_specs=[SMEM] + [VMEM] * has_rows + [ANY] * (len(parts) + len(after)),
        out_specs=VMEM,
        scratch_shapes=[pltpu.SemaphoreType.DMA((12,))],
        input_output_aliases={1: 0} if has_rows else {},
        compiler_params=pltpu.CompilerParams(vmem_limit_bytes=2 * 2**20),
        name="lay",
    )(spot, *([rows] if has_rows else []), *parts, *after)


def hold_kernel(first, second, _, first_out, second_out, mark, sems):
    copies = [
        pltpu.make_async_copy(first, first_out, sems.at[0]),
        pltpu.make_async_copy(second, second_out, sems.at[1]),
    ]
    for copy in copies:
        copy.start()
    mark[...] = jnp.zeros_like(mark)
    for copy in copies:
        copy.wait()


def hold(first, second, after):
    kept = pltpu.VMEM(first.shape, first.dtype)
    return pl.pallas_call(
        hold_kernel,
        out_shape=(kept, kept, jax.ShapeDtypeStruct((8, 128), jnp.float32)),
        in_specs=[ANY, ANY, ANY],
        out_specs=(VMEM, VMEM, VMEM),
        scratch_shapes=[pltpu.SemaphoreType.DMA((2,))],
        compiler_params=pltpu.CompilerParams(vmem_limit_bytes=2 * 2**20),
        name="hold",
    )(first, second, after)


def score_kernel(spot, terms_ref, their_terms_ref, factors_ref, their_factors_ref, rows_ref, partial_ref):
    comps, span, feats = factors_ref.shape
    own = pl.multiple_of(spot[3] * span, span)
    eye = lax.broadcasted_iota(jnp.int32, (span, span), 0) == lax.broadcasted_iota(
        jnp.int32, (span, span), 1
    )
    for group, (factors, terms) in enumerate(((factors_ref, terms_ref), (their_factors_ref, their_terms_ref))):
        offsets = terms[:, :span].T
        projected = lax.dot_general(
            factors[...].reshape(comps * span, feats),
            rows_ref[...],
            (((1,), (1,)), ((), ())),
            preferred_element_type=jnp.float32,
        )
        for k in range(comps):
            square = factors[k, :, pl.ds(own, span)].astype(jnp.float32)
            diag = jnp.sum(jnp.where(eye, square, 0.0), axis=1, keepdims=True)
            log_det = jnp.sum(jnp.log(diag), axis=0, keepdims=True)
            centered = projected[k * span : (k + 1) * span] - offsets[:, k : k + 1]
            quadratic = jnp.sum(centered * centered, axis=0, keepdims=True)
            at = group * comps + k
            partial_ref[at : at + 1, :] = log_det - 0.5 * quadratic


def score(spot, terms, their_terms, factors, their_factors, rows):
    comps, span, feats = factors.shape
    total = rows.shape[0]
    return pl.pallas_call(
        score_kernel,
        out_shape=jax.ShapeDtypeStruct((2 * comps, total), jnp.float32),
        in_specs=[SMEM, VMEM, VMEM, VMEM, VMEM, VMEM],
        out_specs=VMEM,
        compiler_params=pltpu.CompilerParams(vmem_limit_bytes=14 * 2**20),
        cost_estimate=pl.CostEstimate(
            flops=4 * total * comps * span * feats, bytes_accessed=8 * 2**20, transcendentals=0
        ),
        name="score",
    )(spot, terms, their_terms, factors, their_factors, rows)


def turn_kernel(spot, mine_ref, theirs_ref, _, out_ref, held, sem):
    span, half = out_ref.shape[0], mine_ref.shape[0]
    own = pl.multiple_of(spot[3] * span, span)
    copy = pltpu.make_async_copy(theirs_ref, held, sem)
    copy.start()
    out_ref[:, :half] = mine_ref[:, pl.ds(own, span)].T
    copy.wait()
    out_ref[:, half:] = held[:, pl.ds(own, span)].T


def turn(spot, mine, theirs, span, after):
    return pl.pallas_call(
        turn_kernel,
        out_shape=(
            pltpu.VMEM((span, 2 * mine.shape[0]), mine.dtype),
            pltpu.VMEM(theirs.shape, theirs.dtype),
        ),
        in_specs=[SMEM, VMEM, ANY, ANY],
        out_specs=(VMEM, VMEM),
        scratch_shapes=[pltpu.SemaphoreType.DMA],
        compiler_params=pltpu.CompilerParams(vmem_limit_bytes=4 * 2**20),
        cost_estimate=pl.CostEstimate(flops=0, bytes_accessed=8 * 2**20, transcendentals=0),
        name="turn",
    )(spot, mine, theirs, after)


def moment_kernel(
    spot, loglik_ref, their_loglik_ref, norms_ref, their_norms_ref, own_ref, mine_ref, theirs_ref,
    norm_ref, means_ref, cov_ref, all_means, stage, sems,
):
    comps, half = loglik_ref.shape
    span, total = own_ref.shape
    feats = mine_ref.shape[1]
    turned = pltpu.roll(jnp.broadcast_to(norms_ref[1:2], (8, half)), lax.rem(half - spot[5], half), 1)
    norm_ref[...] = turned[0:1, : norm_ref.shape[1]]
    resp = jnp.concatenate(
        [
            jnp.exp((loglik_ref[...] - norms_ref[0:1]) - norms_ref[1:2]),
            jnp.exp((their_loglik_ref[...] - their_norms_ref[0:1]) - their_norms_ref[1:2]),
        ],
        axis=1,
    )
    inverse = 1.0 / (jnp.sum(resp, axis=1, keepdims=True) + 1.0)
    high = resp.astype(jnp.bfloat16)
    low = (resp - high.astype(jnp.float32)).astype(jnp.bfloat16)
    zero = jnp.zeros((8, total), jnp.bfloat16)

    def product(left, cols):
        right = jnp.concatenate([mine_ref[:, cols], theirs_ref[:, cols]], axis=0)
        return jnp.dot(left, right, preferred_element_type=jnp.float32)

    sums = product(jnp.concatenate([high, low, zero], axis=0), pl.ds(0, feats))
    all_means[...] = (sums[:comps] + sums[comps : 2 * comps]) * inverse
    means_ref[...] = all_means[:, pl.ds(pl.multiple_of(spot[3] * span, span), span)]
    copies = []
    for k in range(comps):
        weighted = own_ref[...].astype(jnp.float32) * resp[k : k + 1]
        own_means = jnp.sum(weighted, axis=1, keepdims=True) * inverse[k : k + 1]
        left = weighted.astype(jnp.bfloat16)
        tile = feats if k + 1 < comps else feats // 4
        for at in range(0, feats, tile):
            cols = pl.ds(at, tile)
            gram = product(left, cols)
            stage[k, :, cols] = (
                gram * inverse[k : k + 1] - own_means * all_means[k : k + 1, cols]
            ).astype(jnp.bfloat16)
            copy = pltpu.make_async_copy(stage.at[k, :, cols], cov_ref.at[k, :, cols], sems.at[len(copies)])
            copy.start()
            copies.append(copy)
    for copy in copies:
        copy.wait()


def moments(spot, loglik, their_loglik, norms, their_norms, own, mine, theirs, rows_here):
    comps = loglik.shape[0]
    span, feats = own.shape[0], mine.shape[1]
    return pl.pallas_call(
        moment_kernel,
        out_shape=(
            jax.ShapeDtypeStruct((1, rows_here), jnp.float32),
            jax.ShapeDtypeStruct((comps, span), jnp.float32),
            jax.ShapeDtypeStruct((comps, span, feats), jnp.bfloat16),
        ),
        in_specs=[SMEM] + [VMEM] * 7,
        out_specs=(VMEM, VMEM, ANY),
        scratch_shapes=[
            pltpu.VMEM((comps, feats), jnp.float32),
            pltpu.VMEM((comps, span, feats), jnp.bfloat16),
            pltpu.SemaphoreType.DMA((comps + 3,)),
        ],
        compiler_params=pltpu.CompilerParams(vmem_limit_bytes=14 * 2**20),
        name="moments",
    )(spot, loglik, their_loglik, norms, their_norms, own, mine, theirs)


def x_even(z, y, x, c):
    return (z, y, x ^ 1, c)


def x_odd(z, y, x, c):
    return (z, y, 3 - x, c)


def y_far(z, y, x, c):
    return (z, y + 2, x, c)


def y_near(z, y, x, c):
    return (z, y ^ 1, x, c)


def z_even(z, y, x, c):
    return (z ^ 1, y, x, c)


def z_odd(z, y, x, c):
    return (z + 1 if z % 2 else z - 1, y, x, c)


Z_LAST = {1: 6, 6: 1, 2: 5, 5: 2, 3: 0, 0: 3, 4: 7, 7: 4}


def z_far(z, y, x, c):
    return (Z_LAST[z], y, x, c)


def shards(samples, inverse_factors, offsets, log_weights):
    z, y, x, c = place()
    rows_here = samples.shape[0]
    comps, span, _ = inverse_factors.shape
    first_row = (z * 2 + y % 2) * rows_here
    spot = jnp.stack([y, x, c, lax.axis_index("narrow"), z, first_row]).astype(jnp.int32)
    terms = jnp.concatenate([offsets, jnp.broadcast_to(log_weights[:, None], (comps, 128))], axis=1)
    their_factors = send(inverse_factors, core_swap)
    their_terms = send(terms, core_swap)
    mine, held, (terms, their_terms) = gather(spot, samples, (inverse_factors, their_factors), (terms, their_terms))
    theirs = send(mine, core_swap)
    loglik = score(spot, terms, their_terms, *held, mine)
    for move in (x_even, x_odd, y_far):
        loglik = loglik + send(loglik, move)
    loglik = loglik + jnp.concatenate([terms[:, span:], their_terms[:, span:]], axis=0)[:, :1]
    their_loglik = send(loglik[comps:], core_swap)
    peak = jnp.max(loglik, axis=0)
    total = jnp.sum(jnp.exp(loglik - peak[None, :]), axis=0)
    for move in (y_near, z_even, z_odd, z_far):
        pair = jnp.stack([peak, total])
        if move is z_far:
            own, theirs = turn(spot, mine, theirs, span, pair)
        got = send(pair, move)
        peak = jnp.maximum(pair[0], got[0])
        total = pair[1] * jnp.exp(pair[0] - peak) + got[1] * jnp.exp(got[0] - peak)
    norms = jnp.stack([peak, jnp.log(total)])
    their_norms = send(norms, core_swap)
    norm, means, covariance = moments(
        spot, loglik[:comps], their_loglik, norms, their_norms, own, mine, theirs, rows_here
    )
    return (norm.reshape(rows_here), means, covariance)


def solution(mesh):
    return jax.shard_map(
        shards,
        mesh=mesh,
        in_specs=(P("wide", "narrow"), P("wide", "narrow", None), P("wide", "narrow"), P("wide")),
        out_specs=(P("wide"), P("wide", "narrow"), P("wide", "narrow", None)),
        check_vma=False,
    )
```

time: 111 us -> 106 us (0.955)
  the two profiles are of different devices: /device:TPU:8 before, /device:TPU:1 now
where the time goes in v3:
time: 106 us
  starting transfers between devices  51.3 us (48%)
  waiting for transfers between devices  26.7 us (25%)
  Pallas kernels  23.8 us (22%)
  local copies, waits for them, and re-layouts  1.83 us (2%)
  between operations  1.09 us (1%)
    ppermute x28, starting transfers between devices, send(): return lax.ppermute(value, AXES, pairs(move))  51.3 us
    ppermute x28, waiting for transfers between devices, send(): return lax.ppermute(value, AXES, pairs(move))  26.7 us
    pallas_call x1, Pallas kernels, moments(): pl.pallas_call(moment_kernel, out_shape=(jax.ShapeDtypeStruct((1, rows_he...  10.4 us
    pallas_call x1, Pallas kernels, score(): pl.pallas_call(score_kernel, out_shape=jax.ShapeDtypeStruct((2 * comps, t...  7.48 us
    pallas_call x1, Pallas kernels, hold(): pl.pallas_call(hold_kernel, out_shape=(kept, kept, jax.ShapeDtypeStruct((...  2.49 us
  transfers between devices with their start and end apart: 28, of which 12 were waited for; matrix products, arithmetic and copies ran while one was open for 2% of the time, Pallas kernels for 12%

profile of v3, /device:TPU:1, one launch (start us, length us, event | category | flops | bytes accessed | tf_op | source)
XLA Modules:
  0.0 105.8 jit_solution(257792600135371045)
XLA Ops:
  0.6 3.3 %collective-permute-start.8 = (bf16[4,256,2048]{2,1,0:T(8,128)(2,1)}, bf16[4,256,2048]{2,1,0:T(8,128)(2,1)}, u32[]{:S(2)}, u32[]{:S(2)}) collective-permute-start(bf16[4,256,2048]{2,1,0:T(8,128)(2,1)} %first.1), channel_id=1, source_target_pairs={{0,8},{8,0},{1,9},{9,1},{2,10},{10,2},{3,11},{11,3},{16,24},{24,16... | collective-permute-start | bytes 12582920 | tf_op jit(solution)/shard_map/ppermute | solution.py:30
  4.0 4.3 %collective-permute-start.1 = (bf16[48,256]{1,0:T(8,128)(2,1)}, bf16[48,256]{1,0:T(8,128)(2,1)S(1)}, u32[]{:S(2)}, u32[]{:S(2)}) collective-permute-start(bf16[48,256]{1,0:T(8,128)(2,1)} %refs_0_.1), channel_id=1, source_target_pairs={{0,192},{8,200},{1,193},{9,201},{2,194},{10,202},{3,195},{11,203},... | collective-permute-start | bytes 73736 | tf_op jit(solution)/shard_map/ppermute | solution.py:30
  8.3 3.1 %collective-permute-start = (bf16[48,256]{1,0:T(8,128)(2,1)}, bf16[48,256]{1,0:T(8,128)(2,1)S(1)}, u32[]{:S(2)}, u32[]{:S(2)}) collective-permute-start(bf16[48,256]{1,0:T(8,128)(2,1)} %refs_0_.1), channel_id=1, source_target_pairs={{0,224},{8,232},{1,225},{9,233},{2,226},{10,234},{3,227},{11,235},... | collective-permute-start | bytes 73736 | tf_op jit(solution)/shard_map/ppermute | solution.py:30
  11.4 2.7 %collective-permute-start.2 = (bf16[48,256]{1,0:T(8,128)(2,1)S(1)}, bf16[48,256]{1,0:T(8,128)(2,1)S(1)}, u32[]{:S(2)}, u32[]{:S(2)}) collective-permute-start(bf16[48,256]{1,0:T(8,128)(2,1)S(1)} %collective-permute-done.1.refs_2_), channel_id=1, source_target_pairs={{0,224},{8,232},{1,225},{9,233},{2,226},{10,234},{3,227},{11,235},... | collective-permute-start | bytes 73736 | tf_op jit(solution)/shard_map/ppermute | solution.py:30
  14.1 1.3 %collective-permute-start.5 = (bf16[48,256]{1,0:T(8,128)(2,1)S(1)}, bf16[48,256]{1,0:T(8,128)(2,1)S(1)}, u32[]{:S(2)}, u32[]{:S(2)}) collective-permute-start(bf16[48,256]{1,0:T(8,128)(2,1)S(1)} %collective-permute-done.4.refs_6_), channel_id=1, source_target_pairs={{0,32},{8,40},{1,33},{9,41},{2,34},{10,42},{3,35},{11,43},{16,48},... | collective-permute-start | bytes 73736 | tf_op jit(solution)/shard_map/ppermute | solution.py:30
  16.8 1.8 %collective-permute-start.7 = (f32[4,384]{1,0:T(4,128)S(1)}, f32[4,384]{1,0:T(4,128)S(1)}, u32[]{:S(2)}, u32[]{:S(2)}) collective-permute-start(f32[4,384]{1,0:T(4,128)S(1)} %pad_maximum_fusion.2.terms_ref), channel_id=1, source_target_pairs={{0,8},{8,0},{1,9},{9,1},{2,10},{10,2},{3,11},{11,3},{16,24},{24,16... | collective-permute-start | bytes 18440 | tf_op jit(solution)/shard_map/ppermute | solution.py:30
  18.6 0.9 copy-done.1
  20.1 2.8 %collective-permute-start.10 = (bf16[8,48,256]{2,1,0:T(8,128)(2,1)S(1)}, bf16[8,48,256]{2,1,0:T(8,128)(2,1)S(1)}, u32[]{:S(2)}, u32[]{:S(2)}) collective-permute-start(bf16[8,48,256]{2,1,0:T(8,128)(2,1)S(1)} %column.1), channel_id=1, source_target_pairs={{0,4},{8,10},{1,5},{9,11},{2,6},{10,8},{3,7},{11,9},{16,20},{24,26... | collective-permute-start | bytes 589832 | tf_op jit(solution)/shard_map/ppermute | solution.py:30
  23.3 2.4 %collective-permute-start.9 = (bf16[8,48,256]{2,1,0:T(8,128)(2,1)S(1)}, bf16[8,48,256]{2,1,0:T(8,128)(2,1)S(1)}, u32[]{:S(2)}, u32[]{:S(2)}) collective-permute-start(bf16[8,48,256]{2,1,0:T(8,128)(2,1)S(1)} %column.1), channel_id=1, source_target_pairs={{0,20},{8,11},{1,21},{9,8},{2,22},{10,9},{3,23},{11,10},{16,0},{24... | collective-permute-start | bytes 589832 | tf_op jit(solution)/shard_map/ppermute | solution.py:30
  26.2 2.6 %collective-permute-done.11 = bf16[8,48,256]{2,1,0:T(8,128)(2,1)S(1)} collective-permute-done((bf16[8,48,256]{2,1,0:T(8,128)(2,1)S(1)}, bf16[8,48,256]{2,1,0:T(8,128)(2,1)S(1)}, u32[]{:S(2)}, u32[]{:S(2)}) %collective-permute-start.11) | collective-permute-done | bytes 196640 | tf_op jit(solution)/shard_map/ppermute | solution.py:30
  28.9 2.8 %collective-permute-start.13 = (bf16[2,8,48,256]{3,2,1,0:T(8,128)(2,1)S(1)}, bf16[2,8,48,256]{3,2,1,0:T(8,128)(2,1)S(1)}, u32[]{:S(2)}, u32[]{:S(2)}) collective-permute-start(bf16[2,8,48,256]{3,2,1,0:T(8,128)(2,1)S(1)} %pad_maximum_fusion.1.refs_1_), channel_id=1, source_target_pairs={{0,3},{8,28},{1,0},{9,29},{2,1},{10,30},{3,2},{11,31},{16,19},{24,... | collective-permute-start | bytes 1179656 | tf_op jit(solution)/shard_map/ppermute | solution.py:30
  32.0 2.7 %collective-permute-start.15 = (bf16[2,8,48,256]{3,2,1,0:T(8,128)(2,1)S(1)}, bf16[2,8,48,256]{3,2,1,0:T(8,128)(2,1)S(1)}, u32[]{:S(2)}, u32[]{:S(2)}) collective-permute-start(bf16[2,8,48,256]{3,2,1,0:T(8,128)(2,1)S(1)} %pad_maximum_fusion.refs_0_), channel_id=1, source_target_pairs={{0,3},{8,28},{1,0},{9,29},{2,1},{10,30},{3,2},{11,31},{16,19},{24,... | collective-permute-start | bytes 1179656 | tf_op jit(solution)/shard_map/ppermute | solution.py:30
  34.6 1.8 %collective-permute-done.13.refs_3_ = bf16[2,8,48,256]{3,2,1,0:T(8,128)(2,1)S(1)} collective-permute-done((bf16[2,8,48,256]{3,2,1,0:T(8,128)(2,1)S(1)}, bf16[2,8,48,256]{3,2,1,0:T(8,128)(2,1)S(1)}, u32[]{:S(2)}, u32[]{:S(2)}) %collective-permute-start.13) | collective-permute-done | bytes 393248 | tf_op jit(solution)/shard_map/ppermute | solution.py:30
  36.4 3.1 %collective-permute-start.17 = (bf16[2,8,48,256]{3,2,1,0:T(8,128)(2,1)S(1)}, bf16[2,8,48,256]{3,2,1,0:T(8,128)(2,1)S(1)}, u32[]{:S(2)}, u32[]{:S(2)}) collective-permute-start(bf16[2,8,48,256]{3,2,1,0:T(8,128)(2,1)S(1)} %collective-permute-done.13.refs_3_), channel_id=1, source_target_pairs={{0,3},{8,28},{1,0},{9,29},{2,1},{10,30},{3,2},{11,31},{16,19},{24,... | collective-permute-start | bytes 1179656 | tf_op jit(solution)/shard_map/ppermute | solution.py:30
  40.0 4.2 %collective-permute-done.14.refs_4_ = bf16[2,8,48,256]{3,2,1,0:T(8,128)(2,1)S(1)} collective-permute-done((bf16[2,8,48,256]{3,2,1,0:T(8,128)(2,1)S(1)}, bf16[2,8,48,256]{3,2,1,0:T(8,128)(2,1)S(1)}, u32[]{:S(2)}, u32[]{:S(2)}) %collective-permute-start.14) | collective-permute-done | bytes 393248 | tf_op jit(solution)/shard_map/ppermute | solution.py:30
  44.2 1.0 lay.2._.refs_0_
  45.2 2.5 %hold.1 = (bf16[4,256,2048]{2,1,0:T(8,128)(2,1)S(1)}, bf16[4,256,2048]{2,1,0:T(8,128)(2,1)S(1)}, f32[8,128]{1,0:T(8,128)S(1)}) custom-call(bf16[4,256,2048]{2,1,0:T(8,128)(2,1)S(1)} %copy-done, bf16[4,256,2048]{2,1,0:T(8,128)(2,1)} %collective-permute-done.8.second, bf16[768,2048]{1,0:T(8,128)(2,1)S(1)} %lay.2._.refs_0_), custom_call_target="tpu_custom_call" | custom-call | tf_op jit(solution)/shard_map/hold/pallas_call | solution.py:148
  48.9 5.1 %collective-permute-start.27 = (bf16[768,2048]{1,0:T(8,128)(2,1)S(1)}, bf16[768,2048]{1,0:T(8,128)(2,1)S(1)}, u32[]{:S(2)}, u32[]{:S(2)}) collective-permute-start(bf16[768,2048]{1,0:T(8,128)(2,1)S(1)} %lay.3.rows_ref.mine_ref), channel_id=1, source_target_pairs={{0,8},{8,0},{1,9},{9,1},{2,10},{10,2},{3,11},{11,3},{16,24},{24,16... | collective-permute-start | bytes 9437192 | tf_op jit(solution)/shard_map/ppermute | solution.py:30
  54.0 7.5 %score.1 = f32[8,768]{1,0:T(8,128)S(1)} custom-call(s32[6]{0:T(128)S(1)} %stack.72.spot, f32[4,384]{1,0:T(4,128)S(1)} %pad_maximum_fusion.2.terms_ref, f32[4,384]{1,0:T(4,128)S(1)} %collective-permute-done.7.their_terms_ref, bf16[4,256,2048]{2,1,0:T(8,128)(2,1)S(1)} %get-tuple-element.17.factors_ref, ...), custom_call_target="tpu_custom_call" | custom-call | flops 6442450944 | bytes 8388608 | tf_op jit(solution)/shard_map/score/pallas_call | solution.py:186
  61.6 2.6 %collective-permute-done.18 = f32[8,768]{1,0:T(8,128)S(1)} collective-permute-done((f32[8,768]{1,0:T(8,128)S(1)}, f32[8,768]{1,0:T(8,128)S(1)}, u32[]{:S(2)}, u32[]{:S(2)}) %collective-permute-start.18) | collective-permute-done | bytes 24608 | tf_op jit(solution)/shard_map/ppermute | solution.py:30
  64.3 3.9 %collective-permute-done.19 = f32[8,768]{1,0:T(8,128)S(1)} collective-permute-done((f32[8,768]{1,0:T(8,128)S(1)}, f32[8,768]{1,0:T(8,128)S(1)}, u32[]{:S(2)}, u32[]{:S(2)}) %collective-permute-start.19) | collective-permute-done | bytes 24608 | tf_op jit(solution)/shard_map/ppermute | solution.py:30
  68.2 1.3 %collective-permute-start.20 = (f32[8,768]{1,0:T(8,128)S(1)}, f32[8,768]{1,0:T(8,128)S(1)}, u32[]{:S(2)}, u32[]{:S(2)}) collective-permute-start(f32[8,768]{1,0:T(8,128)S(1)} %add.70), channel_id=1, source_target_pairs={{0,4},{8,12},{1,5},{9,13},{2,6},{10,14},{3,7},{11,15},{16,20},{24,... | collective-permute-start | bytes 73736 | tf_op jit(solution)/shard_map/ppermute | solution.py:30
  69.6 2.7 %collective-permute-done.20 = f32[8,768]{1,0:T(8,128)S(1)} collective-permute-done((f32[8,768]{1,0:T(8,128)S(1)}, f32[8,768]{1,0:T(8,128)S(1)}, u32[]{:S(2)}, u32[]{:S(2)}) %collective-permute-start.20) | collective-permute-done | bytes 24608 | tf_op jit(solution)/shard_map/ppermute | solution.py:30
  73.3 2.1 %collective-permute-done.22 = f32[2,768]{1,0:T(2,128)S(1)} collective-permute-done((f32[2,768]{1,0:T(2,128)S(1)}, f32[2,768]{1,0:T(2,128)S(1)}, u32[]{:S(2)}, u32[]{:S(2)}) %collective-permute-start.22) | collective-permute-done | bytes 6176 | tf_op jit(solution)/shard_map/ppermute | solution.py:30
  75.6 2.4 %collective-permute-done.23 = f32[2,768]{1,0:T(2,128)S(1)} collective-permute-done((f32[2,768]{1,0:T(2,128)S(1)}, f32[2,768]{1,0:T(2,128)S(1)}, u32[]{:S(2)}, u32[]{:S(2)}) %collective-permute-start.23) | collective-permute-done | bytes 6176 | tf_op jit(solution)/shard_map/ppermute | solution.py:30
  78.0 0.9 collective-permute-start.24
  78.9 2.9 %collective-permute-done.24 = f32[2,768]{1,0:T(2,128)S(1)} collective-permute-done((f32[2,768]{1,0:T(2,128)S(1)}, f32[2,768]{1,0:T(2,128)S(1)}, u32[]{:S(2)}, u32[]{:S(2)}) %collective-permute-start.24) | collective-permute-done | bytes 6176 | tf_op jit(solution)/shard_map/ppermute | solution.py:30
  81.8 1.2 %collective-permute-start.25 = (f32[2,768]{1,0:T(2,128)S(1)}, f32[2,768]{1,0:T(2,128)S(1)}, u32[]{:S(2)}, u32[]{:S(2)}) collective-permute-start(f32[2,768]{1,0:T(2,128)S(1)} %pad_maximum_fusion.6._), channel_id=1, source_target_pairs={{0,96},{8,104},{1,97},{9,105},{2,98},{10,106},{3,99},{11,107},{16,... | collective-permute-start | bytes 18440 | tf_op jit(solution)/shard_map/ppermute | solution.py:30
  83.1 6.9 %collective-permute-start.21 = (f32[4,768]{1,0:T(4,128)S(1)}, f32[4,768]{1,0:T(4,128)S(1)}, u32[]{:S(2)}, u32[]{:S(2)}) collective-permute-start(f32[4,768]{1,0:T(4,128)S(1)} %get-tuple-element.33), channel_id=1, source_target_pairs={{0,8},{8,0},{1,9},{9,1},{2,10},{10,2},{3,11},{11,3},{16,24},{24,16... | collective-permute-start | bytes 36872 | tf_op jit(solution)/shard_map/ppermute | solution.py:30
  90.0 4.1 %collective-permute-start.26 = (f32[2,768]{1,0:T(2,128)S(1)}, f32[2,768]{1,0:T(2,128)S(1)}, u32[]{:S(2)}, u32[]{:S(2)}) collective-permute-start(f32[2,768]{1,0:T(2,128)S(1)} %pad_maximum_fusion.7.norms_ref), channel_id=1, source_target_pairs={{0,8},{8,0},{1,9},{9,1},{2,10},{10,2},{3,11},{11,3},{16,24},{24,16... | collective-permute-start | bytes 18440 | tf_op jit(solution)/shard_map/ppermute | solution.py:30
  94.1 1.1 %turn.1 = (bf16[256,1536]{1,0:T(8,128)(2,1)S(1)}, bf16[768,2048]{1,0:T(8,128)(2,1)S(1)}) custom-call(s32[6]{0:T(128)S(1)} %stack.72.spot, bf16[768,2048]{1,0:T(8,128)(2,1)S(1)} %lay.3.rows_ref.mine_ref, bf16[768,2048]{1,0:T(8,128)(2,1)S(1)} %collective-permute-done.27.theirs_ref, f32[2,768]{1,0:T(2,128)S(1)} %pad_maximum_fusion.6._), custom_call_target="tpu_custom_call" | custom-call | bytes 8388608 | tf_op jit(solution)/shard_map/turn/pallas_call | solution.py:210
  95.2 10.4 %moments.1 = (f32[1,48]{1,0:T(1,128)}, f32[4,256]{1,0:T(4,128)}, bf16[4,256,2048]{2,1,0:T(8,128)(2,1)}) custom-call(s32[6]{0:T(128)S(1)} %stack.72.spot, f32[4,768]{1,0:T(4,128)S(1)} %get-tuple-element.34.loglik_ref, f32[4,768]{1,0:T(4,128)S(1)} %collective-permute-done.21.their_loglik_ref, f32[2,768]{1,0:T(2,128)S(1)} %pad_maximum_fusion.7.norms_ref, ...), custom_call_target="tpu_custom_call" | custom-call | tf_op jit(solution)/shard_map/moments/pallas_call | solution.py:275
  (60 shorter events, 6.3 us)
Async XLA Ops:
  0.6 44.6 %collective-permute-start.8 = (bf16[4,256,2048]{2,1,0:T(8,128)(2,1)}, bf16[4,256,2048]{2,1,0:T(8,128)(2,1)}, u32[]{:S(2)}, u32[]{:S(2)}) collective-permute-start(bf16[4,256,2048]{2,1,0:T(8,128)(2,1)} %first.1), channel_id=1, source_target_pairs={{0,8},{8,0},{1,9},{9,1},{2,10},{10,2},{3,11},{11,3},{16,24},{24,16... | collective-permute-start | bytes 12582920 | tf_op jit(solution)/shard_map/ppermute | solution.py:30
  4.0 7.4 %collective-permute-start.1 = (bf16[48,256]{1,0:T(8,128)(2,1)}, bf16[48,256]{1,0:T(8,128)(2,1)S(1)}, u32[]{:S(2)}, u32[]{:S(2)}) collective-permute-start(bf16[48,256]{1,0:T(8,128)(2,1)} %refs_0_.1), channel_id=1, source_target_pairs={{0,192},{8,200},{1,193},{9,201},{2,194},{10,202},{3,195},{11,203},... | collective-permute-start | bytes 73736 | tf_op jit(solution)/shard_map/ppermute | solution.py:30
  8.3 5.8 %collective-permute-start.4 = (bf16[48,256]{1,0:T(8,128)(2,1)}, bf16[48,256]{1,0:T(8,128)(2,1)S(1)}, u32[]{:S(2)}, u32[]{:S(2)}) collective-permute-start(bf16[48,256]{1,0:T(8,128)(2,1)} %refs_0_.1), channel_id=1, source_target_pairs={{0,64},{8,72},{1,65},{9,73},{2,66},{10,74},{3,67},{11,75},{16,80},... | collective-permute-start | bytes 73736 | tf_op jit(solution)/shard_map/ppermute | solution.py:30
  8.3 5.8 %collective-permute-start = (bf16[48,256]{1,0:T(8,128)(2,1)}, bf16[48,256]{1,0:T(8,128)(2,1)S(1)}, u32[]{:S(2)}, u32[]{:S(2)}) collective-permute-start(bf16[48,256]{1,0:T(8,128)(2,1)} %refs_0_.1), channel_id=1, source_target_pairs={{0,224},{8,232},{1,225},{9,233},{2,226},{10,234},{3,227},{11,235},... | collective-permute-start | bytes 73736 | tf_op jit(solution)/shard_map/ppermute | solution.py:30
  11.4 5.4 %collective-permute-start.6 = (bf16[48,256]{1,0:T(8,128)(2,1)}, bf16[48,256]{1,0:T(8,128)(2,1)S(1)}, u32[]{:S(2)}, u32[]{:S(2)}) collective-permute-start(bf16[48,256]{1,0:T(8,128)(2,1)} %refs_0_.1), channel_id=1, source_target_pairs={{0,32},{8,40},{1,33},{9,41},{2,34},{10,42},{3,35},{11,43},{16,48},... | collective-permute-start | bytes 73736 | tf_op jit(solution)/shard_map/ppermute | solution.py:30
  11.4 7.2 %collective-permute-start.2 = (bf16[48,256]{1,0:T(8,128)(2,1)S(1)}, bf16[48,256]{1,0:T(8,128)(2,1)S(1)}, u32[]{:S(2)}, u32[]{:S(2)}) collective-permute-start(bf16[48,256]{1,0:T(8,128)(2,1)S(1)} %collective-permute-done.1.refs_2_), channel_id=1, source_target_pairs={{0,224},{8,232},{1,225},{9,233},{2,226},{10,234},{3,227},{11,235},... | collective-permute-start | bytes 73736 | tf_op jit(solution)/shard_map/ppermute | solution.py:30
  14.1 4.5 %collective-permute-start.3 = (bf16[48,256]{1,0:T(8,128)(2,1)S(1)}, bf16[48,256]{1,0:T(8,128)(2,1)S(1)}, u32[]{:S(2)}, u32[]{:S(2)}) collective-permute-start(bf16[48,256]{1,0:T(8,128)(2,1)S(1)} %collective-permute-done.1.refs_2_), channel_id=1, source_target_pairs={{0,192},{8,200},{1,193},{9,201},{2,194},{10,202},{3,195},{11,203},... | collective-permute-start | bytes 73736 | tf_op jit(solution)/shard_map/ppermute | solution.py:30
  14.1 4.5 %collective-permute-start.5 = (bf16[48,256]{1,0:T(8,128)(2,1)S(1)}, bf16[48,256]{1,0:T(8,128)(2,1)S(1)}, u32[]{:S(2)}, u32[]{:S(2)}) collective-permute-start(bf16[48,256]{1,0:T(8,128)(2,1)S(1)} %collective-permute-done.4.refs_6_), channel_id=1, source_target_pairs={{0,32},{8,40},{1,33},{9,41},{2,34},{10,42},{3,35},{11,43},{16,48},... | collective-permute-start | bytes 73736 | tf_op jit(solution)/shard_map/ppermute | solution.py:30
  16.8 3.3 %collective-permute-start.7 = (f32[4,384]{1,0:T(4,128)S(1)}, f32[4,384]{1,0:T(4,128)S(1)}, u32[]{:S(2)}, u32[]{:S(2)}) collective-permute-start(f32[4,384]{1,0:T(4,128)S(1)} %pad_maximum_fusion.2.terms_ref), channel_id=1, source_target_pairs={{0,8},{8,0},{1,9},{9,1},{2,10},{10,2},{3,11},{11,3},{16,24},{24,16... | collective-permute-start | bytes 18440 | tf_op jit(solution)/shard_map/ppermute | solution.py:30
  18.6 26.6 %copy-start = (bf16[4,256,2048]{2,1,0:T(8,128)(2,1)S(1)}, bf16[4,256,2048]{2,1,0:T(8,128)(2,1)}, u32[]{:S(2)}) copy-start(bf16[4,256,2048]{2,1,0:T(8,128)(2,1)} %first.1) | copy-start | bytes 12582916
  18.6 0.9 copy-start.1
  20.1 6.1 %collective-permute-start.10 = (bf16[8,48,256]{2,1,0:T(8,128)(2,1)S(1)}, bf16[8,48,256]{2,1,0:T(8,128)(2,1)S(1)}, u32[]{:S(2)}, u32[]{:S(2)}) collective-permute-start(bf16[8,48,256]{2,1,0:T(8,128)(2,1)S(1)} %column.1), channel_id=1, source_target_pairs={{0,4},{8,10},{1,5},{9,11},{2,6},{10,8},{3,7},{11,9},{16,20},{24,26... | collective-permute-start | bytes 589832 | tf_op jit(solution)/shard_map/ppermute | solution.py:30
  22.9 5.9 %collective-permute-start.11 = (bf16[8,48,256]{2,1,0:T(8,128)(2,1)S(1)}, bf16[8,48,256]{2,1,0:T(8,128)(2,1)S(1)}, u32[]{:S(2)}, u32[]{:S(2)}) collective-permute-start(bf16[8,48,256]{2,1,0:T(8,128)(2,1)S(1)} %column.1), channel_id=1, source_target_pairs={{0,16},{8,9},{1,17},{9,10},{2,18},{10,11},{3,19},{11,8},{16,4},{24... | collective-permute-start | bytes 589832 | tf_op jit(solution)/shard_map/ppermute | solution.py:30
  23.3 8.5 %collective-permute-start.9 = (bf16[8,48,256]{2,1,0:T(8,128)(2,1)S(1)}, bf16[8,48,256]{2,1,0:T(8,128)(2,1)S(1)}, u32[]{:S(2)}, u32[]{:S(2)}) collective-permute-start(bf16[8,48,256]{2,1,0:T(8,128)(2,1)S(1)} %column.1), channel_id=1, source_target_pairs={{0,20},{8,11},{1,21},{9,8},{2,22},{10,9},{3,23},{11,10},{16,0},{24... | collective-permute-start | bytes 589832 | tf_op jit(solution)/shard_map/ppermute | solution.py:30
  28.9 7.5 %collective-permute-start.13 = (bf16[2,8,48,256]{3,2,1,0:T(8,128)(2,1)S(1)}, bf16[2,8,48,256]{3,2,1,0:T(8,128)(2,1)S(1)}, u32[]{:S(2)}, u32[]{:S(2)}) collective-permute-start(bf16[2,8,48,256]{3,2,1,0:T(8,128)(2,1)S(1)} %pad_maximum_fusion.1.refs_1_), channel_id=1, source_target_pairs={{0,3},{8,28},{1,0},{9,29},{2,1},{10,30},{3,2},{11,31},{16,19},{24,... | collective-permute-start | bytes 1179656 | tf_op jit(solution)/shard_map/ppermute | solution.py:30
  31.8 8.2 %collective-permute-start.12 = (bf16[2,8,48,256]{3,2,1,0:T(8,128)(2,1)S(1)}, bf16[2,8,48,256]{3,2,1,0:T(8,128)(2,1)S(1)}, u32[]{:S(2)}, u32[]{:S(2)}) collective-permute-start(bf16[2,8,48,256]{3,2,1,0:T(8,128)(2,1)S(1)} %pad_maximum_fusion.refs_0_), channel_id=1, source_target_pairs={{0,1},{8,24},{1,2},{9,25},{2,3},{10,26},{3,0},{11,27},{16,17},{24,... | collective-permute-start | bytes 1179656 | tf_op jit(solution)/shard_map/ppermute | solution.py:30
  31.9 12.3 %collective-permute-start.14 = (bf16[2,8,48,256]{3,2,1,0:T(8,128)(2,1)S(1)}, bf16[2,8,48,256]{3,2,1,0:T(8,128)(2,1)S(1)}, u32[]{:S(2)}, u32[]{:S(2)}) collective-permute-start(bf16[2,8,48,256]{3,2,1,0:T(8,128)(2,1)S(1)} %pad_maximum_fusion.1.refs_1_), channel_id=1, source_target_pairs={{0,1},{8,24},{1,2},{9,25},{2,3},{10,26},{3,0},{11,27},{16,17},{24,... | collective-permute-start | bytes 1179656 | tf_op jit(solution)/shard_map/ppermute | solution.py:30
  32.0 12.2 %collective-permute-start.15 = (bf16[2,8,48,256]{3,2,1,0:T(8,128)(2,1)S(1)}, bf16[2,8,48,256]{3,2,1,0:T(8,128)(2,1)S(1)}, u32[]{:S(2)}, u32[]{:S(2)}) collective-permute-start(bf16[2,8,48,256]{3,2,1,0:T(8,128)(2,1)S(1)} %pad_maximum_fusion.refs_0_), channel_id=1, source_target_pairs={{0,3},{8,28},{1,0},{9,29},{2,1},{10,30},{3,2},{11,31},{16,19},{24,... | collective-permute-start | bytes 1179656 | tf_op jit(solution)/shard_map/ppermute | solution.py:30
  36.4 11.3 %collective-permute-start.17 = (bf16[2,8,48,256]{3,2,1,0:T(8,128)(2,1)S(1)}, bf16[2,8,48,256]{3,2,1,0:T(8,128)(2,1)S(1)}, u32[]{:S(2)}, u32[]{:S(2)}) collective-permute-start(bf16[2,8,48,256]{3,2,1,0:T(8,128)(2,1)S(1)} %collective-permute-done.13.refs_3_), channel_id=1, source_target_pairs={{0,3},{8,28},{1,0},{9,29},{2,1},{10,30},{3,2},{11,31},{16,19},{24,... | collective-permute-start | bytes 1179656 | tf_op jit(solution)/shard_map/ppermute | solution.py:30
  40.0 8.1 %collective-permute-start.16 = (bf16[2,8,48,256]{3,2,1,0:T(8,128)(2,1)S(1)}, bf16[2,8,48,256]{3,2,1,0:T(8,128)(2,1)S(1)}, u32[]{:S(2)}, u32[]{:S(2)}) collective-permute-start(bf16[2,8,48,256]{3,2,1,0:T(8,128)(2,1)S(1)} %collective-permute-done.12.refs_2_), channel_id=1, source_target_pairs={{0,1},{8,24},{1,2},{9,25},{2,3},{10,26},{3,0},{11,27},{16,17},{24,... | collective-permute-start | bytes 1179656 | tf_op jit(solution)/shard_map/ppermute | solution.py:30
  48.9 45.2 %collective-permute-start.27 = (bf16[768,2048]{1,0:T(8,128)(2,1)S(1)}, bf16[768,2048]{1,0:T(8,128)(2,1)S(1)}, u32[]{:S(2)}, u32[]{:S(2)}) collective-permute-start(bf16[768,2048]{1,0:T(8,128)(2,1)S(1)} %lay.3.rows_ref.mine_ref), channel_id=1, source_target_pairs={{0,8},{8,0},{1,9},{9,1},{2,10},{10,2},{3,11},{11,3},{16,24},{24,16... | collective-permute-start | bytes 9437192 | tf_op jit(solution)/shard_map/ppermute | solution.py:30
  61.5 2.8 %collective-permute-start.18 = (f32[8,768]{1,0:T(8,128)S(1)}, f32[8,768]{1,0:T(8,128)S(1)}, u32[]{:S(2)}, u32[]{:S(2)}) collective-permute-start(f32[8,768]{1,0:T(8,128)S(1)} %score.1), channel_id=1, source_target_pairs={{0,1},{8,9},{1,0},{9,8},{2,3},{10,11},{3,2},{11,10},{16,17},{24,25... | collective-permute-start | bytes 73736 | tf_op jit(solution)/shard_map/ppermute | solution.py:30
  64.3 3.9 %collective-permute-start.19 = (f32[8,768]{1,0:T(8,128)S(1)}, f32[8,768]{1,0:T(8,128)S(1)}, u32[]{:S(2)}, u32[]{:S(2)}) collective-permute-start(f32[8,768]{1,0:T(8,128)S(1)} %add.69), channel_id=1, source_target_pairs={{0,3},{8,11},{1,2},{9,10},{2,1},{10,9},{3,0},{11,8},{16,19},{24,27... | collective-permute-start | bytes 73736 | tf_op jit(solution)/shard_map/ppermute | solution.py:30
  68.2 4.2 %collective-permute-start.20 = (f32[8,768]{1,0:T(8,128)S(1)}, f32[8,768]{1,0:T(8,128)S(1)}, u32[]{:S(2)}, u32[]{:S(2)}) collective-permute-start(f32[8,768]{1,0:T(8,128)S(1)} %add.70), channel_id=1, source_target_pairs={{0,4},{8,12},{1,5},{9,13},{2,6},{10,14},{3,7},{11,15},{16,20},{24,... | collective-permute-start | bytes 73736 | tf_op jit(solution)/shard_map/ppermute | solution.py:30
  72.5 2.9 %collective-permute-start.22 = (f32[2,768]{1,0:T(2,128)S(1)}, f32[2,768]{1,0:T(2,128)S(1)}, u32[]{:S(2)}, u32[]{:S(2)}) collective-permute-start(f32[2,768]{1,0:T(2,128)S(1)} %pad_maximum_fusion.3), channel_id=1, source_target_pairs={{0,16},{8,24},{1,17},{9,25},{2,18},{10,26},{3,19},{11,27},{16,0},{... | collective-permute-start | bytes 18440 | tf_op jit(solution)/shard_map/ppermute | solution.py:30
  75.4 2.6 %collective-permute-start.23 = (f32[2,768]{1,0:T(2,128)S(1)}, f32[2,768]{1,0:T(2,128)S(1)}, u32[]{:S(2)}, u32[]{:S(2)}) collective-permute-start(f32[2,768]{1,0:T(2,128)S(1)} %pad_maximum_fusion.4), channel_id=1, source_target_pairs={{0,32},{8,40},{1,33},{9,41},{2,34},{10,42},{3,35},{11,43},{16,48},... | collective-permute-start | bytes 18440 | tf_op jit(solution)/shard_map/ppermute | solution.py:30
  78.0 3.8 %collective-permute-start.24 = (f32[2,768]{1,0:T(2,128)S(1)}, f32[2,768]{1,0:T(2,128)S(1)}, u32[]{:S(2)}, u32[]{:S(2)}) collective-permute-start(f32[2,768]{1,0:T(2,128)S(1)} %pad_maximum_fusion.5), channel_id=1, source_target_pairs={{0,224},{8,232},{1,225},{9,233},{2,226},{10,234},{3,227},{11,235},... | collective-permute-start | bytes 18440 | tf_op jit(solution)/shard_map/ppermute | solution.py:30
  81.8 8.1 %collective-permute-start.25 = (f32[2,768]{1,0:T(2,128)S(1)}, f32[2,768]{1,0:T(2,128)S(1)}, u32[]{:S(2)}, u32[]{:S(2)}) collective-permute-start(f32[2,768]{1,0:T(2,128)S(1)} %pad_maximum_fusion.6._), channel_id=1, source_target_pairs={{0,96},{8,104},{1,97},{9,105},{2,98},{10,106},{3,99},{11,107},{16,... | collective-permute-start | bytes 18440 | tf_op jit(solution)/shard_map/ppermute | solution.py:30
  83.1 12.2 %collective-permute-start.21 = (f32[4,768]{1,0:T(4,128)S(1)}, f32[4,768]{1,0:T(4,128)S(1)}, u32[]{:S(2)}, u32[]{:S(2)}) collective-permute-start(f32[4,768]{1,0:T(4,128)S(1)} %get-tuple-element.33), channel_id=1, source_target_pairs={{0,8},{8,0},{1,9},{9,1},{2,10},{10,2},{3,11},{11,3},{16,24},{24,16... | collective-permute-start | bytes 36872 | tf_op jit(solution)/shard_map/ppermute | solution.py:30
  90.0 5.2 %collective-permute-start.26 = (f32[2,768]{1,0:T(2,128)S(1)}, f32[2,768]{1,0:T(2,128)S(1)}, u32[]{:S(2)}, u32[]{:S(2)}) collective-permute-start(f32[2,768]{1,0:T(2,128)S(1)} %pad_maximum_fusion.7.norms_ref), channel_id=1, source_target_pairs={{0,8},{8,0},{1,9},{9,1},{2,10},{10,2},{3,11},{11,3},{16,24},{24,16... | collective-permute-start | bytes 18440 | tf_op jit(solution)/shard_map/ppermute | solution.py:30

commit v4 on v3

--- a/solution.py
+++ b/solution.py
@@ -83,8 +83,8 @@
     far_high = send(after_high, second_step(-1))
     near = [low, high, before_low, after_high, before_high, after_low]
     near_rows = lay(spot, NEAR, None, near)
-    *held, mark = hold(*factors, near_rows)
-    return lay(spot, FAR, near_rows, [far_low, far_high], [mark]), held, terms
+    *held, log_det = hold(spot, *factors, near_rows)
+    return lay(spot, FAR, near_rows, [far_low, far_high], [log_det]), [log_det, *held], terms
 
 
 NEAR = ((0, 0, 2), (0, 2, 2), (3, 0, 2), (1, 2, 2), (3, 2, 2), (1, 0, 2))
@@ -131,37 +131,44 @@
     )(spot, *([rows] if has_rows else []), *parts, *after)
 
 
-def hold_kernel(first, second, _, first_out, second_out, mark, sems):
+def hold_kernel(spot, first, second, _, first_out, second_out, log_det_ref, sems):
     copies = [
         pltpu.make_async_copy(first, first_out, sems.at[0]),
         pltpu.make_async_copy(second, second_out, sems.at[1]),
     ]
     for copy in copies:
         copy.start()
-    mark[...] = jnp.zeros_like(mark)
+    comps, span, _ = first_out.shape
+    own = pl.multiple_of(spot[3] * span, span)
+    eye = lax.broadcasted_iota(jnp.int32, (span, span), 0) == lax.broadcasted_iota(
+        jnp.int32, (span, span), 1
+    )
     for copy in copies:
         copy.wait()
-
-
-def hold(first, second, after):
+    for group, factors in enumerate((first_out, second_out)):
+        for k in range(comps):
+            square = factors[k, :, pl.ds(own, span)].astype(jnp.float32)
+            diag = jnp.sum(jnp.where(eye, square, 0.0), axis=1, keepdims=True)
+            total = jnp.sum(jnp.log(diag), axis=0, keepdims=True)
+            at = group * comps + k
+            log_det_ref[at : at + 1, :] = jnp.broadcast_to(total, (1, log_det_ref.shape[1]))
+
+
+def hold(spot, first, second, after):
     kept = pltpu.VMEM(first.shape, first.dtype)
     return pl.pallas_call(
         hold_kernel,
-        out_shape=(kept, kept, jax.ShapeDtypeStruct((8, 128), jnp.float32)),
-        in_specs=[ANY, ANY, ANY],
+        out_shape=(kept, kept, jax.ShapeDtypeStruct((2 * first.shape[0], 128), jnp.float32)),
+        in_specs=[SMEM, ANY, ANY, ANY],
         out_specs=(VMEM, VMEM, VMEM),
         scratch_shapes=[pltpu.SemaphoreType.DMA((2,))],
         compiler_params=pltpu.CompilerParams(vmem_limit_bytes=2 * 2**20),
         name="hold",
-    )(first, second, after)
-
-
-def score_kernel(spot, terms_ref, their_terms_ref, factors_ref, their_factors_ref, rows_ref, partial_ref):
+    )(spot, first, second, after)
+
+
+def score_kernel(terms_ref, their_terms_ref, log_det_ref, factors_ref, their_factors_ref, rows_ref, partial_ref):
     comps, span, feats = factors_ref.shape
-    own = pl.multiple_of(spot[3] * span, span)
-    eye = lax.broadcasted_iota(jnp.int32, (span, span), 0) == lax.broadcasted_iota(
-        jnp.int32, (span, span), 1
-    )
     for group, (factors, terms) in enumerate(((factors_ref, terms_ref), (their_factors_ref, their_terms_ref))):
         offsets = terms[:, :span].T
         projected = lax.dot_general(
@@ -171,29 +178,26 @@
             preferred_element_type=jnp.float32,
         )
         for k in range(comps):
-            square = factors[k, :, pl.ds(own, span)].astype(jnp.float32)
-            diag = jnp.sum(jnp.where(eye, square, 0.0), axis=1, keepdims=True)
-            log_det = jnp.sum(jnp.log(diag), axis=0, keepdims=True)
             centered = projected[k * span : (k + 1) * span] - offsets[:, k : k + 1]
             quadratic = jnp.sum(centered * centered, axis=0, keepdims=True)
             at = group * comps + k
-            partial_ref[at : at + 1, :] = log_det - 0.5 * quadratic
-
-
-def score(spot, terms, their_terms, factors, their_factors, rows):
+            partial_ref[at : at + 1, :] = log_det_ref[at : at + 1, 0:1] - 0.5 * quadratic
+
+
+def score(terms, their_terms, log_det, factors, their_factors, rows):
     comps, span, feats = factors.shape
     total = rows.shape[0]
     return pl.pallas_call(
         score_kernel,
         out_shape=jax.ShapeDtypeStruct((2 * comps, total), jnp.float32),
-        in_specs=[SMEM, VMEM, VMEM, VMEM, VMEM, VMEM],
+        in_specs=[VMEM] * 6,
         out_specs=VMEM,
         compiler_params=pltpu.CompilerParams(vmem_limit_bytes=14 * 2**20),
         cost_estimate=pl.CostEstimate(
             flops=4 * total * comps * span * feats, bytes_accessed=8 * 2**20, transcendentals=0
         ),
         name="score",
-    )(spot, terms, their_terms, factors, their_factors, rows)
+    )(terms, their_terms, log_det, factors, their_factors, rows)
 
 
 def turn_kernel(spot, mine_ref, theirs_ref, _, out_ref, held, sem):
@@ -333,7 +337,7 @@
     their_terms = send(terms, core_swap)
     mine, held, (terms, their_terms) = gather(spot, samples, (inverse_factors, their_factors), (terms, their_terms))
     theirs = send(mine, core_swap)
-    loglik = score(spot, terms, their_terms, *held, mine)
+    loglik = score(terms, their_terms, *held, mine)
     for move in (x_even, x_odd, y_far):
         loglik = loglik + send(loglik, move)
     loglik = loglik + jnp.concatenate([terms[:, span:], their_terms[:, span:]], axis=0)[:, :1]

time: 106 us -> 105 us (level)
  transfers between devices with their start and end apart: 28 -> 28, of which waited for: 12 -> 11; matrix products, arithmetic and copies ran while one was open for 2% -> 2% of each run, Pallas kernels for 12% -> 12%
where the time goes in v4:
time: 105 us
  starting transfers between devices  50.7 us (48%)
  waiting for transfers between devices  26.4 us (25%)
  Pallas kernels  23.9 us (23%)
  local copies, waits for them, and re-layouts  1.83 us (2%)
  between operations  1.1 us (1%)
    ppermute x28, starting transfers between devices, send(): return lax.ppermute(value, AXES, pairs(move))  50.7 us
    ppermute x28, waiting for transfers between devices, send(): return lax.ppermute(value, AXES, pairs(move))  26.4 us
    pallas_call x1, Pallas kernels, moments(): pl.pallas_call(moment_kernel, out_shape=(jax.ShapeDtypeStruct((1, rows_he...  10.4 us
    pallas_call x1, Pallas kernels, score(): pl.pallas_call(score_kernel, out_shape=jax.ShapeDtypeStruct((2 * comps, t...  6.73 us
    pallas_call x1, Pallas kernels, hold(): pl.pallas_call(hold_kernel, out_shape=(kept, kept, jax.ShapeDtypeStruct((...  3.39 us
  transfers between devices with their start and end apart: 28, of which 11 were waited for; matrix products, arithmetic and copies ran while one was open for 2% of the time, Pallas kernels for 12%

profile of v4, /device:TPU:1, one launch (start us, length us, event | category | flops | bytes accessed | tf_op | source)
XLA Modules:
  0.0 105.0 jit_solution(404385527391331284)
XLA Ops:
  0.6 3.3 %collective-permute-start.8 = (bf16[4,256,2048]{2,1,0:T(8,128)(2,1)}, bf16[4,256,2048]{2,1,0:T(8,128)(2,1)}, u32[]{:S(2)}, u32[]{:S(2)}) collective-permute-start(bf16[4,256,2048]{2,1,0:T(8,128)(2,1)} %first.1), channel_id=1, source_target_pairs={{0,8},{8,0},{1,9},{9,1},{2,10},{10,2},{3,11},{11,3},{16,24},{24,16... | collective-permute-start | bytes 12582920 | tf_op jit(solution)/shard_map/ppermute | solution.py:30
  4.0 4.3 %collective-permute-start.1 = (bf16[48,256]{1,0:T(8,128)(2,1)}, bf16[48,256]{1,0:T(8,128)(2,1)S(1)}, u32[]{:S(2)}, u32[]{:S(2)}) collective-permute-start(bf16[48,256]{1,0:T(8,128)(2,1)} %refs_0_.1), channel_id=1, source_target_pairs={{0,192},{8,200},{1,193},{9,201},{2,194},{10,202},{3,195},{11,203},... | collective-permute-start | bytes 73736 | tf_op jit(solution)/shard_map/ppermute | solution.py:30
  8.3 3.1 %collective-permute-start = (bf16[48,256]{1,0:T(8,128)(2,1)}, bf16[48,256]{1,0:T(8,128)(2,1)S(1)}, u32[]{:S(2)}, u32[]{:S(2)}) collective-permute-start(bf16[48,256]{1,0:T(8,128)(2,1)} %refs_0_.1), channel_id=1, source_target_pairs={{0,224},{8,232},{1,225},{9,233},{2,226},{10,234},{3,227},{11,235},... | collective-permute-start | bytes 73736 | tf_op jit(solution)/shard_map/ppermute | solution.py:30
  11.4 2.7 %collective-permute-start.2 = (bf16[48,256]{1,0:T(8,128)(2,1)S(1)}, bf16[48,256]{1,0:T(8,128)(2,1)S(1)}, u32[]{:S(2)}, u32[]{:S(2)}) collective-permute-start(bf16[48,256]{1,0:T(8,128)(2,1)S(1)} %collective-permute-done.1.refs_2_), channel_id=1, source_target_pairs={{0,224},{8,232},{1,225},{9,233},{2,226},{10,234},{3,227},{11,235},... | collective-permute-start | bytes 73736 | tf_op jit(solution)/shard_map/ppermute | solution.py:30
  14.1 1.3 %collective-permute-start.5 = (bf16[48,256]{1,0:T(8,128)(2,1)S(1)}, bf16[48,256]{1,0:T(8,128)(2,1)S(1)}, u32[]{:S(2)}, u32[]{:S(2)}) collective-permute-start(bf16[48,256]{1,0:T(8,128)(2,1)S(1)} %collective-permute-done.4.refs_6_), channel_id=1, source_target_pairs={{0,32},{8,40},{1,33},{9,41},{2,34},{10,42},{3,35},{11,43},{16,48},... | collective-permute-start | bytes 73736 | tf_op jit(solution)/shard_map/ppermute | solution.py:30
  16.8 1.8 %collective-permute-start.7 = (f32[4,384]{1,0:T(4,128)S(1)}, f32[4,384]{1,0:T(4,128)S(1)}, u32[]{:S(2)}, u32[]{:S(2)}) collective-permute-start(f32[4,384]{1,0:T(4,128)S(1)} %pad_maximum_fusion.2.terms_ref), channel_id=1, source_target_pairs={{0,8},{8,0},{1,9},{9,1},{2,10},{10,2},{3,11},{11,3},{16,24},{24,16... | collective-permute-start | bytes 18440 | tf_op jit(solution)/shard_map/ppermute | solution.py:30
  18.6 0.9 copy-done.1
  20.1 2.8 %collective-permute-start.10 = (bf16[8,48,256]{2,1,0:T(8,128)(2,1)S(1)}, bf16[8,48,256]{2,1,0:T(8,128)(2,1)S(1)}, u32[]{:S(2)}, u32[]{:S(2)}) collective-permute-start(bf16[8,48,256]{2,1,0:T(8,128)(2,1)S(1)} %column.1), channel_id=1, source_target_pairs={{0,4},{8,10},{1,5},{9,11},{2,6},{10,8},{3,7},{11,9},{16,20},{24,26... | collective-permute-start | bytes 589832 | tf_op jit(solution)/shard_map/ppermute | solution.py:30
  23.3 2.4 %collective-permute-start.9 = (bf16[8,48,256]{2,1,0:T(8,128)(2,1)S(1)}, bf16[8,48,256]{2,1,0:T(8,128)(2,1)S(1)}, u32[]{:S(2)}, u32[]{:S(2)}) collective-permute-start(bf16[8,48,256]{2,1,0:T(8,128)(2,1)S(1)} %column.1), channel_id=1, source_target_pairs={{0,20},{8,11},{1,21},{9,8},{2,22},{10,9},{3,23},{11,10},{16,0},{24... | collective-permute-start | bytes 589832 | tf_op jit(solution)/shard_map/ppermute | solution.py:30
  26.2 2.6 %collective-permute-done.11 = bf16[8,48,256]{2,1,0:T(8,128)(2,1)S(1)} collective-permute-done((bf16[8,48,256]{2,1,0:T(8,128)(2,1)S(1)}, bf16[8,48,256]{2,1,0:T(8,128)(2,1)S(1)}, u32[]{:S(2)}, u32[]{:S(2)}) %collective-permute-start.11) | collective-permute-done | bytes 196640 | tf_op jit(solution)/shard_map/ppermute | solution.py:30
  28.9 2.8 %collective-permute-start.13 = (bf16[2,8,48,256]{3,2,1,0:T(8,128)(2,1)S(1)}, bf16[2,8,48,256]{3,2,1,0:T(8,128)(2,1)S(1)}, u32[]{:S(2)}, u32[]{:S(2)}) collective-permute-start(bf16[2,8,48,256]{3,2,1,0:T(8,128)(2,1)S(1)} %pad_maximum_fusion.1.refs_1_), channel_id=1, source_target_pairs={{0,3},{8,28},{1,0},{9,29},{2,1},{10,30},{3,2},{11,31},{16,19},{24,... | collective-permute-start | bytes 1179656 | tf_op jit(solution)/shard_map/ppermute | solution.py:30
  32.0 2.7 %collective-permute-start.15 = (bf16[2,8,48,256]{3,2,1,0:T(8,128)(2,1)S(1)}, bf16[2,8,48,256]{3,2,1,0:T(8,128)(2,1)S(1)}, u32[]{:S(2)}, u32[]{:S(2)}) collective-permute-start(bf16[2,8,48,256]{3,2,1,0:T(8,128)(2,1)S(1)} %pad_maximum_fusion.refs_0_), channel_id=1, source_target_pairs={{0,3},{8,28},{1,0},{9,29},{2,1},{10,30},{3,2},{11,31},{16,19},{24,... | collective-permute-start | bytes 1179656 | tf_op jit(solution)/shard_map/ppermute | solution.py:30
  34.6 1.8 %collective-permute-done.13.refs_3_ = bf16[2,8,48,256]{3,2,1,0:T(8,128)(2,1)S(1)} collective-permute-done((bf16[2,8,48,256]{3,2,1,0:T(8,128)(2,1)S(1)}, bf16[2,8,48,256]{3,2,1,0:T(8,128)(2,1)S(1)}, u32[]{:S(2)}, u32[]{:S(2)}) %collective-permute-start.13) | collective-permute-done | bytes 393248 | tf_op jit(solution)/shard_map/ppermute | solution.py:30
  36.4 3.1 %collective-permute-start.17 = (bf16[2,8,48,256]{3,2,1,0:T(8,128)(2,1)S(1)}, bf16[2,8,48,256]{3,2,1,0:T(8,128)(2,1)S(1)}, u32[]{:S(2)}, u32[]{:S(2)}) collective-permute-start(bf16[2,8,48,256]{3,2,1,0:T(8,128)(2,1)S(1)} %collective-permute-done.13.refs_3_), channel_id=1, source_target_pairs={{0,3},{8,28},{1,0},{9,29},{2,1},{10,30},{3,2},{11,31},{16,19},{24,... | collective-permute-start | bytes 1179656 | tf_op jit(solution)/shard_map/ppermute | solution.py:30
  40.0 4.2 %collective-permute-done.14.refs_4_ = bf16[2,8,48,256]{3,2,1,0:T(8,128)(2,1)S(1)} collective-permute-done((bf16[2,8,48,256]{3,2,1,0:T(8,128)(2,1)S(1)}, bf16[2,8,48,256]{3,2,1,0:T(8,128)(2,1)S(1)}, u32[]{:S(2)}, u32[]{:S(2)}) %collective-permute-start.14) | collective-permute-done | bytes 393248 | tf_op jit(solution)/shard_map/ppermute | solution.py:30
  44.2 1.0 lay.2._.refs_0_
  45.2 3.4 %hold.1 = (bf16[4,256,2048]{2,1,0:T(8,128)(2,1)S(1)}, bf16[4,256,2048]{2,1,0:T(8,128)(2,1)S(1)}, f32[8,128]{1,0:T(8,128)S(1)}) custom-call(s32[6]{0:T(128)S(1)} %stack.72.spot, bf16[4,256,2048]{2,1,0:T(8,128)(2,1)S(1)} %copy-done, bf16[4,256,2048]{2,1,0:T(8,128)(2,1)} %collective-permute-done.8.second, bf16[768,2048]{1,0:T(8,128)(2,1)S(1)} %lay.2._.refs_0_), custom_call_target="tpu_custom_call" | custom-call | tf_op jit(solution)/shard_map/hold/pallas_call | solution.py:159
  49.5 4.6 %collective-permute-start.27 = (bf16[768,2048]{1,0:T(8,128)(2,1)S(1)}, bf16[768,2048]{1,0:T(8,128)(2,1)S(1)}, u32[]{:S(2)}, u32[]{:S(2)}) collective-permute-start(bf16[768,2048]{1,0:T(8,128)(2,1)S(1)} %lay.3.rows_ref.mine_ref), channel_id=1, source_target_pairs={{0,8},{8,0},{1,9},{9,1},{2,10},{10,2},{3,11},{11,3},{16,24},{24,16... | collective-permute-start | bytes 9437192 | tf_op jit(solution)/shard_map/ppermute | solution.py:30
  54.0 6.7 %score.1 = f32[8,768]{1,0:T(8,128)S(1)} custom-call(f32[4,384]{1,0:T(4,128)S(1)} %pad_maximum_fusion.2.terms_ref, f32[4,384]{1,0:T(4,128)S(1)} %collective-permute-done.7.their_terms_ref, f32[8,128]{1,0:T(8,128)S(1)} %get-tuple-element.17.refs_3_.log_det_ref, bf16[4,256,2048]{2,1,0:T(8,128)(2,1)S(1)} %get-tuple-element.18.factors_ref, ...), custom_call_target="tpu_custom_call" | custom-call | flops 6442450944 | bytes 8388608 | tf_op jit(solution)/shard_map/score/pallas_call | solution.py:190
  60.9 2.6 %collective-permute-done.18 = f32[8,768]{1,0:T(8,128)S(1)} collective-permute-done((f32[8,768]{1,0:T(8,128)S(1)}, f32[8,768]{1,0:T(8,128)S(1)}, u32[]{:S(2)}, u32[]{:S(2)}) %collective-permute-start.18) | collective-permute-done | bytes 24608 | tf_op jit(solution)/shard_map/ppermute | solution.py:30
  63.6 3.9 %collective-permute-done.19 = f32[8,768]{1,0:T(8,128)S(1)} collective-permute-done((f32[8,768]{1,0:T(8,128)S(1)}, f32[8,768]{1,0:T(8,128)S(1)}, u32[]{:S(2)}, u32[]{:S(2)}) %collective-permute-start.19) | collective-permute-done | bytes 24608 | tf_op jit(solution)/shard_map/ppermute | solution.py:30
  67.4 1.3 %collective-permute-start.20 = (f32[8,768]{1,0:T(8,128)S(1)}, f32[8,768]{1,0:T(8,128)S(1)}, u32[]{:S(2)}, u32[]{:S(2)}) collective-permute-start(f32[8,768]{1,0:T(8,128)S(1)} %add.70), channel_id=1, source_target_pairs={{0,4},{8,12},{1,5},{9,13},{2,6},{10,14},{3,7},{11,15},{16,20},{24,... | collective-permute-start | bytes 73736 | tf_op jit(solution)/shard_map/ppermute | solution.py:30
  68.9 2.7 %collective-permute-done.20 = f32[8,768]{1,0:T(8,128)S(1)} collective-permute-done((f32[8,768]{1,0:T(8,128)S(1)}, f32[8,768]{1,0:T(8,128)S(1)}, u32[]{:S(2)}, u32[]{:S(2)}) %collective-permute-start.20) | collective-permute-done | bytes 24608 | tf_op jit(solution)/shard_map/ppermute | solution.py:30
  72.5 2.1 %collective-permute-done.22 = f32[2,768]{1,0:T(2,128)S(1)} collective-permute-done((f32[2,768]{1,0:T(2,128)S(1)}, f32[2,768]{1,0:T(2,128)S(1)}, u32[]{:S(2)}, u32[]{:S(2)}) %collective-permute-start.22) | collective-permute-done | bytes 6176 | tf_op jit(solution)/shard_map/ppermute | solution.py:30
  74.9 2.4 %collective-permute-done.23 = f32[2,768]{1,0:T(2,128)S(1)} collective-permute-done((f32[2,768]{1,0:T(2,128)S(1)}, f32[2,768]{1,0:T(2,128)S(1)}, u32[]{:S(2)}, u32[]{:S(2)}) %collective-permute-start.23) | collective-permute-done | bytes 6176 | tf_op jit(solution)/shard_map/ppermute | solution.py:30
  77.3 0.8 collective-permute-start.24
  78.1 2.9 %collective-permute-done.24 = f32[2,768]{1,0:T(2,128)S(1)} collective-permute-done((f32[2,768]{1,0:T(2,128)S(1)}, f32[2,768]{1,0:T(2,128)S(1)}, u32[]{:S(2)}, u32[]{:S(2)}) %collective-permute-start.24) | collective-permute-done | bytes 6176 | tf_op jit(solution)/shard_map/ppermute | solution.py:30
  81.1 1.2 %collective-permute-start.25 = (f32[2,768]{1,0:T(2,128)S(1)}, f32[2,768]{1,0:T(2,128)S(1)}, u32[]{:S(2)}, u32[]{:S(2)}) collective-permute-start(f32[2,768]{1,0:T(2,128)S(1)} %pad_maximum_fusion.6._), channel_id=1, source_target_pairs={{0,96},{8,104},{1,97},{9,105},{2,98},{10,106},{3,99},{11,107},{16,... | collective-permute-start | bytes 18440 | tf_op jit(solution)/shard_map/ppermute | solution.py:30
  82.3 6.9 %collective-permute-start.21 = (f32[4,768]{1,0:T(4,128)S(1)}, f32[4,768]{1,0:T(4,128)S(1)}, u32[]{:S(2)}, u32[]{:S(2)}) collective-permute-start(f32[4,768]{1,0:T(4,128)S(1)} %get-tuple-element.33), channel_id=1, source_target_pairs={{0,8},{8,0},{1,9},{9,1},{2,10},{10,2},{3,11},{11,3},{16,24},{24,16... | collective-permute-start | bytes 36872 | tf_op jit(solution)/shard_map/ppermute | solution.py:30
  89.3 4.1 %collective-permute-start.26 = (f32[2,768]{1,0:T(2,128)S(1)}, f32[2,768]{1,0:T(2,128)S(1)}, u32[]{:S(2)}, u32[]{:S(2)}) collective-permute-start(f32[2,768]{1,0:T(2,128)S(1)} %pad_maximum_fusion.7.norms_ref), channel_id=1, source_target_pairs={{0,8},{8,0},{1,9},{9,1},{2,10},{10,2},{3,11},{11,3},{16,24},{24,16... | collective-permute-start | bytes 18440 | tf_op jit(solution)/shard_map/ppermute | solution.py:30
  93.4 1.1 %turn.1 = (bf16[256,1536]{1,0:T(8,128)(2,1)S(1)}, bf16[768,2048]{1,0:T(8,128)(2,1)S(1)}) custom-call(s32[6]{0:T(128)S(1)} %stack.72.spot, bf16[768,2048]{1,0:T(8,128)(2,1)S(1)} %lay.3.rows_ref.mine_ref, bf16[768,2048]{1,0:T(8,128)(2,1)S(1)} %collective-permute-done.27.theirs_ref, f32[2,768]{1,0:T(2,128)S(1)} %pad_maximum_fusion.6._), custom_call_target="tpu_custom_call" | custom-call | bytes 8388608 | tf_op jit(solution)/shard_map/turn/pallas_call | solution.py:214
  94.5 10.4 %moments.1 = (f32[1,48]{1,0:T(1,128)}, f32[4,256]{1,0:T(4,128)}, bf16[4,256,2048]{2,1,0:T(8,128)(2,1)}) custom-call(s32[6]{0:T(128)S(1)} %stack.72.spot, f32[4,768]{1,0:T(4,128)S(1)} %get-tuple-element.34.loglik_ref, f32[4,768]{1,0:T(4,128)S(1)} %collective-permute-done.21.their_loglik_ref, f32[2,768]{1,0:T(2,128)S(1)} %pad_maximum_fusion.7.norms_ref, ...), custom_call_target="tpu_custom_call" | custom-call | tf_op jit(solution)/shard_map/moments/pallas_call | solution.py:279
  (60 shorter events, 5.9 us)
Async XLA Ops:
  0.6 44.6 %collective-permute-start.8 = (bf16[4,256,2048]{2,1,0:T(8,128)(2,1)}, bf16[4,256,2048]{2,1,0:T(8,128)(2,1)}, u32[]{:S(2)}, u32[]{:S(2)}) collective-permute-start(bf16[4,256,2048]{2,1,0:T(8,128)(2,1)} %first.1), channel_id=1, source_target_pairs={{0,8},{8,0},{1,9},{9,1},{2,10},{10,2},{3,11},{11,3},{16,24},{24,16... | collective-permute-start | bytes 12582920 | tf_op jit(solution)/shard_map/ppermute | solution.py:30
  4.0 7.4 %collective-permute-start.1 = (bf16[48,256]{1,0:T(8,128)(2,1)}, bf16[48,256]{1,0:T(8,128)(2,1)S(1)}, u32[]{:S(2)}, u32[]{:S(2)}) collective-permute-start(bf16[48,256]{1,0:T(8,128)(2,1)} %refs_0_.1), channel_id=1, source_target_pairs={{0,192},{8,200},{1,193},{9,201},{2,194},{10,202},{3,195},{11,203},... | collective-permute-start | bytes 73736 | tf_op jit(solution)/shard_map/ppermute | solution.py:30
  8.3 5.8 %collective-permute-start.4 = (bf16[48,256]{1,0:T(8,128)(2,1)}, bf16[48,256]{1,0:T(8,128)(2,1)S(1)}, u32[]{:S(2)}, u32[]{:S(2)}) collective-permute-start(bf16[48,256]{1,0:T(8,128)(2,1)} %refs_0_.1), channel_id=1, source_target_pairs={{0,64},{8,72},{1,65},{9,73},{2,66},{10,74},{3,67},{11,75},{16,80},... | collective-permute-start | bytes 73736 | tf_op jit(solution)/shard_map/ppermute | solution.py:30
  8.3 5.8 %collective-permute-start = (bf16[48,256]{1,0:T(8,128)(2,1)}, bf16[48,256]{1,0:T(8,128)(2,1)S(1)}, u32[]{:S(2)}, u32[]{:S(2)}) collective-permute-start(bf16[48,256]{1,0:T(8,128)(2,1)} %refs_0_.1), channel_id=1, source_target_pairs={{0,224},{8,232},{1,225},{9,233},{2,226},{10,234},{3,227},{11,235},... | collective-permute-start | bytes 73736 | tf_op jit(solution)/shard_map/ppermute | solution.py:30
  11.4 5.4 %collective-permute-start.6 = (bf16[48,256]{1,0:T(8,128)(2,1)}, bf16[48,256]{1,0:T(8,128)(2,1)S(1)}, u32[]{:S(2)}, u32[]{:S(2)}) collective-permute-start(bf16[48,256]{1,0:T(8,128)(2,1)} %refs_0_.1), channel_id=1, source_target_pairs={{0,32},{8,40},{1,33},{9,41},{2,34},{10,42},{3,35},{11,43},{16,48},... | collective-permute-start | bytes 73736 | tf_op jit(solution)/shard_map/ppermute | solution.py:30
  11.4 7.2 %collective-permute-start.2 = (bf16[48,256]{1,0:T(8,128)(2,1)S(1)}, bf16[48,256]{1,0:T(8,128)(2,1)S(1)}, u32[]{:S(2)}, u32[]{:S(2)}) collective-permute-start(bf16[48,256]{1,0:T(8,128)(2,1)S(1)} %collective-permute-done.1.refs_2_), channel_id=1, source_target_pairs={{0,224},{8,232},{1,225},{9,233},{2,226},{10,234},{3,227},{11,235},... | collective-permute-start | bytes 73736 | tf_op jit(solution)/shard_map/ppermute | solution.py:30
  14.1 4.5 %collective-permute-start.3 = (bf16[48,256]{1,0:T(8,128)(2,1)S(1)}, bf16[48,256]{1,0:T(8,128)(2,1)S(1)}, u32[]{:S(2)}, u32[]{:S(2)}) collective-permute-start(bf16[48,256]{1,0:T(8,128)(2,1)S(1)} %collective-permute-done.1.refs_2_), channel_id=1, source_target_pairs={{0,192},{8,200},{1,193},{9,201},{2,194},{10,202},{3,195},{11,203},... | collective-permute-start | bytes 73736 | tf_op jit(solution)/shard_map/ppermute | solution.py:30
  14.1 4.5 %collective-permute-start.5 = (bf16[48,256]{1,0:T(8,128)(2,1)S(1)}, bf16[48,256]{1,0:T(8,128)(2,1)S(1)}, u32[]{:S(2)}, u32[]{:S(2)}) collective-permute-start(bf16[48,256]{1,0:T(8,128)(2,1)S(1)} %collective-permute-done.4.refs_6_), channel_id=1, source_target_pairs={{0,32},{8,40},{1,33},{9,41},{2,34},{10,42},{3,35},{11,43},{16,48},... | collective-permute-start | bytes 73736 | tf_op jit(solution)/shard_map/ppermute | solution.py:30
  16.8 3.3 %collective-permute-start.7 = (f32[4,384]{1,0:T(4,128)S(1)}, f32[4,384]{1,0:T(4,128)S(1)}, u32[]{:S(2)}, u32[]{:S(2)}) collective-permute-start(f32[4,384]{1,0:T(4,128)S(1)} %pad_maximum_fusion.2.terms_ref), channel_id=1, source_target_pairs={{0,8},{8,0},{1,9},{9,1},{2,10},{10,2},{3,11},{11,3},{16,24},{24,16... | collective-permute-start | bytes 18440 | tf_op jit(solution)/shard_map/ppermute | solution.py:30
  18.6 26.6 %copy-start = (bf16[4,256,2048]{2,1,0:T(8,128)(2,1)S(1)}, bf16[4,256,2048]{2,1,0:T(8,128)(2,1)}, u32[]{:S(2)}) copy-start(bf16[4,256,2048]{2,1,0:T(8,128)(2,1)} %first.1) | copy-start | bytes 12582916
  18.6 0.9 copy-start.1
  20.1 6.1 %collective-permute-start.10 = (bf16[8,48,256]{2,1,0:T(8,128)(2,1)S(1)}, bf16[8,48,256]{2,1,0:T(8,128)(2,1)S(1)}, u32[]{:S(2)}, u32[]{:S(2)}) collective-permute-start(bf16[8,48,256]{2,1,0:T(8,128)(2,1)S(1)} %column.1), channel_id=1, source_target_pairs={{0,4},{8,10},{1,5},{9,11},{2,6},{10,8},{3,7},{11,9},{16,20},{24,26... | collective-permute-start | bytes 589832 | tf_op jit(solution)/shard_map/ppermute | solution.py:30
  22.9 5.9 %collective-permute-start.11 = (bf16[8,48,256]{2,1,0:T(8,128)(2,1)S(1)}, bf16[8,48,256]{2,1,0:T(8,128)(2,1)S(1)}, u32[]{:S(2)}, u32[]{:S(2)}) collective-permute-start(bf16[8,48,256]{2,1,0:T(8,128)(2,1)S(1)} %column.1), channel_id=1, source_target_pairs={{0,16},{8,9},{1,17},{9,10},{2,18},{10,11},{3,19},{11,8},{16,4},{24... | collective-permute-start | bytes 589832 | tf_op jit(solution)/shard_map/ppermute | solution.py:30
  23.3 8.5 %collective-permute-start.9 = (bf16[8,48,256]{2,1,0:T(8,128)(2,1)S(1)}, bf16[8,48,256]{2,1,0:T(8,128)(2,1)S(1)}, u32[]{:S(2)}, u32[]{:S(2)}) collective-permute-start(bf16[8,48,256]{2,1,0:T(8,128)(2,1)S(1)} %column.1), channel_id=1, source_target_pairs={{0,20},{8,11},{1,21},{9,8},{2,22},{10,9},{3,23},{11,10},{16,0},{24... | collective-permute-start | bytes 589832 | tf_op jit(solution)/shard_map/ppermute | solution.py:30
  28.9 7.5 %collective-permute-start.13 = (bf16[2,8,48,256]{3,2,1,0:T(8,128)(2,1)S(1)}, bf16[2,8,48,256]{3,2,1,0:T(8,128)(2,1)S(1)}, u32[]{:S(2)}, u32[]{:S(2)}) collective-permute-start(bf16[2,8,48,256]{3,2,1,0:T(8,128)(2,1)S(1)} %pad_maximum_fusion.1.refs_1_), channel_id=1, source_target_pairs={{0,3},{8,28},{1,0},{9,29},{2,1},{10,30},{3,2},{11,31},{16,19},{24,... | collective-permute-start | bytes 1179656 | tf_op jit(solution)/shard_map/ppermute | solution.py:30
  31.8 8.2 %collective-permute-start.12 = (bf16[2,8,48,256]{3,2,1,0:T(8,128)(2,1)S(1)}, bf16[2,8,48,256]{3,2,1,0:T(8,128)(2,1)S(1)}, u32[]{:S(2)}, u32[]{:S(2)}) collective-permute-start(bf16[2,8,48,256]{3,2,1,0:T(8,128)(2,1)S(1)} %pad_maximum_fusion.refs_0_), channel_id=1, source_target_pairs={{0,1},{8,24},{1,2},{9,25},{2,3},{10,26},{3,0},{11,27},{16,17},{24,... | collective-permute-start | bytes 1179656 | tf_op jit(solution)/shard_map/ppermute | solution.py:30
  31.9 12.3 %collective-permute-start.14 = (bf16[2,8,48,256]{3,2,1,0:T(8,128)(2,1)S(1)}, bf16[2,8,48,256]{3,2,1,0:T(8,128)(2,1)S(1)}, u32[]{:S(2)}, u32[]{:S(2)}) collective-permute-start(bf16[2,8,48,256]{3,2,1,0:T(8,128)(2,1)S(1)} %pad_maximum_fusion.1.refs_1_), channel_id=1, source_target_pairs={{0,1},{8,24},{1,2},{9,25},{2,3},{10,26},{3,0},{11,27},{16,17},{24,... | collective-permute-start | bytes 1179656 | tf_op jit(solution)/shard_map/ppermute | solution.py:30
  32.0 12.2 %collective-permute-start.15 = (bf16[2,8,48,256]{3,2,1,0:T(8,128)(2,1)S(1)}, bf16[2,8,48,256]{3,2,1,0:T(8,128)(2,1)S(1)}, u32[]{:S(2)}, u32[]{:S(2)}) collective-permute-start(bf16[2,8,48,256]{3,2,1,0:T(8,128)(2,1)S(1)} %pad_maximum_fusion.refs_0_), channel_id=1, source_target_pairs={{0,3},{8,28},{1,0},{9,29},{2,1},{10,30},{3,2},{11,31},{16,19},{24,... | collective-permute-start | bytes 1179656 | tf_op jit(solution)/shard_map/ppermute | solution.py:30
  36.4 12.2 %collective-permute-start.17 = (bf16[2,8,48,256]{3,2,1,0:T(8,128)(2,1)S(1)}, bf16[2,8,48,256]{3,2,1,0:T(8,128)(2,1)S(1)}, u32[]{:S(2)}, u32[]{:S(2)}) collective-permute-start(bf16[2,8,48,256]{3,2,1,0:T(8,128)(2,1)S(1)} %collective-permute-done.13.refs_3_), channel_id=1, source_target_pairs={{0,3},{8,28},{1,0},{9,29},{2,1},{10,30},{3,2},{11,31},{16,19},{24,... | collective-permute-start | bytes 1179656 | tf_op jit(solution)/shard_map/ppermute | solution.py:30
  40.0 8.7 %collective-permute-start.16 = (bf16[2,8,48,256]{3,2,1,0:T(8,128)(2,1)S(1)}, bf16[2,8,48,256]{3,2,1,0:T(8,128)(2,1)S(1)}, u32[]{:S(2)}, u32[]{:S(2)}) collective-permute-start(bf16[2,8,48,256]{3,2,1,0:T(8,128)(2,1)S(1)} %collective-permute-done.12.refs_2_), channel_id=1, source_target_pairs={{0,1},{8,24},{1,2},{9,25},{2,3},{10,26},{3,0},{11,27},{16,17},{24,... | collective-permute-start | bytes 1179656 | tf_op jit(solution)/shard_map/ppermute | solution.py:30
  49.5 43.9 %collective-permute-start.27 = (bf16[768,2048]{1,0:T(8,128)(2,1)S(1)}, bf16[768,2048]{1,0:T(8,128)(2,1)S(1)}, u32[]{:S(2)}, u32[]{:S(2)}) collective-permute-start(bf16[768,2048]{1,0:T(8,128)(2,1)S(1)} %lay.3.rows_ref.mine_ref), channel_id=1, source_target_pairs={{0,8},{8,0},{1,9},{9,1},{2,10},{10,2},{3,11},{11,3},{16,24},{24,16... | collective-permute-start | bytes 9437192 | tf_op jit(solution)/shard_map/ppermute | solution.py:30
  60.8 2.8 %collective-permute-start.18 = (f32[8,768]{1,0:T(8,128)S(1)}, f32[8,768]{1,0:T(8,128)S(1)}, u32[]{:S(2)}, u32[]{:S(2)}) collective-permute-start(f32[8,768]{1,0:T(8,128)S(1)} %score.1), channel_id=1, source_target_pairs={{0,1},{8,9},{1,0},{9,8},{2,3},{10,11},{3,2},{11,10},{16,17},{24,25... | collective-permute-start | bytes 73736 | tf_op jit(solution)/shard_map/ppermute | solution.py:30
  63.5 3.9 %collective-permute-start.19 = (f32[8,768]{1,0:T(8,128)S(1)}, f32[8,768]{1,0:T(8,128)S(1)}, u32[]{:S(2)}, u32[]{:S(2)}) collective-permute-start(f32[8,768]{1,0:T(8,128)S(1)} %add.69), channel_id=1, source_target_pairs={{0,3},{8,11},{1,2},{9,10},{2,1},{10,9},{3,0},{11,8},{16,19},{24,27... | collective-permute-start | bytes 73736 | tf_op jit(solution)/shard_map/ppermute | solution.py:30
  67.4 4.2 %collective-permute-start.20 = (f32[8,768]{1,0:T(8,128)S(1)}, f32[8,768]{1,0:T(8,128)S(1)}, u32[]{:S(2)}, u32[]{:S(2)}) collective-permute-start(f32[8,768]{1,0:T(8,128)S(1)} %add.70), channel_id=1, source_target_pairs={{0,4},{8,12},{1,5},{9,13},{2,6},{10,14},{3,7},{11,15},{16,20},{24,... | collective-permute-start | bytes 73736 | tf_op jit(solution)/shard_map/ppermute | solution.py:30
  71.8 2.9 %collective-permute-start.22 = (f32[2,768]{1,0:T(2,128)S(1)}, f32[2,768]{1,0:T(2,128)S(1)}, u32[]{:S(2)}, u32[]{:S(2)}) collective-permute-start(f32[2,768]{1,0:T(2,128)S(1)} %pad_maximum_fusion.3), channel_id=1, source_target_pairs={{0,16},{8,24},{1,17},{9,25},{2,18},{10,26},{3,19},{11,27},{16,0},{... | collective-permute-start | bytes 18440 | tf_op jit(solution)/shard_map/ppermute | solution.py:30
  74.7 2.6 %collective-permute-start.23 = (f32[2,768]{1,0:T(2,128)S(1)}, f32[2,768]{1,0:T(2,128)S(1)}, u32[]{:S(2)}, u32[]{:S(2)}) collective-permute-start(f32[2,768]{1,0:T(2,128)S(1)} %pad_maximum_fusion.4), channel_id=1, source_target_pairs={{0,32},{8,40},{1,33},{9,41},{2,34},{10,42},{3,35},{11,43},{16,48},... | collective-permute-start | bytes 18440 | tf_op jit(solution)/shard_map/ppermute | solution.py:30
  77.3 3.8 %collective-permute-start.24 = (f32[2,768]{1,0:T(2,128)S(1)}, f32[2,768]{1,0:T(2,128)S(1)}, u32[]{:S(2)}, u32[]{:S(2)}) collective-permute-start(f32[2,768]{1,0:T(2,128)S(1)} %pad_maximum_fusion.5), channel_id=1, source_target_pairs={{0,224},{8,232},{1,225},{9,233},{2,226},{10,234},{3,227},{11,235},... | collective-permute-start | bytes 18440 | tf_op jit(solution)/shard_map/ppermute | solution.py:30
  81.1 8.1 %collective-permute-start.25 = (f32[2,768]{1,0:T(2,128)S(1)}, f32[2,768]{1,0:T(2,128)S(1)}, u32[]{:S(2)}, u32[]{:S(2)}) collective-permute-start(f32[2,768]{1,0:T(2,128)S(1)} %pad_maximum_fusion.6._), channel_id=1, source_target_pairs={{0,96},{8,104},{1,97},{9,105},{2,98},{10,106},{3,99},{11,107},{16,... | collective-permute-start | bytes 18440 | tf_op jit(solution)/shard_map/ppermute | solution.py:30
  82.3 12.2 %collective-permute-start.21 = (f32[4,768]{1,0:T(4,128)S(1)}, f32[4,768]{1,0:T(4,128)S(1)}, u32[]{:S(2)}, u32[]{:S(2)}) collective-permute-start(f32[4,768]{1,0:T(4,128)S(1)} %get-tuple-element.33), channel_id=1, source_target_pairs={{0,8},{8,0},{1,9},{9,1},{2,10},{10,2},{3,11},{11,3},{16,24},{24,16... | collective-permute-start | bytes 36872 | tf_op jit(solution)/shard_map/ppermute | solution.py:30
  89.3 5.2 %collective-permute-start.26 = (f32[2,768]{1,0:T(2,128)S(1)}, f32[2,768]{1,0:T(2,128)S(1)}, u32[]{:S(2)}, u32[]{:S(2)}) collective-permute-start(f32[2,768]{1,0:T(2,128)S(1)} %pad_maximum_fusion.7.norms_ref), channel_id=1, source_target_pairs={{0,8},{8,0},{1,9},{9,1},{2,10},{10,2},{3,11},{11,3},{16,24},{24,16... | collective-permute-start | bytes 18440 | tf_op jit(solution)/shard_map/ppermute | solution.py:30
